TPU v7x, 32 devices: a whole 2x2x4 slice. The times are simulated.
32 devices in a mesh: dp: 4 (over x, core), chan: 8 (over z, y).
Axes of the slice: x: 2, y: 2, z: 4, core: 2. Of those that a mesh axis runs over, the one named last changes fastest.
Arguments:
- patches: float32 [4, 93312, 144], P('dp', 'chan'), may hold values from -6 to 6
- class_in: float32 [4, 128, 144], P('dp', 'chan'), may hold values from -6 to 6
- conv_weight: float32 [288, 9], P('chan')
- conv_bias: float32 [288], P('chan')
- head_weight: float32 [144, 288], P(None, 'chan')
- head_bias: float32 [288], P('chan')
- first_conv_w: float32 [288, 9], P('chan'), may hold values from -224 to 224
- first_conv_b: float32 [288], P('chan'), may hold values from -224 to 224
- first_head_w: float32 [144, 288], P(None, 'chan'), may hold values from -16 to 16
- first_head_b: float32 [288], P('chan'), may hold values from -16 to 16
- second_conv_w: float32 [288, 9], P('chan'), may hold values from 100.352 to 401.408
- second_conv_b: float32 [288], P('chan'), may hold values from 100.352 to 401.408
- second_head_w: float32 [144, 288], P(None, 'chan'), may hold values from 0.512 to 2.048
- second_head_b: float32 [288], P('chan'), may hold values from 0.512 to 2.048
- average_conv_w: float32 [288, 9], P('chan'), may hold values from -5 to 5
- average_conv_b: float32 [288], P('chan'), may hold values from -6 to 6
- average_head_w: float32 [144, 288], P(None, 'chan'), may hold values from -3 to 3
- average_head_b: float32 [288], P('chan'), may hold values from -6 to 6
- pooled_cot: float32 [4, 25088, 288], P('dp', 'chan'), may hold values from -6 to 6
- class_cot: float32 [4, 128, 288], P('dp', 'chan'), may hold values from -6 to 6
Outputs:
- pooled: float32 [4, 25088, 288], P('dp', 'chan')
- class_out: float32 [4, 128, 288], P('dp', 'chan')
- patches_grad: float32 [4, 93312, 144], P('dp', 'chan')
- class_grad: float32 [4, 128, 144], P('dp', 'chan')
- new_first_conv_w: float32 [288, 9], P('chan')
- new_second_conv_w: float32 [288, 9], P('chan')
- new_conv_w: float32 [288, 9], P('chan')
- new_average_conv_w: float32 [288, 9], P('chan')
- new_first_conv_b: float32 [288], P('chan')
- new_second_conv_b: float32 [288], P('chan')
- new_conv_b: float32 [288], P('chan')
- new_average_conv_b: float32 [288], P('chan')
- new_first_head_w: float32 [144, 288], P(None, 'chan')
- new_second_head_w: float32 [144, 288], P(None, 'chan')
- new_head_w: float32 [144, 288], P(None, 'chan')
- new_average_head_w: float32 [144, 288], P(None, 'chan')
- new_first_head_b: float32 [288], P('chan')
- new_second_head_b: float32 [288], P('chan')
- new_head_b: float32 [288], P('chan')
- new_average_head_b: float32 [288], P('chan')
- trust_ratios: float32 [4], replicated
All inputs are finite; a program needn't handle non-finite values.
Results may differ from a plain program's by a relative error of at most 0.0003.
Values sent between devices are 32-bit elements; how exact they have to be, the bound alone decides.
No kernel may reach another device: no remote copies, remote signals or barrier semaphores. Data moves between devices by JAX's collectives and lax.ppermute only.
A program may use at most 512 MiB of HBM per device.

v0:
```python
import jax
import jax.numpy as jnp
import numpy as np
from jax import lax
from jax.sharding import PartitionSpec as P

GRID = 27
TAPS = 9
OUTG = 14


beta_one = 0.9
beta_two = 0.999
fix_first = 1.0 - 0.9**10
fix_second = 1.0 - 0.999**10
small_eps = 1e-06
learn_rate = 0.5
keep_rate = 0.9


def moments(weight, grad, first, second, decay):
    first_new = beta_one * first + (1.0 - beta_one) * grad
    second_new = beta_two * second + (1.0 - beta_two) * grad * grad
    update = (
        first_new / fix_first / (jnp.sqrt(second_new / fix_second) + small_eps) + decay * weight
    )
    return (first_new, second_new, update)


def per_device(
    patches,
    class_in,
    conv_weight,
    conv_bias,
    head_weight,
    head_bias,
    first_conv_w,
    first_conv_b,
    first_head_w,
    first_head_b,
    second_conv_w,
    second_conv_b,
    second_head_w,
    second_head_b,
    average_conv_w,
    average_conv_b,
    average_head_w,
    average_head_b,
    pooled_cot,
    class_cot,
):
    highest = lax.Precision.HIGHEST
    groups = lax.axis_size("chan")
    per_dev = conv_weight.shape[0]
    local_patches = patches[0]
    local_class = class_in[0]
    local_class_cot = class_cot[0]
    images = local_class.shape[0] * groups
    channels_in = local_patches.shape[1]
    wide = images * per_dev
    weights = (conv_weight, conv_bias, head_weight, head_bias)
    weight_sq = lax.psum(tuple((jnp.sum(item * item) for item in weights)), "chan")
    in_width = per_dev // 2 + 1
    starts = np.arange(groups) * per_dev // 2
    fold_table = np.zeros((groups * in_width, channels_in), np.float32)
    for owner in range(groups):
        for slot in range(in_width):
            if starts[owner] + slot < channels_in:
                fold_table[owner * in_width + slot, starts[owner] + slot] = 1.0
    doubled = jnp.repeat(local_patches, 2, axis=1)
    columns = lax.all_to_all(doubled, "chan", split_axis=1, concat_axis=0, tiled=True)
    grid = columns.reshape(GRID, GRID, wide)
    padded = jnp.pad(grid, ((1, 1), (1, 1), (0, 0)))
    span = 2 * OUTG - 1
    tap_rows = [jnp.tile(conv_weight[:, tap], images) for tap in range(TAPS)]
    total = jnp.zeros((OUTG, OUTG, wide), jnp.float32) + jnp.tile(conv_bias, images)
    for row_tap in range(3):
        for col_tap in range(3):
            window = padded[row_tap : row_tap + span : 2, col_tap : col_tap + span : 2]
            total = total + window * tap_rows[3 * row_tap + col_tap]
    pooled = lax.all_to_all(
        total.reshape(OUTG * OUTG * images, per_dev),
        "chan",
        split_axis=0,
        concat_axis=1,
        tiled=True,
    )
    full_weight, full_bias = (
        lax.all_gather(head_weight, "chan", axis=1, tiled=True),
        lax.all_gather(head_bias, "chan", axis=0, tiled=True),
    )
    class_out = jnp.dot(local_class, full_weight, precision=highest) + full_bias
    class_grad = jnp.dot(local_class_cot, full_weight.T, precision=highest)
    part_weight = jnp.dot(local_class.T, local_class_cot, precision=highest)
    part_bias = jnp.sum(local_class_cot, axis=0)
    grad_hw, grad_hb = (
        lax.psum_scatter(part_weight, "chan", scatter_dimension=1, tiled=True),
        lax.psum_scatter(part_bias, "chan", scatter_dimension=0, tiled=True),
    )
    cot_grid = lax.all_to_all(
        pooled_cot[0], "chan", split_axis=1, concat_axis=0, tiled=True
    ).reshape(OUTG, OUTG, wide)
    grad_cb = jnp.sum(jnp.sum(cot_grid, axis=(0, 1)).reshape(images, per_dev), axis=0)
    tap_grads = []
    back = jnp.zeros(padded.shape, jnp.float32)
    zero = jnp.float32(0.0)
    for row_tap in range(3):
        for col_tap in range(3):
            window = padded[row_tap : row_tap + span : 2, col_tap : col_tap + span : 2]
            tap_wide = jnp.sum(cot_grid * window, axis=(0, 1))
            tap_grads.append(jnp.sum(tap_wide.reshape(images, per_dev), axis=0))
            spread_back = cot_grid * tap_rows[3 * row_tap + col_tap]
            back = back + lax.pad(
                spread_back, zero, ((row_tap, 2 - row_tap, 1), (col_tap, 2 - col_tap, 1), (0, 0, 0))
            )
    grad_cw = jnp.stack(tap_grads, axis=1)
    back_cols = back[1 : GRID + 1, 1 : GRID + 1].reshape(GRID * GRID * images, per_dev)
    back_tokens = lax.all_to_all(back_cols, "chan", split_axis=0, concat_axis=1, tiled=True)
    patches_grad = jnp.sum(back_tokens.reshape(-1, channels_in, 2), axis=2)
    grad_cw, grad_cb, grad_hw, grad_hb = lax.psum((grad_cw, grad_cb, grad_hw, grad_hb), "dp")
    conv_w_set = moments(conv_weight, grad_cw, first_conv_w, second_conv_w, 0.05)
    conv_b_set = moments(conv_bias, grad_cb, first_conv_b, second_conv_b, 0.0)
    head_w_set = moments(head_weight, grad_hw, first_head_w, second_head_w, 0.05)
    head_b_set = moments(head_bias, grad_hb, first_head_b, second_head_b, 0.0)
    updates = (conv_w_set[2], conv_b_set[2], head_w_set[2], head_b_set[2])
    update_local = tuple((jnp.sum(item * item) for item in updates))
    update_sq = lax.psum(update_local, "chan")
    ratios = [jnp.sqrt(weight_sq[k]) / jnp.sqrt(update_sq[k]) for k in range(4)]
    averages = (average_conv_w, average_conv_b, average_head_w, average_head_b)
    sets = (conv_w_set, conv_b_set, head_w_set, head_b_set)
    results = []
    for k in range(4):
        weight_new = weights[k] - learn_rate * ratios[k] * updates[k]
        average_new = keep_rate * averages[k] + (1.0 - keep_rate) * weight_new
        results.extend([sets[k][0], sets[k][1], weight_new, average_new])
    trust = jnp.stack(ratios)
    return tuple(
        [pooled[None], class_out[None], patches_grad[None], class_grad[None]] + results + [trust]
    )


def solution(mesh):
    return jax.shard_map(
        per_device,
        mesh=mesh,
        in_specs=(
            P("dp", "chan", None),
            P("dp", "chan", None),
            P("chan", None),
            P("chan"),
            P(None, "chan"),
            P("chan"),
            P("chan", None),
            P("chan"),
            P(None, "chan"),
            P("chan"),
            P("chan", None),
            P("chan"),
            P(None, "chan"),
            P("chan"),
            P("chan", None),
            P("chan"),
            P(None, "chan"),
            P("chan"),
            P("dp", "chan", None),
            P("dp", "chan", None),
        ),
        out_specs=(
            P("dp", "chan", None),
            P("dp", "chan", None),
            P("dp", "chan", None),
            P("dp", "chan", None),
            P("chan", None),
            P("chan", None),
            P("chan", None),
            P("chan", None),
            P("chan"),
            P("chan"),
            P("chan"),
            P("chan"),
            P(None, "chan"),
            P(None, "chan"),
            P(None, "chan"),
            P(None, "chan"),
            P("chan"),
            P("chan"),
            P("chan"),
            P("chan"),
            P(),
        ),
        check_vma=False,
    )
```

profile of v0, /device:TPU:9, one launch (start us, length us, event | category | flops | bytes accessed | tf_op | source)
XLA Modules:
  0.0 1516.0 jit_solution(9973411330882244951)
XLA Ops:
  0.7 3.7 all_to_all.54
  4.3 5.7 all-to-all-start.2
  10.1 9.4 broadcast_in_dim.16
  19.5 15.4 %all_to_all.48 = f32[11664,8,36]{0,2,1:T(8,128)} reshape(f32[11664,144,2]{0,2,1:T(2,128)} %broadcast_in_dim.16) | data formatting | bytes 26873856 | tf_op jit(solution)/shard_map/all_to_all | solution.py:71
  34.8 64.6 %all-to-all-done.2 = f32[3136,8,36]{0,2,1:T(8,128)} async-done(((f32[3136,8,36]{0,2,1:T(8,128)}), f32[3136,8,36]{0,2,1:T(8,128)}, u32[]{:S(2)}, u32[]{:S(2)}) %all-to-all-start.2) | async-done | bytes 3612704 | tf_op jit(solution)/shard_map/all_to_all | solution.py:100
  99.4 6.4 all-to-all-start
  107.1 9.0 copy.48
  116.0 14.2 reshape.126
  130.2 4.6 broadcast_multiply_fusion
  134.8 15.8 %pad.56 = f32[28,28,4608]{2,1,0:T(8,128)} pad(f32[14,14,4608]{2,1,0:T(8,128)} %broadcast_multiply_fusion, f32[]{:T(128)} %constant.10.clone.1), padding=1_0_1x1_0_1x0_0_0 | pad | bytes 18063364
  150.7 280.0 %all-to-all-done = f32[11664,8,36]{0,2,1:T(8,128)} async-done(((f32[11664,8,36]{0,2,1:T(8,128)}), f32[11664,8,36]{0,2,1:T(8,128)}, u32[]{:S(2)}, u32[]{:S(2)}) %all-to-all-start) | async-done | bytes 13436960 | tf_op jit(solution)/shard_map/all_to_all | solution.py:71
  430.6 28.6 %copy.46 = f32[8,11664,36]{2,1,0:T(8,128)} copy(f32[8,11664,36]{1,2,0:T(8,128)} %bitcast.1) | data formatting | bytes 26873856 | tf_op jit(solution)/shard_map/all_to_all | solution.py:71
  459.3 45.7 %reshape.125 = f32[27,27,4608]{2,1,0:T(8,128)} reshape(f32[8,11664,36]{2,1,0:T(8,128)} %copy.46) | data formatting | bytes 26873856 | tf_op jit(solution)/shard_map/reshape | solution.py:72
  504.9 11.5 pad.31
  516.5 18.1 %slice.82 = f32[14,14,4608]{2,1,0:T(8,128)} slice(f32[29,29,4608]{2,1,0:T(8,128)} %pad.31), slice={[2:29:2], [2:29:2], [0:4608:1]} | slice | bytes 7225344 | tf_op jit(solution)/shard_map/slice | solution.py:79
  534.5 17.9 %slice.80 = f32[14,14,4608]{2,1,0:T(8,128)} slice(f32[29,29,4608]{2,1,0:T(8,128)} %pad.31), slice={[2:29:2], [1:28:2], [0:4608:1]} | slice | bytes 7225344 | tf_op jit(solution)/shard_map/slice | solution.py:79
  552.4 17.9 %slice.78 = f32[14,14,4608]{2,1,0:T(8,128)} slice(f32[29,29,4608]{2,1,0:T(8,128)} %pad.31), slice={[2:29:2], [0:27:2], [0:4608:1]} | slice | bytes 7225344 | tf_op jit(solution)/shard_map/slice | solution.py:79
  570.3 18.2 %slice.76 = f32[14,14,4608]{2,1,0:T(8,128)} slice(f32[29,29,4608]{2,1,0:T(8,128)} %pad.31), slice={[1:28:2], [2:29:2], [0:4608:1]} | slice | bytes 7225344 | tf_op jit(solution)/shard_map/slice | solution.py:79
  588.5 18.0 %slice.74 = f32[14,14,4608]{2,1,0:T(8,128)} slice(f32[29,29,4608]{2,1,0:T(8,128)} %pad.31), slice={[1:28:2], [1:28:2], [0:4608:1]} | slice | bytes 7225344 | tf_op jit(solution)/shard_map/slice | solution.py:79
  606.6 18.0 %slice.72 = f32[14,14,4608]{2,1,0:T(8,128)} slice(f32[29,29,4608]{2,1,0:T(8,128)} %pad.31), slice={[1:28:2], [0:27:2], [0:4608:1]} | slice | bytes 7225344 | tf_op jit(solution)/shard_map/slice | solution.py:79
  624.6 18.2 %slice.70 = f32[14,14,4608]{2,1,0:T(8,128)} slice(f32[29,29,4608]{2,1,0:T(8,128)} %pad.31), slice={[0:27:2], [2:29:2], [0:4608:1]} | slice | bytes 7225344 | tf_op jit(solution)/shard_map/slice | solution.py:79
  642.8 18.0 %slice.68 = f32[14,14,4608]{2,1,0:T(8,128)} slice(f32[29,29,4608]{2,1,0:T(8,128)} %pad.31), slice={[0:27:2], [1:28:2], [0:4608:1]} | slice | bytes 7225344 | tf_op jit(solution)/shard_map/slice | solution.py:79
  660.8 18.0 %slice.66 = f32[14,14,4608]{2,1,0:T(8,128)} slice(f32[29,29,4608]{2,1,0:T(8,128)} %pad.31), slice={[0:27:2], [0:27:2], [0:4608:1]} | slice | bytes 7225344 | tf_op jit(solution)/shard_map/slice | solution.py:79
  678.8 27.1 %fusion.16 = (f32[4608]{0:T(1024)}, f32[4608]{0:T(1024)}, f32[4608]{0:T(1024)}, f32[4608]{0:T(1024)}, f32[4608]{0:T(1024)}, /*index=5*/f32[4608]{0:T(1024)}, f32...) fusion(f32[14,14,4608]{2,1,0:T(8,128)} %reshape.126, ...), kind=kLoop, calls=%fused_computation.77 | loop fusion | flops 24339456 | bytes 65359872 | tf_op jit(solution)/shard_map/reduce_sum | solution.py:103
  706.0 14.5 multiply_add_fusion
  720.5 19.2 %all_to_all.51 = f32[8,3136,36]{2,1,0:T(8,128)} reshape(f32[14,14,4608]{2,1,0:T(8,128)} %multiply_add_fusion) | data formatting | bytes 7225344 | tf_op jit(solution)/shard_map/all_to_all | solution.py:81
  739.6 9.3 copy.47
  748.9 5.6 all-to-all-start.1
  754.5 16.1 %pad.34 = f32[29,29,4608]{2,1,0:T(8,128)} pad(f32[14,14,4608]{2,1,0:T(8,128)} %get-tuple-element.70, f32[]{:T(128)} %constant.10.clone.1), padding=0_2_1x2_0_1x0_0_0 | pad | bytes 19113988 | tf_op jit(solution)/shard_map/pad | solution.py:113
  770.6 16.0 %pad.32 = f32[29,29,4608]{2,1,0:T(8,128)} pad(f32[14,14,4608]{2,1,0:T(8,128)} %get-tuple-element.69, f32[]{:T(128)} %constant.10.clone.1), padding=0_2_1x0_2_1x0_0_0 | pad | bytes 19113988 | tf_op jit(solution)/shard_map/pad | solution.py:113
  786.6 15.9 %pad.33 = f32[29,29,4608]{2,1,0:T(8,128)} pad(f32[14,14,4608]{2,1,0:T(8,128)} %get-tuple-element.68, f32[]{:T(128)} %constant.10.clone.1), padding=0_2_1x1_1_1x0_0_0 | pad | bytes 19113988 | tf_op jit(solution)/shard_map/pad | solution.py:113
  802.5 23.3 %add_add_fusion = f32[29,29,4608]{2,1,0:T(8,128)} fusion(f32[29,29,4608]{2,1,0:T(8,128)} %pad.34, f32[29,29,4608]{2,1,0:T(8,128)} %pad.32, f32[29,29,4608]{2,1,0:T(8,128)} %pad.33), kind=kLoop, calls=%fused_computation | loop fusion | flops 7750656 | bytes 62005248 | tf_op jit(solution)/shard_map/add | solution.py:113
  825.8 15.8 %pad.46 = f32[27,27,4608]{2,1,0:T(8,128)} pad(f32[14,14,4608]{2,1,0:T(8,128)} %get-tuple-element.72, f32[]{:T(128)} %constant.10.clone.1), padding=0_0_1x0_0_1x0_0_0 | pad | bytes 17049604 | tf_op jit(solution)/shard_map/slice | solution.py:117
  841.6 15.7 %pad.60 = f32[27,28,4608]{2,1,0:T(8,128)} pad(f32[14,14,4608]{2,1,0:T(8,128)} %get-tuple-element.71, f32[]{:T(128)} %constant.10.clone.1), padding=0_0_1x0_1_1x0_0_0 | pad | bytes 17547268
  857.3 15.8 %pad.59 = f32[27,28,4608]{2,1,0:T(8,128)} pad(f32[14,14,4608]{2,1,0:T(8,128)} %get-tuple-element.73, f32[]{:T(128)} %constant.10.clone.1), padding=0_0_1x1_0_1x0_0_0 | pad | bytes 17547268
  873.1 15.8 %pad.58 = f32[28,28,4608]{2,1,0:T(8,128)} pad(f32[14,14,4608]{2,1,0:T(8,128)} %get-tuple-element.74, f32[]{:T(128)} %constant.10.clone.1), padding=1_0_1x0_1_1x0_0_0 | pad | bytes 18063364
  888.9 15.8 %pad.57 = f32[28,27,4608]{2,1,0:T(8,128)} pad(f32[14,14,4608]{2,1,0:T(8,128)} %get-tuple-element.75, f32[]{:T(128)} %constant.10.clone.1), padding=1_0_1x0_0_1x0_0_0 | pad | bytes 17547268
  904.7 40.6 %fusion.5 = f32[27,27,4608]{2,1,0:T(8,128)} fusion(f32[27,27,4608]{2,1,0:T(8,128)} %pad.46, f32[29,29,4608]{2,1,0:T(8,128)} %add_add_fusion, f32[27,28,4608]{2,1,0:T(8,128)} %pad.60, f32[27,28,4608]{2,1,0:T(8,128)} %pad.59, f32[28,28,4608]{2,1,0:T(8,128)} %pad.58, f32[28,27,4608]{2,1,0:T(8,128)} %pad.57, f32[28,28,4608]{2,1,0:T(8,128)} %pad.56), kind=kLoop, calls=%fused_computation.6 | loop fusion | flops 20155392 | bytes 107495424 | tf_op jit(solution)/shard_map/add | solution.py:113
  945.3 64.2 %all_to_all.57 = f32[8,11664,36]{2,1,0:T(8,128)} reshape(f32[27,27,4608]{2,1,0:T(8,128)} %fusion.5) | data formatting | bytes 26873856 | tf_op jit(solution)/shard_map/all_to_all | solution.py:118
  1009.5 31.1 %copy.49 = f32[8,11664,36]{1,2,0:T(8,128)} copy(f32[8,11664,36]{2,1,0:T(8,128)} %all_to_all.57) | data formatting | bytes 26873856 | tf_op jit(solution)/shard_map/all_to_all | solution.py:118
  1040.9 5.7 all-to-all-start.3
  1046.7 0.4 fusion.8
  1047.1 332.4 %fusion = f32[144,40]{0,1:T(8,128)S(1)} fusion(f32[144,288]{0,1:T(8,128)S(1)} %fusion.8), kind=kCustom, calls=%all-reduce-scatter | all-reduce-scatter fusion | flops 46081 | bytes 189440
  1379.6 3.8 collective-permute-start
  1383.4 20.6 %all-gather = f32[8,36,144]{2,1,0:T(8,128)S(1)} all-gather(f32[1,36,144]{2,1,0:T(8,128)S(1)} %bitcast.70), channel_id=1, replica_groups=mesh['dp'=4,'chan'=8] {'chan'}, dimensions={0}, use_global_device_ids=true | all-gather | bytes 186624 | tf_op jit(solution)/shard_map/all_gather | solution.py:89
  1404.1 0.9 convolution_bitcast_fusion
  1405.0 0.6 fusion.21
  1407.5 16.0 %all-reduce.12 = f32[288]{0:T(512)S(1)} all-reduce(f32[288]{0:T(512)S(1)} %reduce_sum.297), channel_id=3, replica_groups=mesh['dp'=4,'chan'=8] {'chan'}, use_global_device_ids=true, to_apply=%region_38.39.clone | all-reduce | flops 288 | bytes 2304
  1423.6 0.2 dynamic-update-slice
  1423.8 0.1 concatenate
  1425.6 24.4 %all-reduce.15 = (f32[36,9]{0,1:T(8,128)S(1)}, f32[36]{0:T(128)S(1)}, f32[144,36]{0,1:T(8,128)S(1)}, f32[36]{0:T(128)S(1)}) all-reduce(f32[36,9]{0,1:T(8,128)S(1)} %stack.54, f32[36]{0:T(128)S(1)} %reduce_sum.292, f32[144,36]{0,1:T(8,128)S(1)} %constant_dynamic-slice_fusion, ...), channel_id=1, replica_groups=mesh['dp'=4,'chan'=8] {'dp'}, use_global_device_ids=true, to_apply=%region_19.20 | all-reduce | flops 5580 | bytes 44640 | tf_op jit(solution)/shard_map/psum | solution.py:120
  1450.0 1.1 multiply_reduce_fusion.13
  1451.2 0.6 multiply_reduce_fusion.11
  1451.8 0.7 multiply_reduce_fusion.9
  1452.5 14.8 all-reduce.14
  1472.8 0.6 pad_maximum_fusion
  1473.3 1.0 fusion.6
  1474.3 0.5 multiply_add_fusion.10
  1474.8 0.5 multiply_add_fusion.7
  1475.4 0.6 multiply_add_fusion.4
  1476.0 0.7 multiply_add_fusion.1
  1476.7 3.6 broadcast_in_dim.17
  1480.3 15.2 %reshape.127 = f32[11664,144,2]{0,2,1:T(2,128)} reshape(f32[11664,8,36]{0,2,1:T(8,128)} %bitcast.18) | data formatting | bytes 26873856 | tf_op jit(solution)/shard_map/reshape | solution.py:119
  1495.5 20.4 %reduce_sum.270 = f32[11664,144]{0,1:T(8,128)} reduce(f32[11664,144,2]{0,2,1:T(2,128)} %reshape.127, f32[]{:T(128)} %constant.10.clone.1), dimensions={2}, to_apply=%region_0.0 | reduce | flops 1679616 | bytes 20155396 | tf_op jit(solution)/shard_map/reduce_sum | solution.py:119
  (123 shorter events, 2.9 us)
Async XLA Ops:
  0.7 1045.9 %copy-start = (f32[1,16,144]{2,1,0:T(8,128)S(1)}, f32[1,16,144]{2,1,0:T(8,128)}, u32[]{:S(2)}) copy-start(f32[1,16,144]{2,1,0:T(8,128)} %param.21) | copy-start | bytes 27652
  4.3 95.1 %all-to-all-start.2 = ((f32[3136,8,36]{0,2,1:T(8,128)}), f32[3136,8,36]{0,2,1:T(8,128)}, u32[]{:S(2)}, u32[]{:S(2)}) async-start(f32[3136,8,36]{0,2,1:T(8,128)} %all_to_all.54), calls=%async_computation.2 | async-start | bytes 8192000 | tf_op jit(solution)/shard_map/all_to_all | solution.py:100
  34.8 71.0 %copy-start.16 = (f32[36,9]{0,1:T(8,128)S(1)}, f32[36,9]{0,1:T(8,128)}, u32[]{:S(2)}) copy-start(f32[36,9]{0,1:T(8,128)} %param.22) | copy-start | bytes 3892
  34.8 72.1 %copy-start.26 = (f32[36]{0:T(128)S(1)}, f32[36]{0:T(128)}, u32[]{:S(2)}) copy-start(f32[36]{0:T(128)} %param.23) | copy-start | bytes 436
  99.4 331.2 %all-to-all-start = ((f32[11664,8,36]{0,2,1:T(8,128)}), f32[11664,8,36]{0,2,1:T(8,128)}, u32[]{:S(2)}, u32[]{:S(2)}) async-start(f32[11664,8,36]{0,2,1:T(8,128)} %all_to_all.48), calls=%async_computation | async-start | bytes 30146560 | tf_op jit(solution)/shard_map/all_to_all | solution.py:71
  678.8 27.1 %copy-start.1 = (f32[14,14,4608]{2,1,0:T(8,128)S(1)}, f32[14,14,4608]{2,1,0:T(8,128)}, u32[]{:S(2)}) copy-start(f32[14,14,4608]{2,1,0:T(8,128)} %slice.82) | copy-start | bytes 10838020
  748.9 291.9 %all-to-all-start.1 = ((f32[8,3136,36]{1,2,0:T(8,128)}), f32[8,3136,36]{1,2,0:T(8,128)}, u32[]{:S(2)}, u32[]{:S(2)}) async-start(f32[8,3136,36]{1,2,0:T(8,128)} %copy.47), calls=%async_computation.1 | async-start | bytes 8192000 | tf_op jit(solution)/shard_map/all_to_all | solution.py:81
  1040.6 6.0 copy-start.3
  1040.6 342.8 %copy-start.2 = (f32[144,36]{0,1:T(8,128)S(1)}, f32[144,36]{0,1:T(8,128)}, u32[]{:S(2)}) copy-start(f32[144,36]{0,1:T(8,128)} %param.24) | copy-start | bytes 62212
  1040.6 364.3 %copy-start.28 = (u32[32]{0:T(128)S(1)}, u32[32]{0:T(128)}, u32[]{:S(2)}) copy-start(u32[32]{0:T(128)} %constant.88) | copy-start | bytes 388
  1040.6 383.0 %copy-start.29 = (f32[36]{0:T(128)S(1)}, f32[36]{0:T(128)}, u32[]{:S(2)}) copy-start(f32[36]{0:T(128)} %param.25) | copy-start | bytes 436
  1040.7 383.3 %copy-start.15 = (f32[4608]{0:T(1024)S(1)}, f32[4608]{0:T(1024)}, u32[]{:S(2)}) copy-start(f32[4608]{0:T(1024)} %get-tuple-element.30) | copy-start | bytes 55300
  1040.7 383.5 %copy-start.14 = (f32[4608]{0:T(1024)S(1)}, f32[4608]{0:T(1024)}, u32[]{:S(2)}) copy-start(f32[4608]{0:T(1024)} %get-tuple-element.29) | copy-start | bytes 55300
  1040.7 383.6 %copy-start.13 = (f32[4608]{0:T(1024)S(1)}, f32[4608]{0:T(1024)}, u32[]{:S(2)}) copy-start(f32[4608]{0:T(1024)} %get-tuple-element.28) | copy-start | bytes 55300
  1040.7 383.8 %copy-start.12 = (f32[4608]{0:T(1024)S(1)}, f32[4608]{0:T(1024)}, u32[]{:S(2)}) copy-start(f32[4608]{0:T(1024)} %get-tuple-element.27) | copy-start | bytes 55300
  1040.7 383.9 %copy-start.11 = (f32[4608]{0:T(1024)S(1)}, f32[4608]{0:T(1024)}, u32[]{:S(2)}) copy-start(f32[4608]{0:T(1024)} %get-tuple-element.26) | copy-start | bytes 55300
  1040.7 384.1 %copy-start.10 = (f32[4608]{0:T(1024)S(1)}, f32[4608]{0:T(1024)}, u32[]{:S(2)}) copy-start(f32[4608]{0:T(1024)} %get-tuple-element.25) | copy-start | bytes 55300
  1040.7 384.2 %copy-start.9 = (f32[4608]{0:T(1024)S(1)}, f32[4608]{0:T(1024)}, u32[]{:S(2)}) copy-start(f32[4608]{0:T(1024)} %get-tuple-element.24) | copy-start | bytes 55300
  1040.7 384.4 %copy-start.8 = (f32[4608]{0:T(1024)S(1)}, f32[4608]{0:T(1024)}, u32[]{:S(2)}) copy-start(f32[4608]{0:T(1024)} %get-tuple-element.23) | copy-start | bytes 55300
  1040.7 384.5 %copy-start.7 = (f32[4608]{0:T(1024)S(1)}, f32[4608]{0:T(1024)}, u32[]{:S(2)}) copy-start(f32[4608]{0:T(1024)} %get-tuple-element.22) | copy-start | bytes 55300
  1040.8 384.6 %copy-start.6 = (f32[4608]{0:T(1024)S(1)}, f32[4608]{0:T(1024)}, u32[]{:S(2)}) copy-start(f32[4608]{0:T(1024)} %get-tuple-element.21) | copy-start | bytes 55300
  1040.8 409.2 %copy-start.27 = (f32[36]{0:T(128)S(1)}, f32[36]{0:T(128)}, u32[]{:S(2)}) copy-start(f32[36]{0:T(128)} %param.23) | copy-start | bytes 436
  1040.8 409.2 %copy-start.30 = (f32[36]{0:T(128)S(1)}, f32[36]{0:T(128)}, u32[]{:S(2)}) copy-start(f32[36]{0:T(128)} %param.29) | copy-start | bytes 436
  1040.8 409.2 %copy-start.31 = (f32[36]{0:T(128)S(1)}, f32[36]{0:T(128)}, u32[]{:S(2)}) copy-start(f32[36]{0:T(128)} %param.33) | copy-start | bytes 436
  1040.8 409.2 %copy-start.32 = (f32[36]{0:T(128)S(1)}, f32[36]{0:T(128)}, u32[]{:S(2)}) copy-start(f32[36]{0:T(128)} %param.31) | copy-start | bytes 436
  1040.8 409.2 %copy-start.33 = (f32[36]{0:T(128)S(1)}, f32[36]{0:T(128)}, u32[]{:S(2)}) copy-start(f32[36]{0:T(128)} %param.27) | copy-start | bytes 436
  1040.8 410.3 %copy-start.17 = (f32[36,9]{0,1:T(8,128)S(1)}, f32[36,9]{0,1:T(8,128)}, u32[]{:S(2)}) copy-start(f32[36,9]{0,1:T(8,128)} %param.22) | copy-start | bytes 3892
  1040.8 410.3 %copy-start.23 = (f32[36,9]{0,1:T(8,128)S(1)}, f32[36,9]{0,1:T(8,128)}, u32[]{:S(2)}) copy-start(f32[36,9]{0,1:T(8,128)} %param.26) | copy-start | bytes 3892
  1040.8 410.3 %copy-start.24 = (f32[36,9]{0,1:T(8,128)S(1)}, f32[36,9]{0,1:T(8,128)}, u32[]{:S(2)}) copy-start(f32[36,9]{0,1:T(8,128)} %param.30) | copy-start | bytes 3892
  1040.9 439.4 %all-to-all-start.3 = ((f32[8,11664,36]{1,2,0:T(8,128)}), f32[8,11664,36]{1,2,0:T(8,128)}, u32[]{:S(2)}, u32[]{:S(2)}) async-start(f32[8,11664,36]{1,2,0:T(8,128)} %copy.49), calls=%async_computation.3 | async-start | bytes 30146560 | tf_op jit(solution)/shard_map/all_to_all | solution.py:118
  1046.6 405.2 %copy-start.18 = (f32[144,36]{0,1:T(8,128)S(1)}, f32[144,36]{0,1:T(8,128)}, u32[]{:S(2)}) copy-start(f32[144,36]{0,1:T(8,128)} %param.28) | copy-start | bytes 62212
  1046.6 405.2 %copy-start.19 = (f32[144,36]{0,1:T(8,128)S(1)}, f32[144,36]{0,1:T(8,128)}, u32[]{:S(2)}) copy-start(f32[144,36]{0,1:T(8,128)} %param.32) | copy-start | bytes 62212
  1046.6 427.7 %copy-start.34 = (f32[36]{0:T(128)S(1)}, f32[36]{0:T(128)}, u32[]{:S(2)}) copy-start(f32[36]{0:T(128)} %param.35) | copy-start | bytes 436
  1046.7 428.2 %copy-start.35 = (f32[36]{0:T(128)S(1)}, f32[36]{0:T(128)}, u32[]{:S(2)}) copy-start(f32[36]{0:T(128)} %param.37) | copy-start | bytes 436
  1046.7 428.7 %copy-start.25 = (f32[36,9]{0,1:T(8,128)S(1)}, f32[36,9]{0,1:T(8,128)}, u32[]{:S(2)}) copy-start(f32[36,9]{0,1:T(8,128)} %param.34) | copy-start | bytes 3892
  1046.7 429.3 %copy-start.20 = (f32[144,36]{0,1:T(8,128)S(1)}, f32[144,36]{0,1:T(8,128)}, u32[]{:S(2)}) copy-start(f32[144,36]{0,1:T(8,128)} %param.36) | copy-start | bytes 62212
  1379.6 44.2 %collective-permute-start = (f32[144,28]{0,1:T(8,128)S(1)}, f32[144,28]{0,1:T(8,128)S(1)}, u32[]{:S(2)}, u32[]{:S(2)}) collective-permute-start(f32[144,28]{0,1:T(8,128)S(1)} %slice.86), channel_id=1, source_target_pairs={{0,1},{1,2},{2,3},{3,4},{4,5},{5,6},{6,7},{8,9},{9,10},{10,11},{11... | collective-permute-start | bytes 48392
  1451.8 28.5 %copy-start.21 = (f32[36,9]{0,1:T(8,128)}, f32[36,9]{0,1:T(8,128)S(1)}, u32[]{:S(2)}) copy-start(f32[36,9]{0,1:T(8,128)S(1)} %get-tuple-element.66) | copy-start | bytes 3892
  1451.8 28.5 %copy-start.22 = (f32[36,9]{0,1:T(8,128)}, f32[36,9]{0,1:T(8,128)S(1)}, u32[]{:S(2)}) copy-start(f32[36,9]{0,1:T(8,128)S(1)} %get-tuple-element.67) | copy-start | bytes 3892
  1452.4 27.8 %copy-start.4 = (f32[144,36]{0,1:T(8,128)}, f32[144,36]{0,1:T(8,128)S(1)}, u32[]{:S(2)}) copy-start(f32[144,36]{0,1:T(8,128)S(1)} %get-tuple-element.60) | copy-start | bytes 62212
  1452.5 27.8 %copy-start.5 = (f32[144,36]{0,1:T(8,128)}, f32[144,36]{0,1:T(8,128)S(1)}, u32[]{:S(2)}) copy-start(f32[144,36]{0,1:T(8,128)S(1)} %get-tuple-element.61) | copy-start | bytes 62212
where the time goes:
time: 1530 us; the launch traced here: 1520 us
  local copies, waits for them, and re-layouts  589 us (38%)
  blocking collectives  408 us (27%)
  waiting for transfers between devices  345 us (23%)
  other arithmetic  136 us (9%)
  starting transfers between devices  27.2 us (2%)
    unnamed x3, blocking collectives  363 us
    all_to_all x1, waiting for transfers between devices, per_device(): lax.all_to_all(doubled, 'chan', split_axis=1, concat_axis=0, tiled=True)  280 us
    slice x9, local copies, waits for them, and re-layouts, per_device(): window = padded[row_tap:row_tap + span:2, col_tap:col_tap + span:2]  162 us
    all_to_all x2, local copies, waits for them, and re-layouts, per_device(): lax.all_to_all(back_cols, 'chan', split_axis=0, concat_axis=1, tiled=True)  95.3 us
    unnamed x85, local copies, waits for them, and re-layouts  80.2 us
    all_to_all x1, waiting for transfers between devices, per_device(): lax.all_to_all(pooled_cot[0], 'chan', split_axis=1, concat_axis=0, tiled=...  64.6 us
    add x2, other arithmetic, per_device(): back + lax.pad(spread_back, zero, ((row_tap, 2 - row_tap, 1), (col_tap, 2...  63.9 us
    pad x3, local copies, waits for them, and re-layouts, per_device(): lax.pad(spread_back, zero, ((row_tap, 2 - row_tap, 1), (col_tap, 2 - col_...  48.1 us
  transfers between devices with their start and end apart: 5, of which 2 were waited for; matrix products, arithmetic and copies ran while one was open for 41% of the time, Pallas kernels for 0%

commit v1 on v0

v1 whole, which is shorter than its diff:
```python
import functools

import jax
import jax.numpy as jnp
import numpy as np
from jax import lax
from jax.experimental import pallas as pl
from jax.experimental.pallas import tpu as pltpu
from jax.sharding import PartitionSpec as P

GRID = 27
TAPS = 9
OUTG = 14
LANES = 128
SUBL = 8

beta_one = 0.9
beta_two = 0.999
fix_first = 1.0 - 0.9**10
fix_second = 1.0 - 0.999**10
small_eps = 1e-06
learn_rate = 0.5
keep_rate = 0.9
highest = lax.Precision.HIGHEST


def make_plan(groups, images, n_in, n_out):
    tiles_img = images // LANES
    n_tiles = OUTG * OUTG * tiles_img
    tap_tile = np.full((n_tiles, TAPS), -1, np.int64)
    for i in range(OUTG):
        for j in range(OUTG):
            for it in range(tiles_img):
                for a in range(3):
                    for e in range(3):
                        r, s = 2 * i + a - 1, 2 * j + e - 1
                        if 0 <= r < GRID and 0 <= s < GRID:
                            tap_tile[(i * OUTG + j) * tiles_img + it, 3 * a + e] = (
                                r * GRID + s
                            ) * tiles_img + it
    step = int(np.gcd(np.gcd(n_in, n_out), LANES))
    wanted = {}
    for lane in range(0, LANES, step):
        p_owner = (np.arange(n_tiles) * LANES + lane) // n_out
        t_owner = (tap_tile * LANES + lane) // n_in
        for p in range(n_tiles):
            k = int(p_owner[p])
            for t in range(TAPS):
                if tap_tile[p, t] >= 0 and t_owner[p, t] != k:
                    wanted.setdefault((k, int(t_owner[p, t])), set()).add(p)
    messages = sorted(wanted.items(), key=lambda kv: (-len(kv[1]), kv[0]))
    ops = []
    for (src, dst), tiles in messages:
        for op in ops:
            if (
                op["size"] - len(tiles) <= 1
                and all(src != s and dst != d for s, d in op["pairs"])
            ):
                break
        else:
            op = {"size": len(tiles), "pairs": [], "tiles": []}
            ops.append(op)
        op["pairs"].append((src, dst))
        op["tiles"].append(sorted(tiles))
    in_base = np.arange(groups) * n_in // LANES
    in_shift = np.arange(groups) * n_in % LANES
    out_base = np.arange(groups) * n_out // LANES
    out_shift = np.arange(groups) * n_out % LANES
    in_tiles = int(max(-(-(in_shift + n_in) // LANES)))
    out_tiles = int(max(-(-(out_shift + n_out) // LANES)))
    sizes = [op["size"] for op in ops]
    halo = sum(sizes)
    own_slot = np.full((groups, halo), out_tiles, np.int64)
    taps = np.full((groups, out_tiles + halo, TAPS), in_tiles, np.int64)

    def tap_rows(device, p):
        local = tap_tile[p] - in_base[device]
        first, last = device * n_in, (device + 1) * n_in
        held = (
            (tap_tile[p] >= 0)
            & (tap_tile[p] * LANES < last)
            & ((tap_tile[p] + 1) * LANES > first)
        )
        return np.where(held, local, in_tiles)

    for k in range(groups):
        for j in range(out_tiles):
            if out_base[k] + j < n_tiles:
                taps[k, j] = tap_rows(k, out_base[k] + j)
    start = 0
    for op in ops:
        for (src, dst), tiles in zip(op["pairs"], op["tiles"]):
            for j, p in enumerate(tiles):
                own_slot[src, start + j] = p - out_base[src]
                taps[dst, out_tiles + start + j] = tap_rows(dst, p)
        start += op["size"]
    table = np.concatenate(
        [
            in_shift[:, None],
            out_shift[:, None],
            own_slot,
            taps.reshape(groups, -1),
        ],
        axis=1,
    ).astype(np.int32)
    return {
        "ops": ops,
        "sizes": sizes,
        "halo": halo,
        "in_tiles": in_tiles,
        "out_tiles": out_tiles,
        "n_in": n_in,
        "n_out": n_out,
        "table": table,
        "slot_at": 2,
        "taps_at": 2 + halo,
    }


def lane_ids():
    return lax.broadcasted_iota(jnp.int32, (SUBL, LANES), 1)


def align_into(load, store, n_local, tiles, shift):
    lane = lane_ids()
    zero = jnp.zeros((SUBL, LANES), jnp.float32)
    local_tiles = -(-n_local // LANES)
    before = zero
    for t in range(tiles):
        if t < local_tiles:
            now = load(t)
            if (t + 1) * LANES > n_local:
                now = jnp.where(lane < n_local - t * LANES, now, 0.0)
            now = pltpu.roll(now, shift, 1)
        else:
            now = zero
        store(t, jnp.where(lane < shift, before, now))
        before = now
    store(tiles, zero)


def unalign_from(load, store, n_local, tiles, shift):
    lane = lane_ids()
    local_tiles = -(-n_local // LANES)
    back = lax.rem(LANES - shift, LANES)
    now = pltpu.roll(load(0), back, 1)
    for t in range(local_tiles):
        later = pltpu.roll(load(t + 1), back, 1) if t + 1 < tiles else now
        store(t, jnp.where(lane < LANES - shift, now, later))
        now = later


def tile_lanes(t):
    return slice(t * LANES, (t + 1) * LANES)


def rows_of(part):
    return slice(part * SUBL, (part + 1) * SUBL)


def of_half(half):
    return pl.ds(half, SUBL, stride=2)


def align_cot(cot_ref, held, plan, shift):
    for part in range(2):
        align_into(
            lambda t: cot_ref[rows_of(part), tile_lanes(t)],
            lambda t, v: held.__setitem__((t, rows_of(part)), v),
            plan["n_out"],
            plan["out_tiles"],
            shift,
        )


def align_patches(x_ref, held, plan, shift):
    align_into(
        lambda t: x_ref[:, tile_lanes(t)],
        lambda t, v: held.__setitem__(t, v),
        plan["n_in"],
        plan["in_tiles"],
        shift,
    )


def tap_weights(w_ref, half, count):
    rows = w_ref[of_half(half), :]
    return [jnp.broadcast_to(rows[:, t : t + 1], (SUBL, LANES)) for t in range(count)]


def tap_slots(tab, plan, entry):
    at = plan["taps_at"] + entry * TAPS
    return [tab[at + t] for t in range(TAPS)]


def add_up(items):
    items = list(items)
    while len(items) > 1:
        items = [
            items[i] + items[i + 1] if i + 1 < len(items) else items[i]
            for i in range(0, len(items), 2)
        ]
    return items[0]


def pack_kernel(plan, tab, cot_ref, *refs):
    outs, held = refs[:-1], refs[-1]
    align_cot(cot_ref, held, plan, tab[1])
    at = plan["slot_at"]
    for out, size in zip(outs, plan["sizes"]):
        for j in range(size):
            slot = tab[at + j]
            out[j] = held[slot]
        at += size


def forward_kernel(plan, own, tab, x_ref, w_ref, *refs):
    outs, held = refs[:-1], refs[-1]
    align_patches(x_ref, held, plan, tab[0])
    count = TAPS + 1 if own else TAPS
    weights = [tap_weights(w_ref, half, count) for half in range(2)]

    def one(out, j, entry):
        slots = tap_slots(tab, plan, entry)
        tiles = [held[s] for s in slots]
        for half in range(2):
            total = add_up([tiles[t] * weights[half][t] for t in range(TAPS)])
            if own:
                total = total + weights[half][TAPS]
            out[j, of_half(half)] = total

    if own:
        for j in range(plan["out_tiles"]):
            one(outs[0], j, j)
    else:
        entry = plan["out_tiles"]
        for out, size in zip(outs, plan["sizes"]):
            for j in range(size):
                one(out, j, entry + j)
            entry += size


def backward_kernel(plan, tab, x_ref, cot_ref, w_ref, *refs):
    n_ops = len(plan["sizes"])
    halos = refs[:n_ops]
    grad_ref, sums_ref, held_x, held_c, back = refs[n_ops:]
    align_patches(x_ref, held_x, plan, tab[0])
    align_cot(cot_ref, held_c, plan, tab[1])
    zero = jnp.zeros((SUBL, LANES), jnp.float32)
    for t in range(plan["in_tiles"] + 1):
        back[t] = zero
    weights = [tap_weights(w_ref, half, TAPS) for half in range(2)]

    def one(source, j, entry, total, own):
        slots = tap_slots(tab, plan, entry)
        cots = [source[j, of_half(half)] for half in range(2)]
        total = list(total)
        for t in range(TAPS):
            tile = held_x[slots[t]]
            for half in range(2):
                total[2 * t + half] = total[2 * t + half] + cots[half] * tile
            back[slots[t]] = back[slots[t]] + (
                cots[0] * weights[0][t] + cots[1] * weights[1][t]
            )
        if own:
            for half in range(2):
                total[2 * TAPS + half] = total[2 * TAPS + half] + cots[half]
        return tuple(total)

    total = (zero,) * (2 * TAPS + 2)
    for j in range(plan["out_tiles"]):
        total = one(held_c, j, j, total, True)
    entry = plan["out_tiles"]
    for halo, size in zip(halos, plan["sizes"]):
        for j in range(size):
            total = one(halo, j, entry + j, total, False)
        entry += size
    unalign_from(
        lambda t: back[t],
        lambda t, v: grad_ref.__setitem__((slice(None), tile_lanes(t)), v),
        plan["n_in"],
        plan["in_tiles"],
        tab[0],
    )
    lane = lane_ids()
    for half in range(2):
        row = zero
        for t in range(TAPS + 1):
            row = jnp.where(lane == t, jnp.sum(total[2 * t + half], axis=1, keepdims=True), row)
        sums_ref[of_half(half), :] = row


def finish_kernel(plan, tab, own_ref, *refs):
    n_ops = len(plan["sizes"])
    halos = refs[:n_ops]
    out_ref, held = refs[n_ops:]
    tiles = plan["out_tiles"]
    for t in range(tiles):
        held[t] = own_ref[t]
    at = plan["slot_at"]
    for halo, size in zip(halos, plan["sizes"]):
        for j in range(size):
            slot = tab[at + j]
            held[slot] = held[slot] + halo[j]
        at += size
    for part in range(2):
        unalign_from(
            lambda t: held[t, rows_of(part)],
            lambda t, v: out_ref.__setitem__((rows_of(part), tile_lanes(t)), v),
            plan["n_out"],
            tiles,
            tab[1],
        )


def call(kernel, table, operands, in_specs, outs, out_specs, scratch, steps, flops):
    moved = sum(4 * int(np.prod(a.shape)) for a in operands) + sum(
        4 * int(np.prod(o.shape)) for o in outs
    )
    return pl.pallas_call(
        kernel,
        grid_spec=pltpu.PrefetchScalarGridSpec(
            num_scalar_prefetch=1,
            grid=(steps,),
            in_specs=in_specs,
            out_specs=out_specs,
            scratch_shapes=scratch,
        ),
        out_shape=outs,
        compiler_params=pltpu.CompilerParams(
            dimension_semantics=("arbitrary",), vmem_limit_bytes=32 * 1024 * 1024
        ),
        cost_estimate=pl.CostEstimate(flops=flops, bytes_accessed=moved, transcendentals=0),
    )(table, *operands)


def round_up(n, m):
    return -(-n // m) * m


def f32(*shape):
    return jax.ShapeDtypeStruct(shape, jnp.float32)


def swap(x, axis, bit):
    size = lax.axis_size(axis)
    return lax.ppermute(x, axis, [(k, k ^ bit) for k in range(size)])


def bits_of(axis):
    size = lax.axis_size(axis)
    assert size & (size - 1) == 0
    bits, b = [], 1
    while b < size:
        bits.append(b)
        b *= 2
    return bits


def sum_over(x, axis):
    for bit in reversed(bits_of(axis)):
        x = x + swap(x, axis, bit)
    return x


def gather_over(x, axis):
    me = lax.axis_index(axis)
    size = lax.axis_size(axis)
    every = jnp.zeros((size,) + x.shape, x.dtype)
    every = lax.dynamic_update_index_in_dim(every, x, me, 0)
    for bit in bits_of(axis):
        base = me // bit * bit
        block = lax.dynamic_slice_in_dim(every, base, bit, 0)
        block = swap(block, axis, bit)
        every = lax.dynamic_update_slice_in_dim(every, block, base ^ bit, 0)
    return every


def moments(weight, grad, first, second, decay):
    first_new = beta_one * first + (1.0 - beta_one) * grad
    second_new = beta_two * second + (1.0 - beta_two) * grad * grad
    update = (
        first_new / fix_first / (jnp.sqrt(second_new / fix_second) + small_eps) + decay * weight
    )
    return (first_new, second_new, update)


def per_device(
    patches,
    class_in,
    conv_weight,
    conv_bias,
    head_weight,
    head_bias,
    first_conv_w,
    first_conv_b,
    first_head_w,
    first_head_b,
    second_conv_w,
    second_conv_b,
    second_head_w,
    second_head_b,
    average_conv_w,
    average_conv_b,
    average_head_w,
    average_head_b,
    pooled_cot,
    class_cot,
):
    groups = lax.axis_size("chan")
    me = lax.axis_index("chan")
    per_dev = conv_weight.shape[0]
    n_in, channels_in = patches.shape[1:]
    n_out, channels = pooled_cot.shape[1:]
    local_images = class_in.shape[1]
    images = local_images * groups
    plan = make_plan(groups, images, n_in, n_out)
    sizes, tiles, in_tiles = plan["sizes"], plan["out_tiles"], plan["in_tiles"]
    table = lax.dynamic_index_in_dim(jnp.asarray(plan["table"]), me, 0, keepdims=False)
    steps = channels_in // SUBL
    x = patches[0].T
    cot = pooled_cot[0].T
    in_lanes, out_lanes = round_up(n_in, LANES), round_up(n_out, LANES)
    x_spec = pl.BlockSpec((SUBL, in_lanes), lambda g, tab: (g, 0))
    cot_spec = pl.BlockSpec((2 * SUBL, out_lanes), lambda g, tab: (g, 0))
    halo_specs = [
        pl.BlockSpec((n, 2 * SUBL, LANES), lambda g, tab: (0, g, 0)) for n in sizes
    ]
    halo_outs = [f32(n, channels, LANES) for n in sizes]
    own_spec = pl.BlockSpec((tiles, 2 * SUBL, LANES), lambda g, tab: (0, g, 0))
    w_spec = pl.BlockSpec((2 * SUBL, LANES), lambda g, tab: (g, 0))
    macs = n_out * channels * TAPS

    sends = call(
        functools.partial(pack_kernel, plan),
        table,
        [cot],
        [cot_spec],
        halo_outs,
        halo_specs,
        [pltpu.VMEM((tiles + 1, 2 * SUBL, LANES), jnp.float32)],
        steps,
        1000,
    )
    cot_halo = [
        lax.ppermute(s, "chan", op["pairs"]) for s, op in zip(sends, plan["ops"])
    ]

    stack3 = [
        jnp.concatenate([w, b[:, None]], axis=1)
        for w, b in (
            (conv_weight, conv_bias),
            (first_conv_w, first_conv_b),
            (second_conv_w, second_conv_b),
        )
    ]
    pieces = [*stack3, head_weight, head_bias, class_in[0], class_cot[0]]
    flat = jnp.concatenate([p.reshape(-1) for p in pieces])
    rows = round_up(flat.shape[0], SUBL * LANES)
    flat = jnp.pad(flat, (0, rows - flat.shape[0])).reshape(-1, LANES)
    full = gather_over(flat, "chan").reshape(groups, -1)
    whole, at = [], 0
    for p in pieces:
        n = int(np.prod(p.shape))
        whole.append(full[:, at : at + n].reshape((groups,) + p.shape))
        at += n
    conv_all, first_all, second_all = [w.reshape(channels, TAPS + 1) for w in whole[:3]]
    head_all = jnp.moveaxis(whole[3], 0, 1).reshape(channels_in, channels)
    head_b_all = whole[4].reshape(channels)
    class_all = whole[5].reshape(images, channels_in)
    class_cot_all = whole[6].reshape(images, channels)

    conv_lanes = jnp.pad(conv_all, ((0, 0), (0, LANES - TAPS - 1)))
    partials = call(
        functools.partial(forward_kernel, plan, False),
        table,
        [x, conv_lanes],
        [x_spec, w_spec],
        halo_outs,
        halo_specs,
        [pltpu.VMEM((in_tiles + 1, SUBL, LANES), jnp.float32)],
        steps,
        2 * macs,
    )
    pooled_halo = [
        lax.ppermute(s, "chan", [(d, s_) for s_, d in op["pairs"]])
        for s, op in zip(partials, plan["ops"])
    ]
    pooled_own = call(
        functools.partial(forward_kernel, plan, True),
        table,
        [x, conv_lanes],
        [x_spec, w_spec],
        [f32(tiles, channels, LANES)],
        [own_spec],
        [pltpu.VMEM((in_tiles + 1, SUBL, LANES), jnp.float32)],
        steps,
        2 * macs,
    )[0]
    x_grad, sums = call(
        functools.partial(backward_kernel, plan),
        table,
        [x, cot, conv_lanes, *cot_halo],
        [x_spec, cot_spec, w_spec, *halo_specs],
        [f32(channels_in, n_in), f32(channels, LANES)],
        [x_spec, pl.BlockSpec((2 * SUBL, LANES), lambda g, tab: (g, 0))],
        [
            pltpu.VMEM((in_tiles + 1, SUBL, LANES), jnp.float32),
            pltpu.VMEM((tiles + 1, 2 * SUBL, LANES), jnp.float32),
            pltpu.VMEM((in_tiles + 1, SUBL, LANES), jnp.float32),
        ],
        steps,
        4 * macs,
    )
    pooled = call(
        functools.partial(finish_kernel, plan),
        table,
        [pooled_own, *pooled_halo],
        [own_spec, *halo_specs],
        [f32(channels, n_out)],
        [cot_spec],
        [pltpu.VMEM((tiles + 1, 2 * SUBL, LANES), jnp.float32)],
        steps,
        1000,
    )[0]

    local_class, local_class_cot = class_in[0], class_cot[0]
    class_out = jnp.dot(local_class, head_all, precision=highest) + head_b_all
    class_grad = jnp.dot(local_class_cot, head_all.T, precision=highest)
    my_cot = lax.dynamic_slice_in_dim(class_cot_all, me * per_dev, per_dev, 1)
    grad_h = jnp.concatenate(
        [jnp.dot(class_all.T, my_cot, precision=highest), jnp.sum(my_cot, axis=0)[None]], axis=0
    )
    grad_h = sum_over(grad_h, "dp")
    head_w_set = moments(head_weight, grad_h[:channels_in], first_head_w, second_head_w, 0.05)
    head_b_set = moments(head_bias, grad_h[channels_in], first_head_b, second_head_b, 0.0)
    norms = jnp.stack([jnp.sum(head_w_set[2] ** 2), jnp.sum(head_b_set[2] ** 2)])
    norms = jnp.where(lax.axis_index("dp") == 0, norms, 0.0)

    mine = jnp.zeros((2 * SUBL, round_up(channels, LANES)), jnp.float32)
    mine = mine.at[: TAPS + 1, :channels].set(sums[:, : TAPS + 1].T)
    mine = mine.at[TAPS + 1, :2].set(norms)
    mine = sum_over(sum_over(mine, "dp"), "chan")
    grad_all = mine[: TAPS + 1, :channels].T
    head_norms = mine[TAPS + 1, :2]
    wide_w = moments(conv_all[:, :TAPS], grad_all[:, :TAPS], first_all[:, :TAPS], second_all[:, :TAPS], 0.05)
    wide_b = moments(conv_all[:, TAPS], grad_all[:, TAPS], first_all[:, TAPS], second_all[:, TAPS], 0.0)
    weight_sq = [
        jnp.sum(conv_all[:, :TAPS] ** 2),
        jnp.sum(conv_all[:, TAPS] ** 2),
        jnp.sum(head_all**2),
        jnp.sum(head_b_all**2),
    ]
    update_sq = [jnp.sum(wide_w[2] ** 2), jnp.sum(wide_b[2] ** 2), head_norms[0], head_norms[1]]
    ratios = [jnp.sqrt(weight_sq[k]) / jnp.sqrt(update_sq[k]) for k in range(4)]

    def cut(v):
        return lax.dynamic_slice_in_dim(v, me * per_dev, per_dev, 0)

    sets = (tuple(cut(v) for v in wide_w), tuple(cut(v) for v in wide_b), head_w_set, head_b_set)
    weights = (conv_weight, conv_bias, head_weight, head_bias)
    averages = (average_conv_w, average_conv_b, average_head_w, average_head_b)
    results = []
    for k in range(4):
        weight_new = weights[k] - learn_rate * ratios[k] * sets[k][2]
        average_new = keep_rate * averages[k] + (1.0 - keep_rate) * weight_new
        results.extend([sets[k][0], sets[k][1], weight_new, average_new])
    trust = jnp.stack(ratios)
    return tuple(
        [pooled.T[None], class_out[None], x_grad.T[None], class_grad[None]] + results + [trust]
    )


def solution(mesh):
    return jax.shard_map(
        per_device,
        mesh=mesh,
        in_specs=(
            P("dp", "chan", None),
            P("dp", "chan", None),
            P("chan", None),
            P("chan"),
            P(None, "chan"),
            P("chan"),
            P("chan", None),
            P("chan"),
            P(None, "chan"),
            P("chan"),
            P("chan", None),
            P("chan"),
            P(None, "chan"),
            P("chan"),
            P("chan", None),
            P("chan"),
            P(None, "chan"),
            P("chan"),
            P("dp", "chan", None),
            P("dp", "chan", None),
        ),
        out_specs=(
            P("dp", "chan", None),
            P("dp", "chan", None),
            P("dp", "chan", None),
            P("dp", "chan", None),
            P("chan", None),
            P("chan", None),
            P("chan", None),
            P("chan", None),
            P("chan"),
            P("chan"),
            P("chan"),
            P("chan"),
            P(None, "chan"),
            P(None, "chan"),
            P(None, "chan"),
            P(None, "chan"),
            P("chan"),
            P("chan"),
            P("chan"),
            P("chan"),
            P(),
        ),
        check_vma=False,
    )
```

time: 1530 us -> 307 us (0.20)
  local copies, waits for them, and re-layouts: 589 us -> 60.3 us
  blocking collectives: 408 us -> 0 us
  waiting for transfers between devices: 345 us -> 68.6 us
  other arithmetic: 136 us -> 26.5 us
  Pallas kernels: 0 us -> 104 us
    unnamed x3 -> x0, blocking collectives: 363 us -> none
    all_to_all x4 -> x0, waiting for transfers between devices: 345 us -> none  [the longest x1 280 us: per_device(): lax.all_to_all(doubled, 'chan', split_axis=1, concat_axis=0, tiled=True)]
    all_to_all x8 -> x0, local copies, waits for them, and re-layouts: 180 us -> none  [the longest x2 95.3 us: per_device(): lax.all_to_all(back_cols, 'chan', split_axis=0, concat_axis=1, tiled=True)]
    slice x10 -> x6, local copies, waits for them, and re-layouts: 178 us -> 7.28 us  [the longest x4 5.77 us: per_device(): whole.append(full[:, at:at + n].reshape((groups,) + p.shape))]
    pallas_call x0 -> x5, Pallas kernels: none -> 104 us  [call(): pl.pallas_call(kernel, grid_spec=pltpu.PrefetchScalarGridSpec(num_scalar_...]
    add x3 -> x7, other arithmetic: 78.4 us -> 3.38 us  [sum_over(): x = x + swap(x, axis, bit)]
    reshape x13 -> x6, local copies, waits for them, and re-layouts: 76.2 us -> 2.58 us  [the longest x1 2.13 us: per_device(): whole.append(full[:, at:at + n].reshape((groups,) + p.shape))]
    ppermute x0 -> x18, waiting for transfers between devices: none -> 68.6 us  [the longest x4 27 us: per_device(): lax.ppermute(s, 'chan', op['pairs'])]
  transfers between devices with their start and end apart: 5 -> 18, of which waited for: 2 -> 9; matrix products, arithmetic and copies ran while one was open for 41% -> 19% of each run, Pallas kernels for 0% -> 10%
where the time goes in v1:
time: 307 us; the launch traced here: 302 us
  Pallas kernels  104 us (34%)
  waiting for transfers between devices  68.6 us (22%)
  local copies, waits for them, and re-layouts  60.3 us (20%)
  starting transfers between devices  32.7 us (11%)
  other arithmetic  26.5 us (9%)
  between operations  6.73 us (2%)
  matrix products  3.17 us (1%)
    pallas_call x5, Pallas kernels, call(): pl.pallas_call(kernel, grid_spec=pltpu.PrefetchScalarGridSpec(num_scalar_...  104 us
    ppermute x4, waiting for transfers between devices, per_device(): lax.ppermute(s, 'chan', op['pairs'])  27 us
    unnamed x65, local copies, waits for them, and re-layouts  22.5 us
    ppermute x4, waiting for transfers between devices, per_device(): lax.ppermute(s, 'chan', [(d, s_) for s_, d in op['pairs']])  21.1 us
    ppermute x10, waiting for transfers between devices, swap(): return lax.ppermute(x, axis, [(k, k ^ bit) for k in range(size)])  20.5 us
    ppermute x10, starting transfers between devices, swap(): return lax.ppermute(x, axis, [(k, k ^ bit) for k in range(size)])  13.2 us
    ppermute x4, starting transfers between devices, per_device(): lax.ppermute(s, 'chan', [(d, s_) for s_, d in op['pairs']])  11.5 us
    dynamic_update_slice x3, local copies, waits for them, and re-layouts, gather_over(): every = lax.dynamic_update_slice_in_dim(every, block, base ^ bit, 0)  11 us
  transfers between devices with their start and end apart: 18, of which 9 were waited for; matrix products, arithmetic and copies ran while one was open for 19% of the time, Pallas kernels for 10%

profile of v1, /device:TPU:9, one launch (start us, length us, event | category | flops | bytes accessed | tf_op | source)
XLA Modules:
  0.0 302.2 jit_solution(4979001295127900647)
XLA Ops:
  6.9 2.8 dynamic_update_slice.13
  9.8 1.3 collective-permute-start
  11.1 1.7 collective-permute-done
  12.8 2.8 dynamic_update_slice.14
  15.8 3.5 %collective-permute-done.1 = f32[2,104,128]{2,0,1:T(2,128)S(1)} collective-permute-done((f32[2,104,128]{2,0,1:T(2,128)S(1)}, f32[2,104,128]{2,0,1:T(2,128)S(1)}, u32[]{:S(2)}, u32[]{:S(2)}) %collective-permute-start.1) | collective-permute-done | bytes 106528 | tf_op jit(solution)/shard_map/ppermute | solution.py:347
  19.3 4.4 %dynamic_update_slice.15 = f32[8,104,128]{2,0,1:T(8,128)S(1)} dynamic-update-slice(f32[8,104,128]{2,0,1:T(8,128)S(1)} %dynamic_update_slice.14, f32[2,104,128]{2,0,1:T(2,128)S(1)} %collective-permute-done.1, s32[]{:T(128)S(6)} %select_n.57, s32[]{:T(128)} %constant.149.clone.1, s32[]{:T(128)} %constant.149.clone.1) | dynamic-update-slice | bytes 212996 | tf_op jit(solution)/shard_map/dynamic_update_slice | solution.py:375
  24.5 2.3 collective-permute-start.2
  27.6 2.0 copy-done.2
  29.6 8.3 %shard_map.367 = (f32[11,288,128]{2,1,0:T(8,128)}, f32[8,288,128]{2,1,0:T(8,128)}, f32[6,288,128]{2,1,0:T(8,128)}, f32[4,288,128]{2,1,0:T(8,128)}) custom-call(s32[517]{0:T(1024)S(1)} %dynamic-slice_reduce_fusion.1.tab, f32[288,3136]{1,0:T(8,128)S(1)} %bitcast.56), custom_call_target="tpu_custom_call" | custom-call | flops 1000 | bytes 7888896 | tf_op jit(solution)/shard_map/pallas_call | solution.py:320
  37.9 3.2 %collective-permute-start.10 = (f32[4,288,128]{2,1,0:T(8,128)}, f32[4,288,128]{2,1,0:T(8,128)S(1)}, u32[]{:S(2)}, u32[]{:S(2)}) collective-permute-start(f32[4,288,128]{2,1,0:T(8,128)} %get-tuple-element.62), channel_id=1, source_target_pairs={{2,3},{5,4},{10,11},{13,12},{18,19},{21,20},{26,27},{29,28}} | collective-permute-start | bytes 1769480 | tf_op jit(solution)/shard_map/ppermute | solution.py:446
  41.0 1.7 collective-permute-start.9
  42.7 1.9 collective-permute-start.8
  44.6 1.3 collective-permute-start.7
  47.3 3.9 %dynamic_update_slice.16 = f32[8,104,128]{2,0,1:T(8,128)} dynamic-update-slice(f32[8,104,128]{2,0,1:T(8,128)} %copy-done.7, f32[4,104,128]{2,0,1:T(4,128)} %collective-permute-done.2, s32[]{:T(128)S(6)} %select_n.60, s32[]{:T(128)} %constant.149.clone.1, s32[]{:T(128)} %constant.149.clone.1) | dynamic-update-slice | bytes 425988 | tf_op jit(solution)/shard_map/dynamic_update_slice | solution.py:375
  51.2 1.6 slice.135
  52.8 1.0 slice.136
  53.8 1.7 reshape_reshape.17
  56.3 1.0 dynamic-slice_reduce_fusion
  57.4 1.3 fusion.4
  58.8 1.2 collective-permute-start.11
  60.0 1.5 fusion.18
  62.7 4.4 %collective-permute-start.12 = (f32[145,36]{0,1:T(8,128)}, f32[145,36]{0,1:T(8,128)}, u32[]{:S(2)}, u32[]{:S(2)}) collective-permute-start(f32[145,36]{0,1:T(8,128)} %fusion.25), channel_id=1, source_target_pairs={{0,8},{8,0},{16,24},{24,16},{1,9},{9,1},{17,25},{25,17},{2,10},{10... | collective-permute-start | bytes 62648 | tf_op jit(solution)/shard_map/ppermute | solution.py:347
  67.1 2.0 multiply_reduce_fusion.6
  69.0 1.7 slice.131
  72.4 2.1 reshape.165
  75.5 1.8 multiply_reduce_fusion.8
  77.4 2.1 multiply_reduce_fusion.5
  79.4 1.9 maximum_select_fusion
  81.3 27.0 %collective-permute-done.7.refs_0_ = f32[11,288,128]{2,1,0:T(8,128)S(1)} collective-permute-done((f32[11,288,128]{2,1,0:T(8,128)}, f32[11,288,128]{2,1,0:T(8,128)S(1)}, u32[]{:S(2)}, u32[]{:S(2)}) %collective-permute-start.7) | collective-permute-done | bytes 1622048 | tf_op jit(solution)/shard_map/ppermute | solution.py:446
  108.3 2.9 copy-done
  111.3 2.0 copy-done.3
  113.3 61.0 %shard_map.368 = (f32[144,11664]{1,0:T(8,128)}, f32[288,128]{1,0:T(8,128)S(1)}) custom-call(s32[517]{0:T(1024)S(1)} %dynamic-slice_reduce_fusion.1.tab, f32[144,11664]{1,0:T(8,128)S(1)} %bitcast.53, f32[288,3136]{1,0:T(8,128)S(1)} %bitcast.57, f32[288,128]{1,0:T(8,128)S(1)} %pad.18.w_ref, f32[11,288,128]{2,1,0:T(8,128)S(1)} %collective-permute-done.7.refs_0_, ...), custom_call_target="tpu_custom_call" | custom-call | flops 32514048 | bytes 21620736 | tf_op jit(solution)/shard_map/pallas_call | solution.py:320
  175.4 1.3 collective-permute-start.13
  176.7 1.8 multiply_reduce_fusion
  178.9 2.5 collective-permute-done.13
  181.5 1.4 collective-permute-start.14
  185.0 7.0 %collective-permute-done.15 = f32[16,384]{0,1:T(8,128)S(1)} collective-permute-done((f32[16,384]{0,1:T(8,128)S(1)}, f32[16,384]{0,1:T(8,128)S(1)}, u32[]{:S(2)}, u32[]{:S(2)}) %collective-permute-start.15) | collective-permute-done | bytes 24608 | tf_op jit(solution)/shard_map/ppermute | solution.py:347
  193.1 5.0 %collective-permute-done.16 = f32[16,384]{0,1:T(8,128)S(1)} collective-permute-done((f32[16,384]{0,1:T(8,128)S(1)}, f32[16,384]{0,1:T(8,128)S(1)}, u32[]{:S(2)}, u32[]{:S(2)}) %collective-permute-start.16) | collective-permute-done | bytes 24608 | tf_op jit(solution)/shard_map/ppermute | solution.py:347
  198.9 1.1 collective-permute-start.17
  203.6 2.9 copy-done.1
  206.5 12.6 %shard_map.365 = (f32[11,288,128]{2,1,0:T(8,128)}, f32[8,288,128]{2,1,0:T(8,128)}, f32[6,288,128]{2,1,0:T(8,128)}, f32[4,288,128]{2,1,0:T(8,128)}) custom-call(s32[517]{0:T(1024)S(1)} %dynamic-slice_reduce_fusion.1.tab, f32[144,11664]{1,0:T(8,128)S(1)} %bitcast.54, f32[288,128]{1,0:T(8,128)S(1)} %pad.18.w_ref), custom_call_target="tpu_custom_call" | custom-call | flops 16257024 | bytes 11142144 | tf_op jit(solution)/shard_map/pallas_call | solution.py:320
  219.1 1.3 collective-permute-start.6
  220.3 1.6 collective-permute-start.5
  221.9 3.8 %collective-permute-start.4 = (f32[8,288,128]{2,1,0:T(8,128)}, f32[8,288,128]{2,1,0:T(8,128)S(1)}, u32[]{:S(2)}, u32[]{:S(2)}) collective-permute-start(f32[8,288,128]{2,1,0:T(8,128)} %get-tuple-element.56), channel_id=1, source_target_pairs={{4,3},{3,4},{2,1},{1,2},{6,5},{5,6},{12,11},{11,12},{10,9},{9,10},... | collective-permute-start | bytes 3538952 | tf_op jit(solution)/shard_map/ppermute | solution.py:486
  225.8 4.7 %collective-permute-start.3 = (f32[11,288,128]{2,1,0:T(8,128)}, f32[11,288,128]{2,1,0:T(8,128)S(1)}, u32[]{:S(2)}, u32[]{:S(2)}) collective-permute-start(f32[11,288,128]{2,1,0:T(8,128)} %get-tuple-element.55), channel_id=1, source_target_pairs={{2,3},{5,4},{0,1},{7,6},{10,11},{13,12},{8,9},{15,14},{18,19},{21,... | collective-permute-start | bytes 4866056 | tf_op jit(solution)/shard_map/ppermute | solution.py:486
  230.6 9.9 %shard_map.364.own_ref = f32[25,288,128]{2,1,0:T(8,128)S(1)} custom-call(s32[517]{0:T(1024)S(1)} %dynamic-slice_reduce_fusion.1.tab, f32[144,11664]{1,0:T(8,128)S(1)} %bitcast.55, f32[288,128]{1,0:T(8,128)S(1)} %pad.18.w_ref), custom_call_target="tpu_custom_call" | custom-call | flops 16257024 | bytes 10552320 | tf_op jit(solution)/shard_map/pallas_call | solution.py:320
  240.5 1.8 copy-done.4
  242.4 1.1 add.177
  244.5 1.2 multiply_reduce_fusion.7
  245.7 1.4 multiply_reduce_fusion.3
  249.8 1.4 multiply_add_fusion.4
  251.2 1.2 multiply_add_fusion.7
  252.5 1.3 fusion.19
  255.2 1.4 copy.73
  256.6 1.3 dynamic_slice.43
  257.9 1.3 dynamic_slice.42
  259.1 1.4 copy.71
  260.5 1.4 copy.70
  261.9 1.4 copy.72
  263.9 1.2 multiply_add_fusion.6
  265.1 1.4 multiply_add_fusion.1
  266.6 21.1 %collective-permute-done.3.refs_0_ = f32[11,288,128]{2,1,0:T(8,128)S(1)} collective-permute-done((f32[11,288,128]{2,1,0:T(8,128)}, f32[11,288,128]{2,1,0:T(8,128)S(1)}, u32[]{:S(2)}, u32[]{:S(2)}) %collective-permute-start.3) | collective-permute-done | bytes 1622048 | tf_op jit(solution)/shard_map/ppermute | solution.py:486
  287.7 2.0 copy-done.5
  289.7 12.5 %shard_map.366 = f32[288,3136]{1,0:T(8,128)} custom-call(s32[517]{0:T(1024)S(1)} %dynamic-slice_reduce_fusion.1.tab, f32[25,288,128]{2,1,0:T(8,128)S(1)} %copy-done.5, f32[11,288,128]{2,1,0:T(8,128)S(1)} %collective-permute-done.3.refs_0_, f32[8,288,128]{2,1,0:T(8,128)S(1)} %collective-permute-done.4.refs_1_, f32[6,288,128]{2,1,0:T(8,128)} %collective-permute-done.5.refs_2_, ...), custom_call_target="tpu_custom_call" | custom-call | flops 1000 | bytes 11575296 | tf_op jit(solution)/shard_map/pallas_call | solution.py:320
  (116 shorter events, 23.3 us)
Async XLA Ops:
  9.8 3.0 %collective-permute-start = (f32[1,104,128]{2,0,1:T(1,128)S(1)}, f32[1,104,128]{2,0,1:T(1,128)S(1)}, u32[]{:S(2)}, u32[]{:S(2)}) collective-permute-start(f32[1,104,128]{2,0,1:T(1,128)S(1)} %constant_dynamic-slice_fusion.4), channel_id=1, source_target_pairs={{0,1},{1,0},{2,3},{3,2},{4,5},{5,4},{6,7},{7,6},{8,9},{9,8},{10,11... | collective-permute-start | bytes 159752 | tf_op jit(solution)/shard_map/ppermute | solution.py:347
  15.7 3.6 %collective-permute-start.1 = (f32[2,104,128]{2,0,1:T(2,128)S(1)}, f32[2,104,128]{2,0,1:T(2,128)S(1)}, u32[]{:S(2)}, u32[]{:S(2)}) collective-permute-start(f32[2,104,128]{2,0,1:T(2,128)S(1)} %constant_dynamic-slice_fusion.3), channel_id=1, source_target_pairs={{0,2},{1,3},{2,0},{3,1},{4,6},{5,7},{6,4},{7,5},{8,10},{9,11},{10,... | collective-permute-start | bytes 319496 | tf_op jit(solution)/shard_map/ppermute | solution.py:347
  23.7 14.2 %copy-start.7 = (f32[8,104,128]{2,0,1:T(8,128)}, f32[8,104,128]{2,0,1:T(8,128)S(1)}, u32[]{:S(2)}) copy-start(f32[8,104,128]{2,0,1:T(8,128)S(1)} %dynamic_update_slice.15) | copy-start | bytes 1277956
  24.5 22.8 %collective-permute-start.2 = (f32[4,104,128]{2,0,1:T(4,128)}, f32[4,104,128]{2,0,1:T(4,128)}, u32[]{:S(2)}, u32[]{:S(2)}) collective-permute-start(f32[4,104,128]{2,0,1:T(4,128)} %constant_dynamic-slice_fusion.2), channel_id=1, source_target_pairs={{0,4},{1,5},{2,6},{3,7},{4,0},{5,1},{6,2},{7,3},{8,12},{9,13},{10,... | collective-permute-start | bytes 638984 | tf_op jit(solution)/shard_map/ppermute | solution.py:347
  27.6 2.0 copy-start.2
  29.6 16.3 %copy-start.21 = (f32[36,9]{0,1:T(8,128)S(1)}, f32[36,9]{0,1:T(8,128)}, u32[]{:S(2)}) copy-start(f32[36,9]{0,1:T(8,128)} %param.27) | copy-start | bytes 3892
  29.6 17.0 %copy-start.25 = (f32[36,9]{0,1:T(8,128)S(1)}, f32[36,9]{0,1:T(8,128)}, u32[]{:S(2)}) copy-start(f32[36,9]{0,1:T(8,128)} %param.39) | copy-start | bytes 3892
  37.9 43.4 %collective-permute-start.10 = (f32[4,288,128]{2,1,0:T(8,128)}, f32[4,288,128]{2,1,0:T(8,128)S(1)}, u32[]{:S(2)}, u32[]{:S(2)}) collective-permute-start(f32[4,288,128]{2,1,0:T(8,128)} %get-tuple-element.62), channel_id=1, source_target_pairs={{2,3},{5,4},{10,11},{13,12},{18,19},{21,20},{26,27},{29,28}} | collective-permute-start | bytes 1769480 | tf_op jit(solution)/shard_map/ppermute | solution.py:446
  41.0 40.2 %collective-permute-start.9 = (f32[6,288,128]{2,1,0:T(8,128)}, f32[6,288,128]{2,1,0:T(8,128)}, u32[]{:S(2)}, u32[]{:S(2)}) collective-permute-start(f32[6,288,128]{2,1,0:T(8,128)} %get-tuple-element.61), channel_id=1, source_target_pairs={{0,1},{7,6},{8,9},{15,14},{16,17},{23,22},{24,25},{31,30}} | collective-permute-start | bytes 2654216 | tf_op jit(solution)/shard_map/ppermute | solution.py:446
  42.7 38.6 %collective-permute-start.8 = (f32[8,288,128]{2,1,0:T(8,128)}, f32[8,288,128]{2,1,0:T(8,128)S(1)}, u32[]{:S(2)}, u32[]{:S(2)}) collective-permute-start(f32[8,288,128]{2,1,0:T(8,128)} %get-tuple-element.60), channel_id=1, source_target_pairs={{3,4},{4,3},{1,2},{2,1},{5,6},{6,5},{11,12},{12,11},{9,10},{10,9},... | collective-permute-start | bytes 3538952 | tf_op jit(solution)/shard_map/ppermute | solution.py:446
  44.6 63.7 %collective-permute-start.7 = (f32[11,288,128]{2,1,0:T(8,128)}, f32[11,288,128]{2,1,0:T(8,128)S(1)}, u32[]{:S(2)}, u32[]{:S(2)}) collective-permute-start(f32[11,288,128]{2,1,0:T(8,128)} %get-tuple-element.59), channel_id=1, source_target_pairs={{3,2},{4,5},{1,0},{6,7},{11,10},{12,13},{9,8},{14,15},{19,18},{20,... | collective-permute-start | bytes 4866056 | tf_op jit(solution)/shard_map/ppermute | solution.py:446
  58.8 3.2 %collective-permute-start.11 = (f32[145,36]{0,1:T(8,128)S(1)}, f32[145,36]{0,1:T(8,128)S(1)}, u32[]{:S(2)}, u32[]{:S(2)}) collective-permute-start(f32[145,36]{0,1:T(8,128)S(1)} %pad_maximum_fusion), channel_id=1, source_target_pairs={{0,16},{8,24},{16,0},{24,8},{1,17},{9,25},{17,1},{25,9},{2,18},{10... | collective-permute-start | bytes 62648 | tf_op jit(solution)/shard_map/ppermute | solution.py:347
  62.7 11.9 %collective-permute-start.12 = (f32[145,36]{0,1:T(8,128)}, f32[145,36]{0,1:T(8,128)}, u32[]{:S(2)}, u32[]{:S(2)}) collective-permute-start(f32[145,36]{0,1:T(8,128)} %fusion.25), channel_id=1, source_target_pairs={{0,8},{8,0},{16,24},{24,16},{1,9},{9,1},{17,25},{25,17},{2,10},{10... | collective-permute-start | bytes 62648 | tf_op jit(solution)/shard_map/ppermute | solution.py:347
  108.3 2.9 copy-start
  111.3 2.0 copy-start.3
  174.4 4.2 %copy-start.6 = (f32[8,144,36]{2,1,0:T(8,128)S(1)}, f32[8,144,36]{2,1,0:T(8,128)}, u32[]{:S(2)}) copy-start(f32[8,144,36]{2,1,0:T(8,128)} %reshape.165) | copy-start | bytes 497668
  174.4 8.5 %copy-start.17 = (f32[1,16,288]{2,1,0:T(8,128)S(1)}, f32[1,16,288]{2,1,0:T(8,128)}, u32[]{:S(2)}) copy-start(f32[1,16,288]{2,1,0:T(8,128)} %param.44) | copy-start | bytes 55300
  174.4 9.4 %copy-start.22 = (f32[8,36]{1,0:T(8,128)S(1)}, f32[8,36]{1,0:T(8,128)}, u32[]{:S(2)}) copy-start(f32[8,36]{1,0:T(8,128)} %get-tuple-element.154) | copy-start | bytes 3460
  175.4 6.0 %collective-permute-start.13 = (f32[16,384]{0,1:T(8,128)S(1)}, f32[16,384]{0,1:T(8,128)S(1)}, u32[]{:S(2)}, u32[]{:S(2)}) collective-permute-start(f32[16,384]{0,1:T(8,128)S(1)} %scatter.9), channel_id=1, source_target_pairs={{0,16},{8,24},{16,0},{24,8},{1,17},{9,25},{17,1},{25,9},{2,18},{10... | collective-permute-start | bytes 73736 | tf_op jit(solution)/shard_map/ppermute | solution.py:347
  178.5 5.6 %copy-start.19 = (f32[1,16,144]{2,1,0:T(8,128)S(1)}, f32[1,16,144]{2,1,0:T(8,128)}, u32[]{:S(2)}) copy-start(f32[1,16,144]{2,1,0:T(8,128)} %param.26) | copy-start | bytes 27652
  178.9 13.3 %copy-start.8 = (f32[288,10]{1,0:T(8,128)S(1)}, f32[288,10]{1,0:T(8,128)}, u32[]{:S(2)}) copy-start(f32[288,10]{1,0:T(8,128)} %reshape_reshape.15) | copy-start | bytes 34564
  178.9 14.1 %copy-start.20 = (f32[8,360]{1,0:T(8,128)S(1)}, f32[8,360]{1,0:T(8,128)}, u32[]{:S(2)}) copy-start(f32[8,360]{1,0:T(8,128)} %get-tuple-element.155) | copy-start | bytes 34564
  181.5 2.5 collective-permute-start.14
  184.0 8.1 %collective-permute-start.15 = (f32[16,384]{0,1:T(8,128)S(1)}, f32[16,384]{0,1:T(8,128)S(1)}, u32[]{:S(2)}, u32[]{:S(2)}) collective-permute-start(f32[16,384]{0,1:T(8,128)S(1)} %add.174), channel_id=1, source_target_pairs={{0,4},{1,5},{2,6},{3,7},{4,0},{5,1},{6,2},{7,3},{8,12},{9,13},{10,... | collective-permute-start | bytes 73736 | tf_op jit(solution)/shard_map/ppermute | solution.py:347
  192.1 6.1 %collective-permute-start.16 = (f32[16,384]{0,1:T(8,128)S(1)}, f32[16,384]{0,1:T(8,128)S(1)}, u32[]{:S(2)}, u32[]{:S(2)}) collective-permute-start(f32[16,384]{0,1:T(8,128)S(1)} %add.175), channel_id=1, source_target_pairs={{0,2},{1,3},{2,0},{3,1},{4,6},{5,7},{6,4},{7,5},{8,10},{9,11},{10,... | collective-permute-start | bytes 73736 | tf_op jit(solution)/shard_map/ppermute | solution.py:347
  193.1 26.0 %copy-start.10 = (f32[288,10]{1,0:T(8,128)}, f32[288,10]{1,0:T(8,128)S(1)}, u32[]{:S(2)}) copy-start(f32[288,10]{1,0:T(8,128)S(1)} %reshape_reshape.16) | copy-start | bytes 34564
  198.9 43.5 %collective-permute-start.17 = (f32[16,384]{0,1:T(8,128)}, f32[16,384]{0,1:T(8,128)}, u32[]{:S(2)}, u32[]{:S(2)}) collective-permute-start(f32[16,384]{0,1:T(8,128)} %add.176), channel_id=1, source_target_pairs={{0,1},{1,0},{2,3},{3,2},{4,5},{5,4},{6,7},{7,6},{8,9},{9,8},{10,11... | collective-permute-start | bytes 73736 | tf_op jit(solution)/shard_map/ppermute | solution.py:347
  203.6 2.9 copy-start.1
  219.1 47.5 %collective-permute-start.6 = (f32[4,288,128]{2,1,0:T(8,128)}, f32[4,288,128]{2,1,0:T(8,128)S(1)}, u32[]{:S(2)}, u32[]{:S(2)}) collective-permute-start(f32[4,288,128]{2,1,0:T(8,128)} %get-tuple-element.58), channel_id=1, source_target_pairs={{3,2},{4,5},{11,10},{12,13},{19,18},{20,21},{27,26},{28,29}} | collective-permute-start | bytes 1769480 | tf_op jit(solution)/shard_map/ppermute | solution.py:486
  220.3 46.2 %collective-permute-start.5 = (f32[6,288,128]{2,1,0:T(8,128)}, f32[6,288,128]{2,1,0:T(8,128)}, u32[]{:S(2)}, u32[]{:S(2)}) collective-permute-start(f32[6,288,128]{2,1,0:T(8,128)} %get-tuple-element.57), channel_id=1, source_target_pairs={{1,0},{6,7},{9,8},{14,15},{17,16},{22,23},{25,24},{30,31}} | collective-permute-start | bytes 2654216 | tf_op jit(solution)/shard_map/ppermute | solution.py:486
  221.9 44.6 %collective-permute-start.4 = (f32[8,288,128]{2,1,0:T(8,128)}, f32[8,288,128]{2,1,0:T(8,128)S(1)}, u32[]{:S(2)}, u32[]{:S(2)}) collective-permute-start(f32[8,288,128]{2,1,0:T(8,128)} %get-tuple-element.56), channel_id=1, source_target_pairs={{4,3},{3,4},{2,1},{1,2},{6,5},{5,6},{12,11},{11,12},{10,9},{9,10},... | collective-permute-start | bytes 3538952 | tf_op jit(solution)/shard_map/ppermute | solution.py:486
  225.8 18.4 %copy-start.12 = (f32[288,10]{1,0:T(8,128)S(1)}, f32[288,10]{1,0:T(8,128)}, u32[]{:S(2)}) copy-start(f32[288,10]{1,0:T(8,128)} %reshape_reshape.19) | copy-start | bytes 34564
  225.8 18.7 %copy-start.23 = (f32[288]{0:T(512)S(1)}, f32[288]{0:T(512)}, u32[]{:S(2)}) copy-start(f32[288]{0:T(512)} %get-tuple-element.129) | copy-start | bytes 3460
  225.8 18.7 %copy-start.24 = (f32[288]{0:T(512)S(1)}, f32[288]{0:T(512)}, u32[]{:S(2)}) copy-start(f32[288]{0:T(512)} %fusion.2) | copy-start | bytes 3460
  225.8 19.9 %copy-start.9 = (f32[288,10]{1,0:T(8,128)S(1)}, f32[288,10]{1,0:T(8,128)}, u32[]{:S(2)}) copy-start(f32[288,10]{1,0:T(8,128)} %reshape_reshape.15) | copy-start | bytes 34564
  225.8 19.9 %copy-start.11 = (f32[288,10]{1,0:T(8,128)S(1)}, f32[288,10]{1,0:T(8,128)}, u32[]{:S(2)}) copy-start(f32[288,10]{1,0:T(8,128)} %copy-done.10) | copy-start | bytes 34564
  225.8 61.8 %collective-permute-start.3 = (f32[11,288,128]{2,1,0:T(8,128)}, f32[11,288,128]{2,1,0:T(8,128)S(1)}, u32[]{:S(2)}, u32[]{:S(2)}) collective-permute-start(f32[11,288,128]{2,1,0:T(8,128)} %get-tuple-element.55), channel_id=1, source_target_pairs={{2,3},{5,4},{0,1},{7,6},{10,11},{13,12},{8,9},{15,14},{18,19},{21,... | collective-permute-start | bytes 4866056 | tf_op jit(solution)/shard_map/ppermute | solution.py:486
  240.5 1.8 copy-start.4
  242.3 7.5 %copy-start.18 = (f32[36,9]{1,0:T(8,128)S(1)}, f32[36,9]{1,0:T(8,128)}, u32[]{:S(2)}) copy-start(f32[36,9]{1,0:T(8,128)} %copy.68) | copy-start | bytes 3892
  242.3 8.9 %copy-start.27 = (f32[36]{0:T(128)S(1)}, f32[36]{0:T(128)}, u32[]{:S(2)}) copy-start(f32[36]{0:T(128)} %param.28) | copy-start | bytes 436
  242.3 21.6 %copy-start.26 = (f32[36]{0:T(128)S(1)}, f32[36]{0:T(128)}, u32[]{:S(2)}) copy-start(f32[36]{0:T(128)} %param.30) | copy-start | bytes 436
  242.3 21.6 %copy-start.28 = (f32[36]{0:T(128)S(1)}, f32[36]{0:T(128)}, u32[]{:S(2)}) copy-start(f32[36]{0:T(128)} %get-tuple-element.150) | copy-start | bytes 436
  242.4 22.7 %copy-start.14 = (f32[144,36]{0,1:T(8,128)S(1)}, f32[144,36]{0,1:T(8,128)}, u32[]{:S(2)}) copy-start(f32[144,36]{0,1:T(8,128)} %param.29) | copy-start | bytes 62212
  242.4 22.7 %copy-start.15 = (f32[144,36]{0,1:T(8,128)S(1)}, f32[144,36]{0,1:T(8,128)}, u32[]{:S(2)}) copy-start(f32[144,36]{0,1:T(8,128)} %get-tuple-element.147) | copy-start | bytes 62212
  242.4 22.7 %copy-start.16 = (f32[144,36]{0,1:T(8,128)S(1)}, f32[144,36]{0,1:T(8,128)}, u32[]{:S(2)}) copy-start(f32[144,36]{0,1:T(8,128)} %get-tuple-element.148) | copy-start | bytes 62212
  243.5 0.7 copy-start.13
  287.7 2.0 copy-start.5

commit v2 on v0

v2 whole, which is shorter than its diff:
```python
import functools

import jax
import jax.numpy as jnp
import numpy as np
from jax import lax
from jax.experimental import pallas as pl
from jax.experimental.pallas import tpu as pltpu
from jax.sharding import PartitionSpec as P

GRID = 27
TAPS = 9
OUTG = 14
LANES = 128
SUBL = 8
UNIT = 16

beta_one = 0.9
beta_two = 0.999
fix_first = 1.0 - 0.9**10
fix_second = 1.0 - 0.999**10
small_eps = 1e-06
learn_rate = 0.5
keep_rate = 0.9
highest = lax.Precision.HIGHEST


def grouped(messages, spare):
    ops = []
    for (src, dst), tiles in sorted(messages, key=lambda kv: (-len(kv[1]), kv[0])):
        for op in ops:
            if op["size"] - len(tiles) <= spare and all(
                src != s and dst != d for s, d in op["pairs"]
            ):
                break
        else:
            op = {"size": len(tiles), "pairs": [], "tiles": []}
            ops.append(op)
        op["pairs"].append((src, dst))
        op["tiles"].append(tiles)
    for op in ops:
        op["near"] = all(src ^ dst == 1 for src, dst in op["pairs"])
    return ops


def make_plan(groups, images, n_in, n_out):
    tiles_img = images // LANES
    n_tiles = OUTG * OUTG * tiles_img
    tap_tile = np.full((n_tiles, TAPS), -1, np.int64)
    for i in range(OUTG):
        for j in range(OUTG):
            for it in range(tiles_img):
                for a in range(3):
                    for e in range(3):
                        r, s = 2 * i + a - 1, 2 * j + e - 1
                        if 0 <= r < GRID and 0 <= s < GRID:
                            tap_tile[(i * OUTG + j) * tiles_img + it, 3 * a + e] = (
                                r * GRID + s
                            ) * tiles_img + it
    step = int(np.gcd(np.gcd(n_in, n_out), LANES))
    wanted = {}
    for lane in range(0, LANES, step):
        p_owner = (np.arange(n_tiles) * LANES + lane) // n_out
        t_owner = (tap_tile * LANES + lane) // n_in
        for p in range(n_tiles):
            k = int(p_owner[p])
            for t in range(TAPS):
                if tap_tile[p, t] >= 0 and t_owner[p, t] != k:
                    wanted.setdefault((k, int(t_owner[p, t])), set()).add(p)
    wanted = {pair: sorted(tiles) for pair, tiles in wanted.items()}
    near = {pair: tiles for pair, tiles in wanted.items() if pair[0] ^ pair[1] == 1}
    even = max([min(len(t), len(near.get(p[::-1], []))) for p, t in near.items()], default=0)
    ops = grouped([(p, t[:even]) for p, t in near.items() if even], even)
    ops += grouped([(p, t[even:]) for p, t in near.items() if len(t) > even], 2)
    ops += grouped([(p, t) for p, t in wanted.items() if p not in near], 2)
    back_ops = grouped([((d, s), t) for (s, d), t in wanted.items()], 2)
    longest = max(op["size"] for op in back_ops)
    for op in back_ops:
        op["early"] = op["near"] and 4 * op["size"] > 3 * longest
    in_base = np.arange(groups) * n_in // LANES
    in_shift = np.arange(groups) * n_in % LANES
    out_base = np.arange(groups) * n_out // LANES
    out_shift = np.arange(groups) * n_out % LANES
    in_tiles = int(max(-(-(in_shift + n_in) // LANES)))
    out_tiles = int(max(-(-(out_shift + n_out) // LANES)))
    sizes = [op["size"] for op in ops]
    halo = sum(sizes)
    back_sizes = [op["size"] for op in back_ops]
    back_halo = sum(back_sizes)
    owned = [
        range(int(out_base[k]), int(out_base[k]) - (-(int(out_shift[k]) + n_out) // LANES))
        for k in range(groups)
    ]
    none = out_tiles + halo
    own_slot = np.full((groups, halo), out_tiles, np.int64)
    got = [[] for _ in range(groups)]
    start = 0
    for op in ops:
        for (src, dst), tiles in zip(op["pairs"], op["tiles"]):
            for j, p in enumerate(tiles):
                own_slot[src, start + j] = p - out_base[src]
                got[dst].append((p, start + j))
        start += op["size"]
    most = max(len(v) for v in got)

    def tap_rows(device, p):
        local = tap_tile[p] - in_base[device]
        first, last = device * n_in, (device + 1) * n_in
        held = (
            (tap_tile[p] >= 0)
            & (tap_tile[p] * LANES < last)
            & ((tap_tile[p] + 1) * LANES > first)
        )
        return np.where(held, local, in_tiles)

    own_taps = np.full((groups, out_tiles, TAPS), in_tiles, np.int64)
    got_taps = np.full((groups, most, 1 + TAPS), in_tiles, np.int64)
    got_taps[:, :, 0] = none
    from_got = np.full((groups, back_halo), most, np.int64)
    adds = [[[] for _ in range(out_tiles)] for _ in range(groups)]
    merges, slot_of = [], []
    for k in range(groups):
        for j, p in enumerate(owned[k]):
            own_taps[k, j] = tap_rows(k, p)
        slot_of.append({p: j for j, p in enumerate(owned[k])})
        merges.append([])
        for n, (p, place) in enumerate(got[k]):
            got_taps[k, n, 0] = out_tiles + place
            got_taps[k, n, 1:] = tap_rows(k, p)
            if p in slot_of[k]:
                merges[k].append([slot_of[k][p], out_tiles + place])
            else:
                slot_of[k][p] = out_tiles + place
    start = 0
    for op in back_ops:
        for (src, dst), tiles in zip(op["pairs"], op["tiles"]):
            names = [p for p, _ in got[src]]
            for j, p in enumerate(tiles):
                from_got[src, start + j] = names.index(p)
                adds[dst][p - out_base[dst]].append(start + j)
        start += op["size"]
    n_merges = max(len(v) for v in merges)
    merges = np.array([v + [[none, none]] * (n_merges - len(v)) for v in merges], np.int64)
    n_adds = max(len(v) for per_dev in adds for v in per_dev)
    adds = np.array([[v + [back_halo] * (n_adds - len(v)) for v in per_dev] for per_dev in adds])
    kinds = [
        [(a, e) for a in ((1,), (0, 2))[row_odd] for e in ((1,), (0, 2))[col_odd]]
        for row_odd in range(2)
        for col_odd in range(2)
    ]
    lists = [[[] for _ in range(groups)] for _ in kinds]
    for k in range(groups):
        count = -(-(int(in_shift[k]) + n_in) // LANES)
        for t in range(count):
            position, it = divmod(int(in_base[k]) + t, tiles_img)
            r, s = divmod(position, GRID)
            kind = 2 * (r % 2) + s % 2
            entry = [t]
            for a, e in kinds[kind]:
                i, j = (r + 1 - a) // 2, (s + 1 - e) // 2
                entry.append(slot_of[k].get((i * OUTG + j) * tiles_img + it, none))
            lists[kind][k].append(entry)
    reach_tables, kind_sizes = [], []
    for kind, per_device_lists in enumerate(lists):
        width = 1 + len(kinds[kind])
        size = max(len(v) for v in per_device_lists)
        kind_sizes.append(size)
        filler = [in_tiles] + [none] * (width - 1)
        reach_tables.append(
            np.array([v + [filler] * (size - len(v)) for v in per_device_lists]).reshape(groups, -1)
        )
    parts = [
        ("shifts", np.stack([in_shift, out_shift], axis=1)),
        ("own_slot", own_slot),
        ("own_taps", own_taps.reshape(groups, -1)),
        ("got_taps", got_taps.reshape(groups, -1)),
        ("from_got", from_got),
        ("merges", merges.reshape(groups, -1)),
        ("adds", adds.reshape(groups, -1)),
        *((f"kind{q}", v) for q, v in enumerate(reach_tables)),
    ]
    at, total = {}, 0
    for name, v in parts:
        at[name] = total
        total += v.shape[1]
    return {
        "ops": ops,
        "sizes": sizes,
        "halo": halo,
        "back_ops": back_ops,
        "back_sizes": back_sizes,
        "back_halo": back_halo,
        "in_tiles": in_tiles,
        "out_tiles": out_tiles,
        "most": most,
        "n_merges": n_merges,
        "n_adds": n_adds,
        "n_in": n_in,
        "n_out": n_out,
        "kinds": [[3 * a + e for a, e in kind] for kind in kinds],
        "kind_sizes": kind_sizes,
        "at": at,
        "table": np.concatenate([v for _, v in parts], axis=1).astype(np.int32),
    }


def lane_ids():
    return lax.broadcasted_iota(jnp.int32, (UNIT, LANES), 1)


def align_into(load, store, n_local, tiles, shift):
    lane = lane_ids()
    zero = jnp.zeros((UNIT, LANES), jnp.float32)
    local_tiles = -(-n_local // LANES)
    before = zero
    for t in range(tiles):
        if t < local_tiles:
            now = load(t)
            if (t + 1) * LANES > n_local:
                now = jnp.where(lane < n_local - t * LANES, now, 0.0)
            now = pltpu.roll(now, shift, 1)
        else:
            now = zero
        store(t, jnp.where(lane < shift, before, now))
        before = now
    store(tiles, zero)


def unalign_from(load, store, n_local, tiles, shift):
    lane = lane_ids()
    local_tiles = -(-n_local // LANES)
    back = lax.rem(LANES - shift, LANES)
    now = pltpu.roll(load(0), back, 1)
    for t in range(local_tiles):
        later = pltpu.roll(load(t + 1), back, 1) if t + 1 < tiles else now
        store(t, jnp.where(lane < LANES - shift, now, later))
        now = later


def tile_lanes(t):
    return slice(t * LANES, (t + 1) * LANES)


def rows_at(unit, part=0, parts=1):
    return pl.ds(pl.multiple_of((unit * parts + part) * UNIT, UNIT), UNIT)


def both_at(unit):
    return pl.ds(pl.multiple_of(unit * 2 * UNIT, UNIT), 2 * UNIT)


def of_half(half, unit=0):
    return pl.ds(unit * 2 * UNIT + half, UNIT, stride=2)


def align_cot(cot_ref, unit, held, plan, shift):
    for part in range(2):
        align_into(
            lambda t: cot_ref[rows_at(unit, part, 2), tile_lanes(t)],
            lambda t, v: held.__setitem__((t, slice(part * UNIT, (part + 1) * UNIT)), v),
            plan["n_out"],
            plan["out_tiles"],
            shift,
        )


def tap_weights(w_ref, unit, half, lanes):
    rows = w_ref[of_half(half, unit), :]
    return [jnp.broadcast_to(rows[:, t : t + 1], (UNIT, LANES)) for t in lanes]


def in_turn(count, size, make, keep):
    for first in range(0, count, size):
        some = range(first, min(first + size, count))
        for j, v in [(j, make(j)) for j in some]:
            keep(j, v)


def over_units(ref, rows, body):
    lax.fori_loop(0, ref.shape[0] // rows, lambda u, c: (body(u), c)[1], 0)


def add_up(items):
    items = list(items)
    while len(items) > 1:
        items = [
            items[i] + items[i + 1] if i + 1 < len(items) else items[i]
            for i in range(0, len(items), 2)
        ]
    return items[0]


BIAS_LANE = 48
HEAD_BIAS_LANE = 72
HEAD_LANE = 96


def small_kernel(per_dev, cw, cb, fw, fb, sw, sb, hb, hw, ci, cc, out, square):
    square[...] = jnp.zeros_like(square)
    for part, (w, b) in enumerate(((cw, cb), (fw, fb), (sw, sb))):
        square[2 * SUBL * part : 2 * SUBL * part + TAPS, :per_dev] = w[...]
        square[BIAS_LANE + SUBL * part : BIAS_LANE + SUBL * part + 1, :per_dev] = b[...]
    square[HEAD_BIAS_LANE : HEAD_BIAS_LANE + 1, :per_dev] = hb[...]
    turned = square[...].T
    rows = hw.shape[0]
    lane = lax.broadcasted_iota(jnp.int32, (rows, LANES), 1)
    rest = pltpu.roll(jnp.where(lane < 2 * SUBL, hw[:, LANES:], 0.0), HEAD_LANE, 1)
    out[0:rows] = jnp.where(lane < HEAD_LANE, turned[0:rows], rest)
    out[rows : 2 * rows] = hw[:, :LANES]
    at, n = 2 * rows, ci.shape[0]
    out[at : at + n] = ci[:, :LANES]
    out[at + n : at + 2 * n] = cc[:, :LANES]
    out[at + 2 * n : at + 3 * n] = cc[:, LANES : 2 * LANES]
    lane = lax.broadcasted_iota(jnp.int32, (n, LANES), 1)
    left = jnp.where(lane < 2 * SUBL, ci[:, LANES:], 0.0)
    right = pltpu.roll(jnp.where(lane < 4 * SUBL, cc[:, 2 * LANES :], 0.0), 4 * SUBL, 1)
    out[at + 3 * n : at + 4 * n] = jnp.where(lane < 4 * SUBL, left, right)


def align_kernel(plan, tab, x_ref, cot_ref, after, x_out, cot_out, held):
    def body(unit):
        align_into(
            lambda t: x_ref[rows_at(unit), tile_lanes(t)],
            lambda t, v: x_out.__setitem__((t, rows_at(unit)), v),
            plan["n_in"],
            plan["in_tiles"],
            tab[0],
        )
        align_cot(cot_ref, unit, held, plan, tab[1])
        for j in range(plan["out_tiles"]):
            for half in range(2):
                cot_out[j, half, rows_at(unit)] = held[j, of_half(half)]

    over_units(x_ref, UNIT, body)


def pack_kernel(plan, tab, cot_ref, after, *refs):
    outs, held = refs[:-1], refs[-1]

    def body(unit):
        align_cot(cot_ref, unit, held, plan, tab[1])
        at = plan["at"]["own_slot"]
        for out, size in zip(outs, plan["sizes"]):
            in_turn(
                size,
                6,
                lambda j, at=at: [held[tab[at + j], of_half(half)] for half in range(2)],
                lambda j, v, out=out: keep_split(out, j, unit, v),
            )
            at += size

    over_units(cot_ref, 2 * UNIT, body)


def tap_sums(tab, at, held, weights):
    totals = [None, None]
    for t in range(TAPS):
        tile = held(tab[at + t])
        for half in range(2):
            term = tile * weights[half][t]
            totals[half] = term if t == 0 else totals[half] + term
    return totals


def keep_halves(ref, j, unit, values):
    for half, v in enumerate(values):
        ref[j, of_half(half, unit)] = v


def keep_split(ref, j, unit, values):
    for half, v in enumerate(values):
        ref[j, half, rows_at(unit)] = v


def partial_kernel(plan, tab, x_ref, w_ref, *refs):
    outs, done = refs[:-1], refs[-1]

    def body(unit):
        def held(slot):
            return x_ref[slot, rows_at(unit)]

        weights = [tap_weights(w_ref, unit, half, range(TAPS)) for half in range(2)]
        in_turn(
            plan["most"],
            4,
            lambda n: tap_sums(tab, plan["at"]["got_taps"] + (1 + TAPS) * n + 1, held, weights),
            lambda n, totals: keep_halves(done, n, 0, totals),
        )
        done[plan["most"]] = jnp.zeros(done.shape[1:], jnp.float32)
        at = plan["at"]["from_got"]
        for out, size in zip(outs, plan["back_sizes"]):
            in_turn(
                size,
                6,
                lambda j, at=at: done[tab[at + j]],
                lambda j, v, out=out: out.__setitem__((j, both_at(unit)), v),
            )
            at += size

    over_units(w_ref, 2 * UNIT, body)


def forward_kernel(plan, tab, x_ref, w_ref, after, out):
    def body(unit):
        def held(slot):
            return x_ref[slot, rows_at(unit)]

        weights = [
            tap_weights(w_ref, unit, half, [*range(TAPS), BIAS_LANE]) for half in range(2)
        ]
        in_turn(
            plan["out_tiles"],
            4,
            lambda j: tap_sums(tab, plan["at"]["own_taps"] + TAPS * j, held, weights),
            lambda j, totals: keep_halves(
                out, j, unit, [totals[half] + weights[half][TAPS] for half in range(2)]
            ),
        )

    over_units(w_ref, 2 * UNIT, body)


def take_cots(plan, unit, cot_ref, halos, cots):
    at = 0
    for ref, size in zip((cot_ref, *halos), (plan["out_tiles"], *plan["sizes"])):
        in_turn(
            size,
            5,
            lambda j, ref=ref: [ref[j, half, rows_at(unit)] for half in range(2)],
            lambda j, v, at=at: keep_split_all(cots, at + j, v),
        )
        at += size
    cots[at] = jnp.zeros(cots.shape[1:], jnp.float32)


def keep_split_all(ref, j, values):
    for half, v in enumerate(values):
        ref[j, half] = v


def merge_cots(plan, tab, cots):
    for n in range(plan["n_merges"]):
        at = plan["at"]["merges"] + 2 * n
        for half in range(2):
            cots[tab[at], half] = cots[tab[at], half] + cots[tab[at + 1], half]


def weights_kernel(plan, tab, x_ref, cot_ref, norms, after, *refs):
    halos = refs[: len(plan["sizes"])]
    sums_ref, cots, rows = refs[len(plan["sizes"]) :]
    step = pl.program_id(0)
    per = x_ref.shape[1] // UNIT
    zero = jnp.zeros((UNIT, LANES), jnp.float32)

    @pl.when(step == 0)
    def _():
        rows[...] = jnp.zeros_like(rows)

    def body(unit):
        take_cots(plan, unit, cot_ref, halos, cots)
        here = step * per + unit
        for half in range(2):
            bias = cots[0, half]
            for j in range(1, plan["out_tiles"]):
                bias = bias + cots[j, half]
            rows[TAPS, of_half(half, here), :] = bias
        merge_cots(plan, tab, cots)
        for q, (kind, size) in enumerate(zip(plan["kinds"], plan["kind_sizes"])):
            width = 1 + len(kind)
            total = [[zero] * len(kind) for _ in range(2)]
            for j in range(size):
                at = plan["at"][f"kind{q}"] + width * j
                tile = x_ref[tab[at], rows_at(unit)]
                for n in range(len(kind)):
                    slot = tab[at + 1 + n]
                    for half in range(2):
                        total[half][n] = total[half][n] + cots[slot, half] * tile
            for n, t in enumerate(kind):
                for half in range(2):
                    rows[t, of_half(half, here), :] = total[half][n]

    lax.fori_loop(0, per, lambda u, c: (body(u), c)[1], 0)

    @pl.when(step == pl.num_programs(0) - 1)
    def _():
        lane = lax.broadcasted_iota(jnp.int32, (LANES, LANES), 1)

        def block(b, carry):
            here = pl.ds(pl.multiple_of(b * LANES, LANES), LANES)
            total = jnp.zeros((LANES, LANES), jnp.float32)
            for t in range(TAPS + 1):
                one = jnp.sum(rows[t, here, :], axis=1, keepdims=True)
                total = jnp.where(lane == t, one, total)
            sums_ref[:, here] = total.T[: 2 * SUBL]
            return carry

        lax.fori_loop(0, rows.shape[1] // LANES, block, 0)
        n_lane = lax.broadcasted_iota(jnp.int32, (1, sums_ref.shape[1]), 1)
        extra = jnp.where(n_lane == 0, norms[0], jnp.where(n_lane == 1, norms[1], 0.0))
        sums_ref[TAPS + 1 : TAPS + 2, :] = extra


def patches_kernel(plan, tab, cot_ref, w_ref, after, *refs):
    halos = refs[: len(plan["sizes"])]
    grad_ref, cots, back = refs[len(plan["sizes"]) :]

    def body(unit):
        take_cots(plan, unit, cot_ref, halos, cots)
        merge_cots(plan, tab, cots)
        for q, (kind, size) in enumerate(zip(plan["kinds"], plan["kind_sizes"])):
            weights = [tap_weights(w_ref, unit, half, kind) for half in range(2)]
            width = 1 + len(kind)

            def one(j, q=q, kind=kind, weights=weights, width=width):
                at = plan["at"][f"kind{q}"] + width * j
                items = []
                for n in range(len(kind)):
                    slot = tab[at + 1 + n]
                    items += [cots[slot, half] * weights[half][n] for half in range(2)]
                return at, add_up(items)

            in_turn(size, 4, one, lambda j, v: back.__setitem__(tab[v[0]], v[1]))
        unalign_from(
            lambda t: back[t],
            lambda t, v: grad_ref.__setitem__((rows_at(unit), tile_lanes(t)), v),
            plan["n_in"],
            plan["in_tiles"],
            tab[0],
        )

    over_units(w_ref, 2 * UNIT, body)


def finish_kernel(plan, tab, own_ref, *refs):
    n_ops = len(plan["back_sizes"])
    halos = refs[:n_ops]
    out_ref, held, got = refs[n_ops:]
    tiles = plan["out_tiles"]

    def body(unit):
        at = 0
        for halo, size in zip(halos, plan["back_sizes"]):
            for j in range(size):
                got[at + j] = halo[j, both_at(unit)]
            at += size
        got[at] = jnp.zeros(got.shape[1:], jnp.float32)

        def whole_sum(j):
            total = own_ref[j, both_at(unit)]
            for n in range(plan["n_adds"]):
                total = total + got[tab[plan["at"]["adds"] + plan["n_adds"] * j + n]]
            return total

        in_turn(tiles, 5, whole_sum, held.__setitem__)
        for part in range(2):
            unalign_from(
                lambda t: held[t, part * UNIT : (part + 1) * UNIT],
                lambda t, v: out_ref.__setitem__((rows_at(unit, part, 2), tile_lanes(t)), v),
                plan["n_out"],
                tiles,
                tab[1],
            )

    over_units(out_ref, 2 * UNIT, body)


def spread_kernel(groups, per_dev, rounds, me, parts, ci, cc, after, wide_out, turned_out, class_out, class_grad, grad_out, norms_out, wide, head, cots, classes):
    rows = round_up(per_dev, SUBL)
    n = ci.shape[0]
    channels = groups * per_dev
    wide[...] = jnp.zeros_like(wide)
    head[...] = jnp.zeros_like(head)
    lane = lax.broadcasted_iota(jnp.int32, (n, LANES), 1)
    at = 2 * rows
    for dev in range(groups):
        apart = jnp.bitwise_xor(me[0], dev)
        part = 0
        for place, bit in enumerate(rounds):
            part = part + jnp.bitwise_and(lax.div(apart, bit), 1) * 2**place
        wide[dev * per_dev : (dev + 1) * per_dev, :] = parts[part, :per_dev]
        head[dev * per_dev : (dev + 1) * per_dev, :LANES] = parts[part, rows : rows + per_dev]
        here = slice(dev * n, (dev + 1) * n)
        classes[here, :LANES] = parts[part, at : at + n]
        cots[here, :LANES] = parts[part, at + n : at + 2 * n]
        cots[here, LANES : 2 * LANES] = parts[part, at + 2 * n : at + 3 * n]
        rest = parts[part, at + 3 * n : at + 4 * n]
        ones = jnp.where(lane == 2 * SUBL, 1.0, 0.0)
        classes[here, LANES:] = jnp.where(lane < 2 * SUBL, rest, ones)
        rest = pltpu.roll(rest, LANES - 4 * SUBL, 1)
        cots[here, 2 * LANES :] = jnp.where(lane < 4 * SUBL, rest, 0.0)
    table = wide[...]
    wide_out[...] = table[:channels]
    for b in range(table.shape[0] // LANES):
        turned_out[:, tile_lanes(b)] = table[tile_lanes(b)].T
    lane = lax.broadcasted_iota(jnp.int32, table.shape, 1)
    rest = jnp.where(lane < 2 * SUBL, pltpu.roll(table, LANES - HEAD_LANE, 1), 0.0)
    bias = pltpu.roll(table, LANES - HEAD_BIAS_LANE + 2 * SUBL, 1)
    main = head[:, :LANES]
    norm_b = jnp.sum(jnp.where(lane == 2 * SUBL, bias * bias, 0.0))
    norm_w = jnp.sum(main * main) + jnp.sum(rest * rest)
    head[:, LANES:] = jnp.where(lane == 2 * SUBL, bias, rest)
    conv = jnp.sum(jnp.where(lane < TAPS, table * table, 0.0))
    conv_b = jnp.sum(jnp.where(lane == BIAS_LANE, table * table, 0.0))
    n_lane = lax.broadcasted_iota(jnp.int32, (SUBL, LANES), 1)
    norms = jnp.zeros((SUBL, LANES), jnp.float32)
    for k, v in enumerate((conv, conv_b, norm_w, norm_b)):
        norms = jnp.where(n_lane == k, v, norms)
    norms_out[...] = norms
    lane = lax.broadcasted_iota(jnp.int32, (n, 2 * LANES), 1)
    edge = LANES + 2 * SUBL
    mine = jnp.where(lane < edge, ci[...], jnp.where(lane == edge, 1.0, 0.0))
    last = (((1,), (1,)), ((), ()))
    first = (((0,), (0,)), ((), ()))
    plain = (((1,), (0,)), ((), ()))

    def dot(a, b, dims):
        return lax.dot_general(
            a, b, dims, precision=highest, preferred_element_type=jnp.float32
        )

    class_out[...] = dot(mine, head[:channels, :], last)
    lane = lax.broadcasted_iota(jnp.int32, (n, 3 * LANES), 1)
    my_cot = jnp.where(lane < channels, cc[...], 0.0)
    class_grad[...] = dot(my_cot, head[...], plain)[:, : class_grad.shape[1]]
    pick = pick_rows(channels, per_dev, me[0], cots.shape[1])
    picked = dot(cots[...], pick, plain)
    grad_out[...] = dot(picked, classes[...], first)[:rows]


def pick_rows(channels, per_dev, me, padded):
    shape = (padded, LANES)
    channel = lax.broadcasted_iota(jnp.int32, shape, 0) - me * per_dev
    column = lax.broadcasted_iota(jnp.int32, shape, 1)
    return jnp.where((channel == column) & (column < per_dev), 1.0, 0.0)


def update_kernel(channels, per_dev, me, sums, table, norms, cw, cb, fw, fb, sw, sb, aw, ab, hw, hu, ha, hb, hub, hab,
                  fw_out, sw_out, w_out, a_out, hw_out, ha_out, rows_out):
    padded = sums.shape[1]
    real = lax.broadcasted_iota(jnp.int32, (1, padded), 1) < channels
    wide = moments(
        table[0:TAPS], sums[0:TAPS], table[16 : 16 + TAPS], table[32 : 32 + TAPS], 0.05
    )[2]
    wide_b = moments(table[48:49], sums[TAPS : TAPS + 1], table[56:57], table[64:65], 0.0)[2]
    lane = lax.broadcasted_iota(jnp.int32, (1, LANES), 1)
    update_sq = sums[TAPS + 1 : TAPS + 2, :LANES]
    update_sq = pltpu.roll(update_sq, 2, 1)
    update_sq = jnp.where(lane == 0, jnp.sum(jnp.where(real, wide * wide, 0.0)), update_sq)
    update_sq = jnp.where(lane == 1, jnp.sum(jnp.where(real, wide_b * wide_b, 0.0)), update_sq)
    ratios = jnp.sqrt(norms[0:1, :]) / jnp.sqrt(update_sq)
    rates = [
        learn_rate * jnp.sum(jnp.where(lane == k, ratios, 0.0), axis=1, keepdims=True)
        for k in range(4)
    ]
    mine = lax.dot_general(
        sums[...],
        pick_rows(channels, per_dev, me[0], padded),
        (((1,), (0,)), ((), ())),
        precision=highest,
        preferred_element_type=jnp.float32,
    )
    first, second, update = moments(cw[...], mine[0:TAPS, :per_dev], fw[...], sw[...], 0.05)
    fw_out[...] = first
    sw_out[...] = second
    w_new = cw[...] - rates[0] * update
    w_out[...] = w_new
    a_out[...] = keep_rate * aw[...] + (1.0 - keep_rate) * w_new
    first, second, update = moments(
        cb[...], mine[TAPS : TAPS + 1, :per_dev], fb[...], sb[...], 0.0
    )
    w_new = cb[...] - rates[1] * update
    rows_out[0:1, :per_dev] = first
    rows_out[1:2, :per_dev] = second
    rows_out[2:3, :per_dev] = w_new
    rows_out[3:4, :per_dev] = keep_rate * ab[...] + (1.0 - keep_rate) * w_new
    w_new = hb[...] - rates[3] * hub[...]
    rows_out[4:5, :per_dev] = w_new
    rows_out[5:6, :per_dev] = keep_rate * hab[...] + (1.0 - keep_rate) * w_new
    rows_out[6:7, :] = ratios
    rows_out[7:8, :] = jnp.zeros((1, LANES), jnp.float32)
    w_new = hw[...] - rates[2] * hu[...]
    hw_out[...] = w_new
    ha_out[...] = keep_rate * ha[...] + (1.0 - keep_rate) * w_new


def call(kernel, tables, operands, in_specs, outs, out_specs, scratch, steps, fills=False):
    moved = sum(4 * int(np.prod(a.shape)) for a in operands) + sum(
        4 * int(np.prod(o.shape)) for o in outs
    )
    return pl.pallas_call(
        kernel,
        grid_spec=pltpu.PrefetchScalarGridSpec(
            num_scalar_prefetch=len(tables),
            grid=(steps,),
            in_specs=in_specs,
            out_specs=out_specs,
            scratch_shapes=scratch,
        ),
        out_shape=outs,
        compiler_params=pltpu.CompilerParams(
            dimension_semantics=("arbitrary",), vmem_limit_bytes=60 * 1024 * 1024
        ),
        cost_estimate=pl.CostEstimate(
            flops=1, bytes_accessed=moved if fills else 1, transcendentals=0
        ),
    )(*tables, *operands)


def whole(*shape):
    return pl.BlockSpec(shape, lambda g, *tab: (0,) * len(shape))


def round_up(n, m):
    return -(-n // m) * m


def f32(*shape):
    return jax.ShapeDtypeStruct(shape, jnp.float32)


def swap(x, axis, bit):
    size = lax.axis_size(axis)
    return lax.ppermute(x, axis, [(k, k ^ bit) for k in range(size)])


def bits_of(axis):
    size = lax.axis_size(axis)
    assert size & (size - 1) == 0
    bits, b = [], 1
    while b < size:
        bits.append(b)
        b *= 2
    return bits


def sum_over(x, axis):
    for bit in reversed(bits_of(axis)):
        x = x + swap(x, axis, bit)
    return x


def tied(one, many):
    one, many = lax.optimization_barrier((one, list(many)))
    return one, many


def moments(weight, grad, first, second, decay):
    first_new = beta_one * first + (1.0 - beta_one) * grad
    second_new = beta_two * second + (1.0 - beta_two) * grad * grad
    update = (
        first_new / fix_first / (jnp.sqrt(second_new / fix_second) + small_eps) + decay * weight
    )
    return (first_new, second_new, update)


def per_device(
    patches,
    class_in,
    conv_weight,
    conv_bias,
    head_weight,
    head_bias,
    first_conv_w,
    first_conv_b,
    first_head_w,
    first_head_b,
    second_conv_w,
    second_conv_b,
    second_head_w,
    second_head_b,
    average_conv_w,
    average_conv_b,
    average_head_w,
    average_head_b,
    pooled_cot,
    class_cot,
):
    groups = lax.axis_size("chan")
    me = lax.axis_index("chan")
    my_id = me.astype(jnp.int32)[None]
    per_dev = conv_weight.shape[0]
    n_in, channels_in = patches.shape[1:]
    n_out, channels = pooled_cot.shape[1:]
    local_images = class_in.shape[1]
    images = local_images * groups
    plan = make_plan(groups, images, n_in, n_out)
    sizes, tiles, in_tiles = plan["sizes"], plan["out_tiles"], plan["in_tiles"]
    table = lax.dynamic_index_in_dim(jnp.asarray(plan["table"]), me, 0, keepdims=False)
    per = 3
    steps = channels_in // (UNIT * per)
    x = patches[0].T
    cot = pooled_cot[0].T
    in_lanes, out_lanes = round_up(n_in, LANES), round_up(n_out, LANES)
    rows, wide_rows = UNIT * per, 2 * UNIT * per
    x_spec = pl.BlockSpec((rows, in_lanes), lambda g, tab: (g, 0))
    cot_spec = pl.BlockSpec((wide_rows, out_lanes), lambda g, tab: (g, 0))
    halo_specs = [
        pl.BlockSpec((n, 2, rows, LANES), lambda g, tab: (0, 0, g, 0)) for n in sizes
    ]
    halo_outs = [f32(n, 2, channels_in, LANES) for n in sizes]
    back_sizes = plan["back_sizes"]
    back_specs = [
        pl.BlockSpec((n, wide_rows, LANES), lambda g, tab: (0, g, 0)) for n in back_sizes
    ]
    back_outs = [f32(n, channels, LANES) for n in back_sizes]
    held_spec = pl.BlockSpec((in_tiles + 1, rows, LANES), lambda g, tab: (0, g, 0))
    split_spec = pl.BlockSpec((tiles, 2, rows, LANES), lambda g, tab: (0, 0, g, 0))
    own_spec = pl.BlockSpec((tiles, wide_rows, LANES), lambda g, tab: (0, g, 0))
    w_spec = pl.BlockSpec((wide_rows, LANES), lambda g, tab: (g, 0))
    anywhere = pl.BlockSpec(memory_space=pl.ANY)
    cot_held = pltpu.VMEM((tiles + 1, 2 * UNIT, LANES), jnp.float32)

    pd_rows = round_up(per_dev, SUBL)
    small_rows = 2 * pd_rows + 4 * local_images
    pieces = [
        conv_weight.T,
        conv_bias[None],
        first_conv_w.T,
        first_conv_b[None],
        second_conv_w.T,
        second_conv_b[None],
        head_bias[None],
        head_weight.T,
        class_in[0],
        class_cot[0],
    ]
    own_specs = [
        *(whole(*p.shape) for p in pieces[:7]),
        whole(pd_rows, 2 * LANES),
        whole(local_images, 2 * LANES),
        whole(local_images, 3 * LANES),
    ]
    small = call(
        functools.partial(small_kernel, per_dev),
        [],
        pieces,
        own_specs,
        [f32(small_rows, LANES)],
        [whole(small_rows, LANES)],
        [pltpu.VMEM((LANES, LANES), jnp.float32)],
        1,
    )[0]

    sends = call(
        functools.partial(pack_kernel, plan),
        [table],
        [cot, small],
        [cot_spec, anywhere],
        halo_outs,
        halo_specs,
        [cot_held],
        steps,
    )
    x_held, cot_split = call(
        functools.partial(align_kernel, plan),
        [table],
        [x, cot, sends[0]],
        [x_spec, cot_spec, anywhere],
        [f32(in_tiles + 1, channels_in, LANES), f32(tiles, 2, channels_in, LANES)],
        [held_spec, split_spec],
        [cot_held],
        steps,
        fills=True,
    )

    sends = list(sends)
    cot_halo = [None] * len(sends)
    parts = small[None]
    rounds = bits_of("chan")
    rounds = rounds[:1] + rounds[:0:-1]
    for bit in rounds:
        got = swap(parts, "chan", bit)
        if bit == 1:
            got, sends = tied(got, sends)
        elif bit == rounds[1]:
            got, (x_held,) = tied(got, [x_held])
        parts = jnp.concatenate([parts, got], axis=0)
        if bit == 1:
            parts, sends = tied(parts, sends)
            for n, op in enumerate(plan["ops"]):
                if op["near"]:
                    cot_halo[n] = lax.ppermute(sends[n], "chan", op["pairs"])
    parts, sends = tied(parts, sends)
    if plan["ops"][0]["near"]:
        cot_halo[0], sends = tied(cot_halo[0], sends)
    for n, op in enumerate(plan["ops"]):
        if not op["near"]:
            cot_halo[n] = lax.ppermute(sends[n], "chan", op["pairs"])
    padded = round_up(channels, LANES)
    wide, turned, class_out, class_grad, grad_h, weight_norms = call(
        functools.partial(spread_kernel, groups, per_dev, rounds),
        [my_id],
        [parts, class_in[0], class_cot[0], x_held],
        [whole(*parts.shape), own_specs[8], own_specs[9], anywhere],
        [
            f32(channels, LANES),
            f32(LANES, padded),
            f32(local_images, channels),
            f32(local_images, channels_in),
            f32(pd_rows, 2 * LANES),
            f32(SUBL, LANES),
        ],
        [
            whole(channels, LANES),
            whole(LANES, padded),
            whole(local_images, channels),
            whole(local_images, channels_in),
            whole(pd_rows, 2 * LANES),
            whole(SUBL, LANES),
        ],
        [
            pltpu.VMEM((padded, LANES), jnp.float32),
            pltpu.VMEM((padded, 2 * LANES), jnp.float32),
            pltpu.VMEM((images, 3 * LANES), jnp.float32),
            pltpu.VMEM((images, 2 * LANES), jnp.float32),
        ],
        1,
    )

    partials = call(
        functools.partial(partial_kernel, plan),
        [table],
        [x_held, wide],
        [held_spec, w_spec],
        back_outs,
        back_specs,
        [pltpu.VMEM((plan["most"] + 1, 2 * UNIT, LANES), jnp.float32)],
        steps,
    )
    partials, late = list(partials), []
    pooled_halo = [None] * len(partials)
    for n, op in enumerate(plan["back_ops"]):
        if op["early"]:
            pooled_halo[n] = lax.ppermute(partials[n], "chan", op["pairs"])
        else:
            late.append(n)
    pooled_own = call(
        functools.partial(forward_kernel, plan),
        [table],
        [x_held, wide, partials[0]],
        [held_spec, w_spec, anywhere],
        [f32(tiles, channels, LANES)],
        [own_spec],
        [],
        steps,
    )[0]

    grad_h = sum_over(grad_h, "dp")
    head_t = head_weight.T
    head_first, head_second, head_update = moments(
        head_t, grad_h[:per_dev, :channels_in], first_head_w.T, second_head_w.T, 0.05
    )
    bias_first, bias_second, bias_update = moments(
        head_bias, grad_h[:per_dev, channels_in], first_head_b, second_head_b, 0.0
    )
    norms = jnp.stack([jnp.sum(head_update**2), jnp.sum(bias_update**2)])
    norms = jnp.where(lax.axis_index("dp") == 0, norms, 0.0)

    waiting = [partials[n] for n in late]
    waiting, cot_halo, pooled_own, norms = lax.optimization_barrier(
        (waiting, cot_halo, pooled_own, norms)
    )
    for n, v in zip(late, waiting):
        pooled_halo[n] = lax.ppermute(v, "chan", plan["back_ops"][n]["pairs"])
    cots_held = pltpu.VMEM((tiles + plan["halo"] + 1, 2, UNIT, LANES), jnp.float32)
    sums = call(
        functools.partial(weights_kernel, plan),
        [table],
        [x_held, cot_split, norms, pooled_own, *cot_halo],
        [held_spec, split_spec, pl.BlockSpec(memory_space=pltpu.SMEM), anywhere, *halo_specs],
        [f32(2 * SUBL, padded)],
        [whole(2 * SUBL, padded)],
        [cots_held, pltpu.VMEM((TAPS + 1, padded, LANES), jnp.float32)],
        steps,
    )[0]
    x_grad = call(
        functools.partial(patches_kernel, plan),
        [table],
        [cot_split, wide, sums, *cot_halo],
        [split_spec, w_spec, anywhere, *halo_specs],
        [f32(channels_in, n_in)],
        [x_spec],
        [cots_held, pltpu.VMEM((in_tiles + 1, UNIT, LANES), jnp.float32)],
        steps,
    )[0]
    sums = sum_over(sum_over(sums, "dp"), "chan")
    conv_shapes = [f32(TAPS, per_dev)] * 4
    head_shapes = [f32(per_dev, channels_in)] * 2
    operands = [
        sums,
        turned,
        weight_norms,
        *pieces[:6],
        average_conv_w.T,
        average_conv_b[None],
        head_t,
        head_update,
        average_head_w.T,
        head_bias[None],
        bias_update[None],
        average_head_b[None],
    ]
    out_shapes = [*conv_shapes, *head_shapes, f32(SUBL, LANES)]
    *conv_new, head_new, head_average, small_new = call(
        functools.partial(update_kernel, channels, per_dev),
        [my_id],
        operands,
        [whole(*v.shape) for v in operands],
        out_shapes,
        [whole(*v.shape) for v in out_shapes],
        [],
        1,
    )

    pooled = call(
        functools.partial(finish_kernel, plan),
        [table],
        [pooled_own, *pooled_halo],
        [own_spec, *back_specs],
        [f32(channels, n_out)],
        [cot_spec],
        [cot_held, pltpu.VMEM((plan["back_halo"] + 1, 2 * UNIT, LANES), jnp.float32)],
        steps,
    )[0]
    bias_new = [small_new[k, :per_dev] for k in range(6)]
    return (
        pooled.T[None],
        class_out[None],
        x_grad.T[None],
        class_grad[None],
        *(v.T for v in conv_new),
        *bias_new[:4],
        head_first.T,
        head_second.T,
        head_new.T,
        head_average.T,
        bias_first,
        bias_second,
        *bias_new[4:],
        small_new[6, :4],
    )


def solution(mesh):
    return jax.shard_map(
        per_device,
        mesh=mesh,
        in_specs=(
            P("dp", "chan", None),
            P("dp", "chan", None),
            P("chan", None),
            P("chan"),
            P(None, "chan"),
            P("chan"),
            P("chan", None),
            P("chan"),
            P(None, "chan"),
            P("chan"),
            P("chan", None),
            P("chan"),
            P(None, "chan"),
            P("chan"),
            P("chan", None),
            P("chan"),
            P(None, "chan"),
            P("chan"),
            P("dp", "chan", None),
            P("dp", "chan", None),
        ),
        out_specs=(
            P("dp", "chan", None),
            P("dp", "chan", None),
            P("dp", "chan", None),
            P("dp", "chan", None),
            P("chan", None),
            P("chan", None),
            P("chan", None),
            P("chan", None),
            P("chan"),
            P("chan"),
            P("chan"),
            P("chan"),
            P(None, "chan"),
            P(None, "chan"),
            P(None, "chan"),
            P(None, "chan"),
            P("chan"),
            P("chan"),
            P("chan"),
            P("chan"),
            P(),
        ),
        check_vma=False,
    )
```

time: 1530 us -> 145 us (0.09)
  local copies, waits for them, and re-layouts: 589 us -> 5.37 us
  blocking collectives: 408 us -> 0 us
  waiting for transfers between devices: 345 us -> 36.3 us
  other arithmetic: 136 us -> 7.36 us
  Pallas kernels: 0 us -> 69.3 us
    unnamed x3 -> x0, blocking collectives: 363 us -> none
    all_to_all x4 -> x0, waiting for transfers between devices: 345 us -> none  [the longest x1 280 us: per_device(): lax.all_to_all(doubled, 'chan', split_axis=1, concat_axis=0, tiled=True)]
    all_to_all x8 -> x0, local copies, waits for them, and re-layouts: 180 us -> none  [the longest x2 95.3 us: per_device(): lax.all_to_all(back_cols, 'chan', split_axis=0, concat_axis=1, tiled=True)]
    slice x10 -> x1, local copies, waits for them, and re-layouts: 178 us -> 0.18 us  [per_device(): grad_h[:per_dev, channels_in]]
    unnamed x85 -> x22, local copies, waits for them, and re-layouts: 80.2 us -> 1.21 us
    add x7, other arithmetic: 80.7 us -> 2.17 us  [sum_over(): x = x + swap(x, axis, bit)]
    reshape x13 -> x0, local copies, waits for them, and re-layouts: 76.2 us -> none  [the longest x1 45.7 us: per_device(): grid = columns.reshape(GRID, GRID, wide)]
    pallas_call x0 -> x10, Pallas kernels: none -> 69.3 us  [call(): pl.pallas_call(kernel, grid_spec=pltpu.PrefetchScalarGridSpec(num_scalar_...]
  transfers between devices with their start and end apart: 5 -> 16, of which waited for: 2 -> 8; matrix products, arithmetic and copies ran while one was open for 41% -> 8% of each run, Pallas kernels for 0% -> 42%
where the time goes in v2:
time: 145 us; the launch traced here: 144 us
  Pallas kernels  69.3 us (48%)
  waiting for transfers between devices  36.3 us (25%)
  starting transfers between devices  24.3 us (17%)
  other arithmetic  7.36 us (5%)
  local copies, waits for them, and re-layouts  5.37 us (4%)
    pallas_call x10, Pallas kernels, call(): pl.pallas_call(kernel, grid_spec=pltpu.PrefetchScalarGridSpec(num_scalar_...  69.3 us
    ppermute x10, waiting for transfers between devices, swap(): return lax.ppermute(x, axis, [(k, k ^ bit) for k in range(size)])  28.3 us
    ppermute x10, starting transfers between devices, swap(): return lax.ppermute(x, axis, [(k, k ^ bit) for k in range(size)])  13.5 us
    ppermute x3, waiting for transfers between devices, per_device(): cot_halo[n] = lax.ppermute(sends[n], 'chan', op['pairs'])  8 us
    ppermute x3, starting transfers between devices, per_device(): cot_halo[n] = lax.ppermute(sends[n], 'chan', op['pairs'])  4.6 us
    ppermute x2, starting transfers between devices, per_device(): pooled_halo[n] = lax.ppermute(v, 'chan', plan['back_ops'][n]['pairs'])  3.21 us
    ppermute x1, starting transfers between devices, per_device(): pooled_halo[n] = lax.ppermute(partials[n], 'chan', op['pairs'])  2.97 us
  transfers between devices with their start and end apart: 16, of which 8 were waited for; matrix products, arithmetic and copies ran while one was open for 8% of the time, Pallas kernels for 42%

profile of v2, /device:TPU:9, one launch (start us, length us, event | category | flops | bytes accessed | tf_op | source)
XLA Modules:
  0.0 143.5 jit_solution(3734450698339540025)
XLA Ops:
  0.7 1.6 %shard_map.364.after = f32[144,128]{1,0:T(8,128)} custom-call(f32[9,36]{1,0:T(8,128)} %bitcast.87, f32[1,36]{1,0:T(1,128)} %bitcast.96, f32[9,36]{1,0:T(8,128)} %bitcast.89, f32[1,36]{1,0:T(1,128)} %bitcast.98, f32[9,36]{1,0:T(8,128)} %bitcast.91, f32[1,36]{1,0:T(1,128)} %bitcast.100, f32[1,36]{1,0:T(1,128)} %bitcast.94, f32[36,144]{1,0:T(8,128)} %bitcast.80, ...), custom_call_target="tpu_custom_call" | custom-call | flops 1 | bytes 1 | tf_op jit(solution)/shard_map/pallas_call | solution.py:690
  2.3 1.2 collective-permute-start
  3.5 1.4 dynamic-slice_reduce_fusion.tab
  4.9 5.9 %shard_map.365 = (f32[6,2,144,128]{3,2,1,0:T(8,128)}, f32[5,2,144,128]{3,2,1,0:T(8,128)}, f32[8,2,144,128]{3,2,1,0:T(8,128)}) custom-call(s32[826]{0:T(1024)} %dynamic-slice_reduce_fusion.tab, f32[288,3136]{1,0:T(8,128)} %bitcast.73, f32[144,128]{1,0:T(8,128)} %shard_map.364.after), custom_call_target="tpu_custom_call" | custom-call | flops 1 | bytes 1 | tf_op jit(solution)/shard_map/pallas_call | solution.py:690
  10.8 0.0 collective-permute-done
  10.8 0.0 copy-done.4
  10.8 0.3 collective-permute-start.3
  11.1 2.3 %collective-permute-start.1 = (f32[2,144,128]{2,1,0:T(8,128)S(1)}, f32[2,144,128]{2,1,0:T(8,128)S(1)}, u32[]{:S(2)}, u32[]{:S(2)}) collective-permute-start(f32[2,144,128]{2,1,0:T(8,128)S(1)} %pad_maximum_fusion.2), channel_id=1, source_target_pairs={{0,4},{1,5},{2,6},{3,7},{4,0},{5,1},{6,2},{7,3},{8,12},{9,13},{10,... | collective-permute-start | bytes 442376 | tf_op jit(solution)/shard_map/ppermute | solution.py:723
  13.5 11.4 %shard_map.366 = (f32[93,144,128]{2,1,0:T(8,128)}, f32[25,2,144,128]{3,2,1,0:T(8,128)}) custom-call(s32[826]{0:T(1024)} %dynamic-slice_reduce_fusion.tab, f32[144,11664]{1,0:T(8,128)} %bitcast.75, f32[288,3136]{1,0:T(8,128)} %bitcast.74, f32[6,2,144,128]{3,2,1,0:T(8,128)} %get-tuple-element.74.after), custom_call_target="tpu_custom_call" | custom-call | flops 1 | bytes 21758976 | tf_op jit(solution)/shard_map/pallas_call | solution.py:690
  24.9 0.0 collective-permute-done.1
  24.9 0.2 collective-permute-start.2
  25.1 6.8 %collective-permute-done.2 = f32[4,144,128]{2,1,0:T(8,128)S(1)} collective-permute-done((f32[4,144,128]{2,1,0:T(8,128)S(1)}, f32[4,144,128]{2,1,0:T(8,128)S(1)}, u32[]{:S(2)}, u32[]{:S(2)}) %collective-permute-start.2) | collective-permute-done | bytes 294944 | tf_op jit(solution)/shard_map/ppermute | solution.py:723
  32.0 0.9 pad_maximum_fusion.parts
  32.9 0.0 collective-permute-done.3.refs_0_
  32.9 3.0 %collective-permute-start.5 = (f32[8,2,144,128]{3,2,1,0:T(8,128)}, f32[8,2,144,128]{3,2,1,0:T(8,128)S(1)}, u32[]{:S(2)}, u32[]{:S(2)}) collective-permute-start(f32[8,2,144,128]{3,2,1,0:T(8,128)} %get-tuple-element.83), channel_id=1, source_target_pairs={{3,4},{4,3},{1,2},{2,1},{5,6},{6,5},{11,12},{12,11},{9,10},{10,9},... | collective-permute-start | bytes 3538952 | tf_op jit(solution)/shard_map/ppermute | solution.py:888
  35.9 2.9 %shard_map.367 = (f32[288,128]{1,0:T(8,128)}, f32[128,384]{1,0:T(8,128)}, f32[16,288]{1,0:T(8,128)}, f32[16,144]{1,0:T(8,128)}, f32[40,256]{1,0:T(8,128)}, /*index=5*/f32[8,128]{1,0:T(8,128)}) custom-call(s32[1]{0:T(128)} %bitcast.16.me, f32[8,144,128]{2,1,0:T(8,128)} %pad_maximum_fusion.parts, f32[16,144]{1,0:T(8,128)} %bitcast.85, f32[16,288]{1,0:T(8,128)} %bitcast.83, ...), custom_call_target="tpu_custom_call" | custom-call | flops 1 | bytes 1 | tf_op jit(solution)/shard_map/pallas_call | solution.py:690
  38.8 0.0 copy-done.1
  38.8 1.2 collective-permute-start.6
  40.0 1.3 collective-permute-start.4
  41.3 0.9 collective-permute-done.6
  42.2 0.8 add.56
  43.0 3.6 %collective-permute-start.7 = (f32[40,256]{1,0:T(8,128)S(1)}, f32[40,256]{1,0:T(8,128)S(1)}, u32[]{:S(2)}, u32[]{:S(2)}) collective-permute-start(f32[40,256]{1,0:T(8,128)S(1)} %add.56), channel_id=1, source_target_pairs={{0,8},{8,0},{16,24},{24,16},{1,9},{9,1},{17,25},{25,17},{2,10},{10... | collective-permute-start | bytes 122888 | tf_op jit(solution)/shard_map/ppermute | solution.py:723
  46.5 8.0 %shard_map.368 = (f32[11,288,128]{2,1,0:T(8,128)}, f32[8,288,128]{2,1,0:T(8,128)}, f32[6,288,128]{2,1,0:T(8,128)}) custom-call(s32[826]{0:T(1024)} %dynamic-slice_reduce_fusion.tab, f32[93,144,128]{2,1,0:T(8,128)} %get-tuple-element.72.after.x_ref, f32[288,128]{1,0:T(8,128)} %get-tuple-element.78.w_ref), custom_call_target="tpu_custom_call" | custom-call | flops 1 | bytes 1 | tf_op jit(solution)/shard_map/pallas_call | solution.py:690
  54.5 0.0 copy-start.5
  54.5 0.0 copy-start.6
  54.6 0.0 copy-start.7
  54.6 9.5 %shard_map.369.own_ref.after = f32[25,288,128]{2,1,0:T(8,128)} custom-call(s32[826]{0:T(1024)} %dynamic-slice_reduce_fusion.tab, f32[93,144,128]{2,1,0:T(8,128)} %get-tuple-element.72.after.x_ref, f32[288,128]{1,0:T(8,128)} %get-tuple-element.78.w_ref, f32[11,288,128]{2,1,0:T(8,128)} %get-tuple-element.84.after), custom_call_target="tpu_custom_call" | custom-call | flops 1 | bytes 1 | tf_op jit(solution)/shard_map/pallas_call | solution.py:690
  64.1 3.0 %collective-permute-start.8 = (f32[11,288,128]{2,1,0:T(8,128)}, f32[11,288,128]{2,1,0:T(8,128)S(1)}, u32[]{:S(2)}, u32[]{:S(2)}) collective-permute-start(f32[11,288,128]{2,1,0:T(8,128)} %get-tuple-element.84.after), channel_id=1, source_target_pairs={{2,3},{5,4},{0,1},{7,6},{10,11},{13,12},{8,9},{15,14},{18,19},{21,... | collective-permute-start | bytes 4866056 | tf_op jit(solution)/shard_map/ppermute | solution.py:934
  67.0 0.0 collective-permute-done.7
  67.1 0.2 slice_reduce_fusion
  67.2 0.0 copy-done.8
  67.3 0.0 copy-done.9
  67.3 0.0 copy-done.10
  67.3 1.1 multiply_reduce_fusion.1
  68.4 1.3 multiply_reduce_fusion
  69.7 1.9 %broadcast_select_fusion.norms = f32[2]{0:T(128)} fusion(pred[]{:T(512)S(6)} %eq.3, f32[1]{0:T(128)} %bitcast.20, f32[1]{0:T(128)} %bitcast.19), kind=kLoop, calls=%fused_computation.12 | loop fusion | flops 4 | bytes 17 | tf_op jit(solution)/shard_map/jit(_where)/select_n | solution.py:957
  71.5 8.0 %collective-permute-done.4.refs_1_ = f32[5,2,144,128]{3,2,1,0:T(8,128)S(1)} collective-permute-done((f32[5,2,144,128]{3,2,1,0:T(8,128)}, f32[5,2,144,128]{3,2,1,0:T(8,128)S(1)}, u32[]{:S(2)}, u32[]{:S(2)}) %collective-permute-start.4) | collective-permute-done | bytes 737312 | tf_op jit(solution)/shard_map/ppermute | solution.py:882
  79.5 0.0 collective-permute-done.5.refs_2_
  79.6 1.9 %collective-permute-start.9 = (f32[8,288,128]{2,1,0:T(8,128)}, f32[8,288,128]{2,1,0:T(8,128)}, u32[]{:S(2)}, u32[]{:S(2)}) collective-permute-start(f32[8,288,128]{2,1,0:T(8,128)} %get-tuple-element.87), channel_id=1, source_target_pairs={{3,4},{4,3},{1,2},{2,1},{5,6},{6,5},{11,12},{12,11},{9,10},{10,9},... | collective-permute-start | bytes 3538952 | tf_op jit(solution)/shard_map/ppermute | solution.py:964
  81.5 1.3 collective-permute-start.10
  82.8 0.0 copy-done.2
  82.8 0.0 copy-done
  82.8 9.1 %shard_map.371.after = f32[16,384]{1,0:T(8,128)} custom-call(s32[826]{0:T(1024)} %dynamic-slice_reduce_fusion.tab, f32[93,144,128]{2,1,0:T(8,128)} %get-tuple-element.72.after.x_ref, f32[25,2,144,128]{3,2,1,0:T(8,128)} %get-tuple-element.90.cot_ref, f32[2]{0:T(128)} %broadcast_select_fusion.norms, f32[25,288,128]{2,1,0:T(8,128)} %shard_map.369.own_ref.after, ...), custom_call_target="tpu_custom_call" | custom-call | flops 1 | bytes 1 | tf_op jit(solution)/shard_map/pallas_call | solution.py:690
  91.9 1.2 collective-permute-start.11
  93.1 2.1 %collective-permute-done.11 = f32[16,384]{1,0:T(8,128)S(1)} collective-permute-done((f32[16,384]{1,0:T(8,128)}, f32[16,384]{1,0:T(8,128)S(1)}, u32[]{:S(2)}, u32[]{:S(2)}) %collective-permute-start.11) | collective-permute-done | bytes 24608 | tf_op jit(solution)/shard_map/ppermute | solution.py:723
  95.2 0.7 add.68
  95.9 1.2 collective-permute-start.12
  97.1 0.8 collective-permute-done.12
  98.0 2.4 %collective-permute-start.13 = (f32[16,384]{1,0:T(8,128)S(1)}, f32[16,384]{1,0:T(8,128)S(1)}, u32[]{:S(2)}, u32[]{:S(2)}) collective-permute-start(f32[16,384]{1,0:T(8,128)S(1)} %add.69), channel_id=1, source_target_pairs={{0,4},{1,5},{2,6},{3,7},{4,0},{5,1},{6,2},{7,3},{8,12},{9,13},{10,... | collective-permute-start | bytes 73736 | tf_op jit(solution)/shard_map/ppermute | solution.py:723
  100.3 8.7 %collective-permute-done.13 = f32[16,384]{1,0:T(8,128)S(1)} collective-permute-done((f32[16,384]{1,0:T(8,128)S(1)}, f32[16,384]{1,0:T(8,128)S(1)}, u32[]{:S(2)}, u32[]{:S(2)}) %collective-permute-start.13) | collective-permute-done | bytes 24608 | tf_op jit(solution)/shard_map/ppermute | solution.py:723
  109.1 0.2 collective-permute-start.14
  109.2 2.9 %collective-permute-done.14 = f32[16,384]{1,0:T(8,128)S(1)} collective-permute-done((f32[16,384]{1,0:T(8,128)S(1)}, f32[16,384]{1,0:T(8,128)S(1)}, u32[]{:S(2)}, u32[]{:S(2)}) %collective-permute-start.14) | collective-permute-done | bytes 24608 | tf_op jit(solution)/shard_map/ppermute | solution.py:723
  112.2 0.0 collective-permute-start.15
  112.2 11.7 %shard_map.372 = f32[144,11664]{1,0:T(8,128)} custom-call(s32[826]{0:T(1024)} %dynamic-slice_reduce_fusion.tab, f32[25,2,144,128]{3,2,1,0:T(8,128)} %get-tuple-element.90.cot_ref, f32[288,128]{1,0:T(8,128)} %get-tuple-element.78.w_ref, f32[16,384]{1,0:T(8,128)} %shard_map.371.after, f32[6,2,144,128]{3,2,1,0:T(8,128)} %copy-done.1, ...), custom_call_target="tpu_custom_call" | custom-call | flops 1 | bytes 1 | tf_op jit(solution)/shard_map/pallas_call | solution.py:690
  123.9 6.1 %collective-permute-done.15 = f32[16,384]{1,0:T(8,128)S(1)} collective-permute-done((f32[16,384]{1,0:T(8,128)S(1)}, f32[16,384]{1,0:T(8,128)S(1)}, u32[]{:S(2)}, u32[]{:S(2)}) %collective-permute-start.15) | collective-permute-done | bytes 24608 | tf_op jit(solution)/shard_map/ppermute | solution.py:723
  129.9 0.6 add.72.sums
  130.5 2.0 %shard_map.373 = (f32[9,36]{1,0:T(8,128)}, f32[9,36]{1,0:T(8,128)}, f32[9,36]{1,0:T(8,128)}, f32[9,36]{1,0:T(8,128)}, f32[36,144]{1,0:T(8,128)}, /*index=5*/f32[36,144]{1,0:T(8,128)}, f32[8,128]{1,0:T(8,128)}) custom-call(s32[1]{0:T(128)} %bitcast.16.me, f32[16,384]{1,0:T(8,128)} %add.72.sums, f32[128,384]{1,0:T(8,128)} %get-tuple-element.96.table, ...), custom_call_target="tpu_custom_call" | custom-call | flops 1 | bytes 1 | tf_op jit(solution)/shard_map/pallas_call | solution.py:690
  132.5 1.2 slice_bitcast_fusion
  133.7 1.4 slice_bitcast_fusion.1
  135.2 0.0 collective-permute-done.8.refs_0_
  135.2 0.0 collective-permute-done.10.refs_2_
  135.2 0.0 collective-permute-done.9.refs_1_
  135.2 1.2 copy-done.3
  136.4 7.2 %shard_map.370 = f32[288,3136]{1,0:T(8,128)} custom-call(s32[826]{0:T(1024)} %dynamic-slice_reduce_fusion.tab, f32[25,288,128]{2,1,0:T(8,128)} %shard_map.369.own_ref.after, f32[11,288,128]{2,1,0:T(8,128)} %copy-done.3, f32[8,288,128]{2,1,0:T(8,128)} %collective-permute-done.9.refs_1_, f32[6,288,128]{2,1,0:T(8,128)} %collective-permute-done.10.refs_2_), custom_call_target="tpu_custom_call" | custom-call | flops 1 | bytes 1 | tf_op jit(solution)/shard_map/pallas_call | solution.py:690
  (17 shorter events, 0.1 us)
Async XLA Ops:
  2.3 8.5 %copy-start.4 = (f32[144,128]{1,0:T(8,128)S(1)}, f32[144,128]{1,0:T(8,128)}, u32[]{:S(2)}) copy-start(f32[144,128]{1,0:T(8,128)} %shard_map.364.after) | copy-start | bytes 221188
  2.3 8.5 %collective-permute-start = (f32[1,144,128]{2,1,0:T(8,128)}, f32[1,144,128]{2,1,0:T(8,128)S(1)}, u32[]{:S(2)}, u32[]{:S(2)}) collective-permute-start(f32[1,144,128]{2,1,0:T(8,128)} %bitcast.78), channel_id=1, source_target_pairs={{0,1},{1,0},{2,3},{3,2},{4,5},{5,4},{6,7},{7,6},{8,9},{9,8},{10,11... | collective-permute-start | bytes 221192 | tf_op jit(solution)/shard_map/ppermute | solution.py:723
  10.8 22.0 %collective-permute-start.3 = (f32[6,2,144,128]{3,2,1,0:T(8,128)}, f32[6,2,144,128]{3,2,1,0:T(8,128)S(1)}, u32[]{:S(2)}, u32[]{:S(2)}) collective-permute-start(f32[6,2,144,128]{3,2,1,0:T(8,128)} %get-tuple-element.74.after), channel_id=1, source_target_pairs={{0,1},{1,0},{3,2},{4,5},{6,7},{7,6},{2,3},{5,4},{8,9},{9,8},{11,10... | collective-permute-start | bytes 2654216 | tf_op jit(solution)/shard_map/ppermute | solution.py:882
  11.1 13.7 %collective-permute-start.1 = (f32[2,144,128]{2,1,0:T(8,128)S(1)}, f32[2,144,128]{2,1,0:T(8,128)S(1)}, u32[]{:S(2)}, u32[]{:S(2)}) collective-permute-start(f32[2,144,128]{2,1,0:T(8,128)S(1)} %pad_maximum_fusion.2), channel_id=1, source_target_pairs={{0,4},{1,5},{2,6},{3,7},{4,0},{5,1},{6,2},{7,3},{8,12},{9,13},{10,... | collective-permute-start | bytes 442376 | tf_op jit(solution)/shard_map/ppermute | solution.py:723
  24.9 7.0 %collective-permute-start.2 = (f32[4,144,128]{2,1,0:T(8,128)S(1)}, f32[4,144,128]{2,1,0:T(8,128)S(1)}, u32[]{:S(2)}, u32[]{:S(2)}) collective-permute-start(f32[4,144,128]{2,1,0:T(8,128)S(1)} %pad_maximum_fusion.1), channel_id=1, source_target_pairs={{0,2},{1,3},{2,0},{3,1},{4,6},{5,7},{6,4},{7,5},{8,10},{9,11},{10,... | collective-permute-start | bytes 884744 | tf_op jit(solution)/shard_map/ppermute | solution.py:723
  32.9 6.0 %copy-start.1 = (f32[6,2,144,128]{3,2,1,0:T(8,128)}, f32[6,2,144,128]{3,2,1,0:T(8,128)S(1)}, u32[]{:S(2)}) copy-start(f32[6,2,144,128]{3,2,1,0:T(8,128)S(1)} %collective-permute-done.3.refs_0_) | copy-start | bytes 2654212
  32.9 46.7 %collective-permute-start.5 = (f32[8,2,144,128]{3,2,1,0:T(8,128)}, f32[8,2,144,128]{3,2,1,0:T(8,128)S(1)}, u32[]{:S(2)}, u32[]{:S(2)}) collective-permute-start(f32[8,2,144,128]{3,2,1,0:T(8,128)} %get-tuple-element.83), channel_id=1, source_target_pairs={{3,4},{4,3},{1,2},{2,1},{5,6},{6,5},{11,12},{12,11},{9,10},{10,9},... | collective-permute-start | bytes 3538952 | tf_op jit(solution)/shard_map/ppermute | solution.py:888
  38.8 3.4 %collective-permute-start.6 = (f32[40,256]{1,0:T(8,128)}, f32[40,256]{1,0:T(8,128)S(1)}, u32[]{:S(2)}, u32[]{:S(2)}) collective-permute-start(f32[40,256]{1,0:T(8,128)} %get-tuple-element.85), channel_id=1, source_target_pairs={{0,16},{8,24},{16,0},{24,8},{1,17},{9,25},{17,1},{25,9},{2,18},{10... | collective-permute-start | bytes 122888 | tf_op jit(solution)/shard_map/ppermute | solution.py:723
  40.0 39.5 %collective-permute-start.4 = (f32[5,2,144,128]{3,2,1,0:T(8,128)}, f32[5,2,144,128]{3,2,1,0:T(8,128)S(1)}, u32[]{:S(2)}, u32[]{:S(2)}) collective-permute-start(f32[5,2,144,128]{3,2,1,0:T(8,128)} %get-tuple-element.75), channel_id=1, source_target_pairs={{3,2},{4,5},{1,0},{6,7},{11,10},{12,13},{9,8},{14,15},{19,18},{20,... | collective-permute-start | bytes 2211848 | tf_op jit(solution)/shard_map/ppermute | solution.py:882
  43.0 24.1 %collective-permute-start.7 = (f32[40,256]{1,0:T(8,128)S(1)}, f32[40,256]{1,0:T(8,128)S(1)}, u32[]{:S(2)}, u32[]{:S(2)}) collective-permute-start(f32[40,256]{1,0:T(8,128)S(1)} %add.56), channel_id=1, source_target_pairs={{0,8},{8,0},{16,24},{24,16},{1,9},{9,1},{17,25},{25,17},{2,10},{10... | collective-permute-start | bytes 122888 | tf_op jit(solution)/shard_map/ppermute | solution.py:723
  54.5 12.7 %copy-start.8 = (f32[36]{0:T(128)S(1)}, f32[36]{0:T(128)}, u32[]{:S(2)}) copy-start(f32[36]{0:T(128)} %param.26) | copy-start | bytes 436
  54.5 12.7 %copy-start.9 = (f32[36]{0:T(128)S(1)}, f32[36]{0:T(128)}, u32[]{:S(2)}) copy-start(f32[36]{0:T(128)} %param.30) | copy-start | bytes 436
  54.5 12.7 %copy-start.10 = (f32[36]{0:T(128)S(1)}, f32[36]{0:T(128)}, u32[]{:S(2)}) copy-start(f32[36]{0:T(128)} %param.34) | copy-start | bytes 436
  54.5 13.9 %copy-start.5 = (f32[144,36]{0,1:T(8,128)S(1)}, f32[144,36]{0,1:T(8,128)}, u32[]{:S(2)}) copy-start(f32[144,36]{0,1:T(8,128)} %param.25) | copy-start | bytes 62212
  54.5 13.9 %copy-start.6 = (f32[144,36]{0,1:T(8,128)S(1)}, f32[144,36]{0,1:T(8,128)}, u32[]{:S(2)}) copy-start(f32[144,36]{0,1:T(8,128)} %param.33) | copy-start | bytes 62212
  54.6 13.9 %copy-start.7 = (f32[144,36]{0,1:T(8,128)S(1)}, f32[144,36]{0,1:T(8,128)}, u32[]{:S(2)}) copy-start(f32[144,36]{0,1:T(8,128)} %param.29) | copy-start | bytes 62212
  64.1 71.1 %collective-permute-start.8 = (f32[11,288,128]{2,1,0:T(8,128)}, f32[11,288,128]{2,1,0:T(8,128)S(1)}, u32[]{:S(2)}, u32[]{:S(2)}) collective-permute-start(f32[11,288,128]{2,1,0:T(8,128)} %get-tuple-element.84.after), channel_id=1, source_target_pairs={{2,3},{5,4},{0,1},{7,6},{10,11},{13,12},{8,9},{15,14},{18,19},{21,... | collective-permute-start | bytes 4866056 | tf_op jit(solution)/shard_map/ppermute | solution.py:934
  79.5 3.2 %copy-start.2 = (f32[5,2,144,128]{3,2,1,0:T(8,128)}, f32[5,2,144,128]{3,2,1,0:T(8,128)S(1)}, u32[]{:S(2)}) copy-start(f32[5,2,144,128]{3,2,1,0:T(8,128)S(1)} %collective-permute-done.4.refs_1_) | copy-start | bytes 2211844
  79.6 3.2 %copy-start = (f32[8,2,144,128]{3,2,1,0:T(8,128)}, f32[8,2,144,128]{3,2,1,0:T(8,128)S(1)}, u32[]{:S(2)}) copy-start(f32[8,2,144,128]{3,2,1,0:T(8,128)S(1)} %collective-permute-done.5.refs_2_) | copy-start | bytes 3538948
  79.6 55.6 %collective-permute-start.9 = (f32[8,288,128]{2,1,0:T(8,128)}, f32[8,288,128]{2,1,0:T(8,128)}, u32[]{:S(2)}, u32[]{:S(2)}) collective-permute-start(f32[8,288,128]{2,1,0:T(8,128)} %get-tuple-element.87), channel_id=1, source_target_pairs={{3,4},{4,3},{1,2},{2,1},{5,6},{6,5},{11,12},{12,11},{9,10},{10,9},... | collective-permute-start | bytes 3538952 | tf_op jit(solution)/shard_map/ppermute | solution.py:964
  81.5 53.7 %collective-permute-start.10 = (f32[6,288,128]{2,1,0:T(8,128)}, f32[6,288,128]{2,1,0:T(8,128)}, u32[]{:S(2)}, u32[]{:S(2)}) collective-permute-start(f32[6,288,128]{2,1,0:T(8,128)} %get-tuple-element.88), channel_id=1, source_target_pairs={{1,0},{6,7},{3,2},{4,5},{9,8},{14,15},{11,10},{12,13},{17,16},{22,... | collective-permute-start | bytes 2654216 | tf_op jit(solution)/shard_map/ppermute | solution.py:964
  91.9 3.3 %collective-permute-start.11 = (f32[16,384]{1,0:T(8,128)}, f32[16,384]{1,0:T(8,128)S(1)}, u32[]{:S(2)}, u32[]{:S(2)}) collective-permute-start(f32[16,384]{1,0:T(8,128)} %shard_map.371.after), channel_id=1, source_target_pairs={{0,16},{8,24},{16,0},{24,8},{1,17},{9,25},{17,1},{25,9},{2,18},{10... | collective-permute-start | bytes 73736 | tf_op jit(solution)/shard_map/ppermute | solution.py:723
  95.9 2.1 %collective-permute-start.12 = (f32[16,384]{1,0:T(8,128)S(1)}, f32[16,384]{1,0:T(8,128)S(1)}, u32[]{:S(2)}, u32[]{:S(2)}) collective-permute-start(f32[16,384]{1,0:T(8,128)S(1)} %add.68), channel_id=1, source_target_pairs={{0,8},{8,0},{16,24},{24,16},{1,9},{9,1},{17,25},{25,17},{2,10},{10... | collective-permute-start | bytes 73736 | tf_op jit(solution)/shard_map/ppermute | solution.py:723
  98.0 11.1 %collective-permute-start.13 = (f32[16,384]{1,0:T(8,128)S(1)}, f32[16,384]{1,0:T(8,128)S(1)}, u32[]{:S(2)}, u32[]{:S(2)}) collective-permute-start(f32[16,384]{1,0:T(8,128)S(1)} %add.69), channel_id=1, source_target_pairs={{0,4},{1,5},{2,6},{3,7},{4,0},{5,1},{6,2},{7,3},{8,12},{9,13},{10,... | collective-permute-start | bytes 73736 | tf_op jit(solution)/shard_map/ppermute | solution.py:723
  109.1 3.1 %collective-permute-start.14 = (f32[16,384]{1,0:T(8,128)S(1)}, f32[16,384]{1,0:T(8,128)S(1)}, u32[]{:S(2)}, u32[]{:S(2)}) collective-permute-start(f32[16,384]{1,0:T(8,128)S(1)} %add.70), channel_id=1, source_target_pairs={{0,2},{1,3},{2,0},{3,1},{4,6},{5,7},{6,4},{7,5},{8,10},{9,11},{10,... | collective-permute-start | bytes 73736 | tf_op jit(solution)/shard_map/ppermute | solution.py:723
  112.2 17.8 %collective-permute-start.15 = (f32[16,384]{1,0:T(8,128)S(1)}, f32[16,384]{1,0:T(8,128)S(1)}, u32[]{:S(2)}, u32[]{:S(2)}) collective-permute-start(f32[16,384]{1,0:T(8,128)S(1)} %add.71), channel_id=1, source_target_pairs={{0,1},{1,0},{2,3},{3,2},{4,5},{5,4},{6,7},{7,6},{8,9},{9,8},{10,11... | collective-permute-start | bytes 73736 | tf_op jit(solution)/shard_map/ppermute | solution.py:723
  135.2 1.2 copy-start.3

commit v3 on v2

--- a/solution.py
+++ b/solution.py
@@ -27,17 +27,27 @@
 
 def grouped(messages, spare):
     ops = []
-    for (src, dst), tiles in sorted(messages, key=lambda kv: (-len(kv[1]), kv[0])):
+    for (src, dst), (full, half) in sorted(
+        messages, key=lambda kv: (-2 * len(kv[1][0]) - len(kv[1][1]), kv[0])
+    ):
         for op in ops:
-            if op["size"] - len(tiles) <= spare and all(
-                src != s and dst != d for s, d in op["pairs"]
+            waste = op["full"] + op["half"] / 2 - len(full) - len(half) / 2
+            if (
+                len(full) <= op["full"]
+                and len(half) <= op["half"]
+                and waste <= spare
+                and all(src != s and dst != d for s, d in op["pairs"])
             ):
                 break
         else:
-            op = {"size": len(tiles), "pairs": [], "tiles": []}
+            op = {"full": len(full), "half": len(half), "pairs": [], "tiles": []}
+            op["size"] = op["full"] + op["half"]
             ops.append(op)
         op["pairs"].append((src, dst))
-        op["tiles"].append(tiles)
+        op["tiles"].append(
+            [(j, *v) for j, v in enumerate(full)]
+            + [(op["full"] + j, *v) for j, v in enumerate(half)]
+        )
     for op in ops:
         op["near"] = all(src ^ dst == 1 for src, dst in op["pairs"])
     return ops
@@ -66,13 +76,26 @@
             k = int(p_owner[p])
             for t in range(TAPS):
                 if tap_tile[p, t] >= 0 and t_owner[p, t] != k:
-                    wanted.setdefault((k, int(t_owner[p, t])), set()).add(p)
-    wanted = {pair: sorted(tiles) for pair, tiles in wanted.items()}
-    near = {pair: tiles for pair, tiles in wanted.items() if pair[0] ^ pair[1] == 1}
-    even = max([min(len(t), len(near.get(p[::-1], []))) for p, t in near.items()], default=0)
-    ops = grouped([(p, t[:even]) for p, t in near.items() if even], even)
-    ops += grouped([(p, t[even:]) for p, t in near.items() if len(t) > even], 2)
-    ops += grouped([(p, t) for p, t in wanted.items() if p not in near], 2)
+                    lanes = wanted.setdefault((k, int(t_owner[p, t])), {}).setdefault(p, set())
+                    lanes.update((lane, lane + step - 1))
+    middle = LANES // 2
+    for pair, tiles in wanted.items():
+        full, half = [], []
+        for p, lanes in sorted(tiles.items()):
+            low, high = max(lanes) < middle, min(lanes) >= middle
+            (half if low or high else full).append((p, int(high)))
+        wanted[pair] = (full, half)
+    near = {p: t for p, t in wanted.items() if p[0] ^ p[1] == 1}
+    weight = {p: 2 * len(t[0]) + len(t[1]) for p, t in near.items()}
+    even = max([min(w, weight.get(p[::-1], 0)) for p, w in weight.items()], default=0)
+    begin, rest = [], []
+    for p, (full, half) in near.items():
+        some = max(even - len(half), 0) // 2
+        begin.append((p, (full[:some], half)))
+        if full[some:]:
+            rest.append((p, (full[some:], [])))
+    ops = grouped(begin, even) + grouped(rest, 2)
+    ops += grouped([(p, t) for p, t in wanted.items() if p[0] ^ p[1] != 1], 2)
     back_ops = grouped([((d, s), t) for (s, d), t in wanted.items()], 2)
     longest = max(op["size"] for op in back_ops)
     for op in back_ops:
@@ -94,12 +117,14 @@
     none = out_tiles + halo
     own_slot = np.full((groups, halo), out_tiles, np.int64)
     got = [[] for _ in range(groups)]
+    upper = np.zeros((4, groups, max(halo, back_halo)), np.int64)
     start = 0
     for op in ops:
         for (src, dst), tiles in zip(op["pairs"], op["tiles"]):
-            for j, p in enumerate(tiles):
+            for j, p, high in tiles:
                 own_slot[src, start + j] = p - out_base[src]
                 got[dst].append((p, start + j))
+                upper[0, src, start + j] = upper[1, dst, start + j] = high
         start += op["size"]
     most = max(len(v) for v in got)
 
@@ -135,9 +160,10 @@
     for op in back_ops:
         for (src, dst), tiles in zip(op["pairs"], op["tiles"]):
             names = [p for p, _ in got[src]]
-            for j, p in enumerate(tiles):
+            for j, p, high in tiles:
                 from_got[src, start + j] = names.index(p)
                 adds[dst][p - out_base[dst]].append(start + j)
+                upper[2, src, start + j] = upper[3, dst, start + j] = high
         start += op["size"]
     n_merges = max(len(v) for v in merges)
     merges = np.array([v + [[none, none]] * (n_merges - len(v)) for v in merges], np.int64)
@@ -177,6 +203,7 @@
         ("from_got", from_got),
         ("merges", merges.reshape(groups, -1)),
         ("adds", adds.reshape(groups, -1)),
+        *((f"upper{q}", v) for q, v in enumerate(upper)),
         *((f"kind{q}", v) for q, v in enumerate(reach_tables)),
     ]
     at, total = {}, 0
@@ -317,7 +344,7 @@
     out[at + 3 * n : at + 4 * n] = jnp.where(lane < 4 * SUBL, left, right)
 
 
-def align_kernel(plan, tab, x_ref, cot_ref, after, x_out, cot_out, held):
+def align_patches_kernel(plan, tab, x_ref, after, x_out):
     def body(unit):
         align_into(
             lambda t: x_ref[rows_at(unit), tile_lanes(t)],
@@ -326,12 +353,18 @@
             plan["in_tiles"],
             tab[0],
         )
+
+    over_units(x_ref, UNIT, body)
+
+
+def align_cot_kernel(plan, tab, cot_ref, after, cot_out, held):
+    def body(unit):
         align_cot(cot_ref, unit, held, plan, tab[1])
         for j in range(plan["out_tiles"]):
             for half in range(2):
                 cot_out[j, half, rows_at(unit)] = held[j, of_half(half)]
 
-    over_units(x_ref, UNIT, body)
+    over_units(cot_ref, 2 * UNIT, body)
 
 
 def pack_kernel(plan, tab, cot_ref, after, *refs):
@@ -339,15 +372,18 @@
 
     def body(unit):
         align_cot(cot_ref, unit, held, plan, tab[1])
-        at = plan["at"]["own_slot"]
-        for out, size in zip(outs, plan["sizes"]):
-            in_turn(
-                size,
-                6,
-                lambda j, at=at: [held[tab[at + j], of_half(half)] for half in range(2)],
-                lambda j, v, out=out: keep_split(out, j, unit, v),
+        at = 0
+        for op, out in zip(plan["ops"], outs):
+            send_tiles(
+                op,
+                lambda j, at=at: [
+                    held[tab[plan["at"]["own_slot"] + at + j], of_half(half)] for half in range(2)
+                ],
+                lambda j, at=at: tab[plan["at"]["upper0"] + at + j],
+                out,
+                unit,
             )
-            at += size
+            at += op["size"]
 
     over_units(cot_ref, 2 * UNIT, body)
 
@@ -367,9 +403,36 @@
         ref[j, of_half(half, unit)] = v
 
 
-def keep_split(ref, j, unit, values):
-    for half, v in enumerate(values):
-        ref[j, half, rows_at(unit)] = v
+def send_tiles(op, load, upper, out, unit):
+    def store(j, pair):
+        for half, v in enumerate(pair):
+            out[2 * j + half, rows_at(unit)] = v
+
+    in_turn(op["full"], 6, load, store)
+    low = lane_ids() < LANES // 2
+    for j in range(op["full"], op["size"]):
+        even, odd = load(j)
+        high = upper(j) > 0
+        left = jnp.where(high, pltpu.roll(even, LANES // 2, 1), even)
+        right = jnp.where(high, odd, pltpu.roll(odd, LANES // 2, 1))
+        out[op["full"] + j, rows_at(unit)] = jnp.where(low, left, right)
+
+
+def received_tiles(op, ref, upper, keep, unit):
+    in_turn(
+        op["full"],
+        5,
+        lambda j: [ref[2 * j + half, rows_at(unit)] for half in range(2)],
+        keep,
+    )
+    low = lane_ids() < LANES // 2
+    for j in range(op["full"], op["size"]):
+        plane = ref[op["full"] + j, rows_at(unit)]
+        turned = pltpu.roll(plane, LANES // 2, 1)
+        high = upper(j) > 0
+        even = jnp.where(high, jnp.where(low, 0.0, turned), jnp.where(low, plane, 0.0))
+        odd = jnp.where(high, jnp.where(low, 0.0, plane), jnp.where(low, turned, 0.0))
+        keep(j, [even, odd])
 
 
 def partial_kernel(plan, tab, x_ref, w_ref, *refs):
@@ -384,18 +447,21 @@
             plan["most"],
             4,
             lambda n: tap_sums(tab, plan["at"]["got_taps"] + (1 + TAPS) * n + 1, held, weights),
-            lambda n, totals: keep_halves(done, n, 0, totals),
+            lambda n, totals: keep_split_all(done, n, totals),
         )
         done[plan["most"]] = jnp.zeros(done.shape[1:], jnp.float32)
-        at = plan["at"]["from_got"]
-        for out, size in zip(outs, plan["back_sizes"]):
-            in_turn(
-                size,
-                6,
-                lambda j, at=at: done[tab[at + j]],
-                lambda j, v, out=out: out.__setitem__((j, both_at(unit)), v),
+        at = 0
+        for op, out in zip(plan["back_ops"], outs):
+            send_tiles(
+                op,
+                lambda j, at=at: [
+                    done[tab[plan["at"]["from_got"] + at + j], half] for half in range(2)
+                ],
+                lambda j, at=at: tab[plan["at"]["upper2"] + at + j],
+                out,
+                unit,
             )
-            at += size
+            at += op["size"]
 
     over_units(w_ref, 2 * UNIT, body)
 
@@ -420,17 +486,25 @@
     over_units(w_ref, 2 * UNIT, body)
 
 
-def take_cots(plan, unit, cot_ref, halos, cots):
+def take_cots(plan, tab, unit, cot_ref, halos, cots):
+    own = plan["out_tiles"]
+    in_turn(
+        own,
+        5,
+        lambda j: [cot_ref[j, half, rows_at(unit)] for half in range(2)],
+        lambda j, v: keep_split_all(cots, j, v),
+    )
     at = 0
-    for ref, size in zip((cot_ref, *halos), (plan["out_tiles"], *plan["sizes"])):
-        in_turn(
-            size,
-            5,
-            lambda j, ref=ref: [ref[j, half, rows_at(unit)] for half in range(2)],
-            lambda j, v, at=at: keep_split_all(cots, at + j, v),
+    for op, ref in zip(plan["ops"], halos):
+        received_tiles(
+            op,
+            ref,
+            lambda j, at=at: tab[plan["at"]["upper1"] + at + j],
+            lambda j, v, at=at: keep_split_all(cots, own + at + j, v),
+            unit,
         )
-        at += size
-    cots[at] = jnp.zeros(cots.shape[1:], jnp.float32)
+        at += op["size"]
+    cots[own + at] = jnp.zeros(cots.shape[1:], jnp.float32)
 
 
 def keep_split_all(ref, j, values):
@@ -445,7 +519,7 @@
             cots[tab[at], half] = cots[tab[at], half] + cots[tab[at + 1], half]
 
 
-def weights_kernel(plan, tab, x_ref, cot_ref, norms, after, *refs):
+def weights_kernel(plan, tab, x_ref, cot_ref, *refs):
     halos = refs[: len(plan["sizes"])]
     sums_ref, cots, rows = refs[len(plan["sizes"]) :]
     step = pl.program_id(0)
@@ -457,7 +531,7 @@
         rows[...] = jnp.zeros_like(rows)
 
     def body(unit):
-        take_cots(plan, unit, cot_ref, halos, cots)
+        take_cots(plan, tab, unit, cot_ref, halos, cots)
         here = step * per + unit
         for half in range(2):
             bias = cots[0, half]
@@ -495,9 +569,6 @@
             return carry
 
         lax.fori_loop(0, rows.shape[1] // LANES, block, 0)
-        n_lane = lax.broadcasted_iota(jnp.int32, (1, sums_ref.shape[1]), 1)
-        extra = jnp.where(n_lane == 0, norms[0], jnp.where(n_lane == 1, norms[1], 0.0))
-        sums_ref[TAPS + 1 : TAPS + 2, :] = extra
 
 
 def patches_kernel(plan, tab, cot_ref, w_ref, after, *refs):
@@ -505,7 +576,7 @@
     grad_ref, cots, back = refs[len(plan["sizes"]) :]
 
     def body(unit):
-        take_cots(plan, unit, cot_ref, halos, cots)
+        take_cots(plan, tab, unit, cot_ref, halos, cots)
         merge_cots(plan, tab, cots)
         for q, (kind, size) in enumerate(zip(plan["kinds"], plan["kind_sizes"])):
             weights = [tap_weights(w_ref, unit, half, kind) for half in range(2)]
@@ -539,10 +610,15 @@
 
     def body(unit):
         at = 0
-        for halo, size in zip(halos, plan["back_sizes"]):
-            for j in range(size):
-                got[at + j] = halo[j, both_at(unit)]
-            at += size
+        for op, halo in zip(plan["back_ops"], halos):
+            received_tiles(
+                op,
+                halo,
+                lambda j, at=at: tab[plan["at"]["upper3"] + at + j],
+                lambda j, v, at=at: keep_halves(got, at + j, 0, v),
+                unit,
+            )
+            at += op["size"]
         got[at] = jnp.zeros(got.shape[1:], jnp.float32)
 
         def whole_sum(j):
@@ -635,7 +711,7 @@
 
 
 def update_kernel(channels, per_dev, me, sums, table, norms, cw, cb, fw, fb, sw, sb, aw, ab, hw, hu, ha, hb, hub, hab,
-                  fw_out, sw_out, w_out, a_out, hw_out, ha_out, rows_out):
+                  fw_out, sw_out, w_out, a_out, hw_out, ha_out, fb_out, sb_out, b_out, ab_out, hb_out, hab_out, ratio_out):
     padded = sums.shape[1]
     real = lax.broadcasted_iota(jnp.int32, (1, padded), 1) < channels
     wide = moments(
@@ -669,24 +745,29 @@
         cb[...], mine[TAPS : TAPS + 1, :per_dev], fb[...], sb[...], 0.0
     )
     w_new = cb[...] - rates[1] * update
-    rows_out[0:1, :per_dev] = first
-    rows_out[1:2, :per_dev] = second
-    rows_out[2:3, :per_dev] = w_new
-    rows_out[3:4, :per_dev] = keep_rate * ab[...] + (1.0 - keep_rate) * w_new
+    fb_out[...] = first.reshape(per_dev)
+    sb_out[...] = second.reshape(per_dev)
+    b_out[...] = w_new.reshape(per_dev)
+    ab_out[...] = (keep_rate * ab[...] + (1.0 - keep_rate) * w_new).reshape(per_dev)
     w_new = hb[...] - rates[3] * hub[...]
-    rows_out[4:5, :per_dev] = w_new
-    rows_out[5:6, :per_dev] = keep_rate * hab[...] + (1.0 - keep_rate) * w_new
-    rows_out[6:7, :] = ratios
-    rows_out[7:8, :] = jnp.zeros((1, LANES), jnp.float32)
+    hb_out[...] = w_new.reshape(per_dev)
+    hab_out[...] = (keep_rate * hab[...] + (1.0 - keep_rate) * w_new).reshape(per_dev)
+    ratio_out[...] = ratios[:, :4].reshape(4)
     w_new = hw[...] - rates[2] * hu[...]
     hw_out[...] = w_new
     ha_out[...] = keep_rate * ha[...] + (1.0 - keep_rate) * w_new
 
 
-def call(kernel, tables, operands, in_specs, outs, out_specs, scratch, steps, fills=False):
+def call(kernel, tables, operands, in_specs, outs, out_specs, scratch, steps, fills=False, tight=False):
     moved = sum(4 * int(np.prod(a.shape)) for a in operands) + sum(
         4 * int(np.prod(o.shape)) for o in outs
     )
+    limit = 60
+    if tight:
+        blocks = [s.block_shape for s in [*in_specs, *out_specs] if s.block_shape]
+        need = 8 * sum(int(np.prod(b)) for b in blocks)
+        need += 4 * sum(int(np.prod(v.shape)) for v in scratch)
+        limit = min(limit, max(24, need * 5 // 2**22 + 4))
     return pl.pallas_call(
         kernel,
         grid_spec=pltpu.PrefetchScalarGridSpec(
@@ -698,7 +779,7 @@
         ),
         out_shape=outs,
         compiler_params=pltpu.CompilerParams(
-            dimension_semantics=("arbitrary",), vmem_limit_bytes=60 * 1024 * 1024
+            dimension_semantics=("arbitrary",), vmem_limit_bytes=limit * 1024 * 1024
         ),
         cost_estimate=pl.CostEstimate(
             flops=1, bytes_accessed=moved if fills else 1, transcendentals=0
@@ -784,7 +865,7 @@
     local_images = class_in.shape[1]
     images = local_images * groups
     plan = make_plan(groups, images, n_in, n_out)
-    sizes, tiles, in_tiles = plan["sizes"], plan["out_tiles"], plan["in_tiles"]
+    tiles, in_tiles = plan["out_tiles"], plan["in_tiles"]
     table = lax.dynamic_index_in_dim(jnp.asarray(plan["table"]), me, 0, keepdims=False)
     per = 3
     steps = channels_in // (UNIT * per)
@@ -794,15 +875,12 @@
     rows, wide_rows = UNIT * per, 2 * UNIT * per
     x_spec = pl.BlockSpec((rows, in_lanes), lambda g, tab: (g, 0))
     cot_spec = pl.BlockSpec((wide_rows, out_lanes), lambda g, tab: (g, 0))
-    halo_specs = [
-        pl.BlockSpec((n, 2, rows, LANES), lambda g, tab: (0, 0, g, 0)) for n in sizes
-    ]
-    halo_outs = [f32(n, 2, channels_in, LANES) for n in sizes]
-    back_sizes = plan["back_sizes"]
-    back_specs = [
-        pl.BlockSpec((n, wide_rows, LANES), lambda g, tab: (0, g, 0)) for n in back_sizes
-    ]
-    back_outs = [f32(n, channels, LANES) for n in back_sizes]
+    planes = [2 * op["full"] + op["half"] for op in plan["ops"]]
+    halo_specs = [pl.BlockSpec((n, rows, LANES), lambda g, tab: (0, g, 0)) for n in planes]
+    halo_outs = [f32(n, channels_in, LANES) for n in planes]
+    planes = [2 * op["full"] + op["half"] for op in plan["back_ops"]]
+    back_specs = [pl.BlockSpec((n, rows, LANES), lambda g, tab: (0, g, 0)) for n in planes]
+    back_outs = [f32(n, channels_in, LANES) for n in planes]
     held_spec = pl.BlockSpec((in_tiles + 1, rows, LANES), lambda g, tab: (0, g, 0))
     split_spec = pl.BlockSpec((tiles, 2, rows, LANES), lambda g, tab: (0, 0, g, 0))
     own_spec = pl.BlockSpec((tiles, wide_rows, LANES), lambda g, tab: (0, g, 0))
@@ -851,17 +929,26 @@
         [cot_held],
         steps,
     )
-    x_held, cot_split = call(
-        functools.partial(align_kernel, plan),
+    x_held = call(
+        functools.partial(align_patches_kernel, plan),
         [table],
-        [x, cot, sends[0]],
-        [x_spec, cot_spec, anywhere],
-        [f32(in_tiles + 1, channels_in, LANES), f32(tiles, 2, channels_in, LANES)],
-        [held_spec, split_spec],
+        [x, sends[0]],
+        [x_spec, anywhere],
+        [f32(in_tiles + 1, channels_in, LANES)],
+        [held_spec],
+        [],
+        steps,
+    )[0]
+    cot_split = call(
+        functools.partial(align_cot_kernel, plan),
+        [table],
+        [cot, x_held],
+        [cot_spec, anywhere],
+        [f32(tiles, 2, channels_in, LANES)],
+        [split_spec],
         [cot_held],
         steps,
-        fills=True,
-    )
+    )[0]
 
     sends = list(sends)
     cot_halo = [None] * len(sends)
@@ -874,6 +961,8 @@
             got, sends = tied(got, sends)
         elif bit == rounds[1]:
             got, (x_held,) = tied(got, [x_held])
+        elif bit == rounds[-1]:
+            got, (cot_split,) = tied(got, [cot_split])
         parts = jnp.concatenate([parts, got], axis=0)
         if bit == 1:
             parts, sends = tied(parts, sends)
@@ -881,8 +970,9 @@
                 if op["near"]:
                     cot_halo[n] = lax.ppermute(sends[n], "chan", op["pairs"])
     parts, sends = tied(parts, sends)
-    if plan["ops"][0]["near"]:
-        cot_halo[0], sends = tied(cot_halo[0], sends)
+    near = [n for n, op in enumerate(plan["ops"]) if op["near"]]
+    if near:
+        cot_halo[near[0]], sends = tied(cot_halo[near[0]], sends)
     for n, op in enumerate(plan["ops"]):
         if not op["near"]:
             cot_halo[n] = lax.ppermute(sends[n], "chan", op["pairs"])
@@ -924,8 +1014,9 @@
         [held_spec, w_spec],
         back_outs,
         back_specs,
-        [pltpu.VMEM((plan["most"] + 1, 2 * UNIT, LANES), jnp.float32)],
+        [pltpu.VMEM((plan["most"] + 1, 2, UNIT, LANES), jnp.float32)],
         steps,
+        tight=True,
     )
     partials, late = list(partials), []
     pooled_halo = [None] * len(partials)
@@ -934,27 +1025,27 @@
             pooled_halo[n] = lax.ppermute(partials[n], "chan", op["pairs"])
         else:
             late.append(n)
+    grad_h = sum_over(grad_h, "dp")
+    head_t = head_weight.T
+    head_first, head_second, head_update = moments(
+        head_t, grad_h[:per_dev, :channels_in], first_head_w.T, second_head_w.T, 0.05
+    )
+    bias_first, bias_second, bias_update = moments(
+        head_bias, grad_h[:per_dev, channels_in], first_head_b, second_head_b, 0.0
+    )
+    norms = [jnp.sum(head_update**2), jnp.sum(bias_update**2)]
+
     pooled_own = call(
         functools.partial(forward_kernel, plan),
         [table],
-        [x_held, wide, partials[0]],
+        [x_held, wide, head_update],
         [held_spec, w_spec, anywhere],
         [f32(tiles, channels, LANES)],
         [own_spec],
         [],
         steps,
+        tight=True,
     )[0]
-
-    grad_h = sum_over(grad_h, "dp")
-    head_t = head_weight.T
-    head_first, head_second, head_update = moments(
-        head_t, grad_h[:per_dev, :channels_in], first_head_w.T, second_head_w.T, 0.05
-    )
-    bias_first, bias_second, bias_update = moments(
-        head_bias, grad_h[:per_dev, channels_in], first_head_b, second_head_b, 0.0
-    )
-    norms = jnp.stack([jnp.sum(head_update**2), jnp.sum(bias_update**2)])
-    norms = jnp.where(lax.axis_index("dp") == 0, norms, 0.0)
 
     waiting = [partials[n] for n in late]
     waiting, cot_halo, pooled_own, norms = lax.optimization_barrier(
@@ -966,12 +1057,13 @@
     sums = call(
         functools.partial(weights_kernel, plan),
         [table],
-        [x_held, cot_split, norms, pooled_own, *cot_halo],
-        [held_spec, split_spec, pl.BlockSpec(memory_space=pltpu.SMEM), anywhere, *halo_specs],
+        [x_held, cot_split, *cot_halo],
+        [held_spec, split_spec, *halo_specs],
         [f32(2 * SUBL, padded)],
         [whole(2 * SUBL, padded)],
         [cots_held, pltpu.VMEM((TAPS + 1, padded, LANES), jnp.float32)],
         steps,
+        tight=True,
     )[0]
     x_grad = call(
         functools.partial(patches_kernel, plan),
@@ -982,8 +1074,31 @@
         [x_spec],
         [cots_held, pltpu.VMEM((in_tiles + 1, UNIT, LANES), jnp.float32)],
         steps,
+        tight=True,
     )[0]
-    sums = sum_over(sum_over(sums, "dp"), "chan")
+    sums = sum_over(sums, "dp")
+    row = lax.broadcasted_iota(jnp.int32, sums.shape, 0)
+    lane = lax.broadcasted_iota(jnp.int32, sums.shape, 1)
+    for k, v in enumerate(norms):
+        sums = jnp.where((row == TAPS + 1) & (lane == k), v, sums)
+    pooled = call(
+        functools.partial(finish_kernel, plan),
+        [table],
+        [pooled_own, *pooled_halo],
+        [own_spec, *back_specs],
+        [f32(channels, n_out)],
+        [cot_spec],
+        [cot_held, pltpu.VMEM((plan["back_halo"] + 1, 2 * UNIT, LANES), jnp.float32)],
+        steps,
+        tight=True,
+    )[0]
+    for bit in bits_of("chan")[::-1]:
+        got = swap(sums, "chan", bit)
+        if bit == bits_of("chan")[-1]:
+            got, (x_grad,) = tied(got, [x_grad])
+        if bit == 1:
+            got, (pooled,) = tied(got, [pooled])
+        sums = sums + got
     conv_shapes = [f32(TAPS, per_dev)] * 4
     head_shapes = [f32(per_dev, channels_in)] * 2
     operands = [
@@ -1000,29 +1115,20 @@
         bias_update[None],
         average_head_b[None],
     ]
-    out_shapes = [*conv_shapes, *head_shapes, f32(SUBL, LANES)]
-    *conv_new, head_new, head_average, small_new = call(
+    specs = [whole(*v.shape) for v in operands]
+    out_shapes = [*conv_shapes, *head_shapes, *[f32(per_dev)] * 6, f32(4)]
+    *new, trust = call(
         functools.partial(update_kernel, channels, per_dev),
         [my_id],
         operands,
-        [whole(*v.shape) for v in operands],
+        specs,
         out_shapes,
         [whole(*v.shape) for v in out_shapes],
         [],
         1,
     )
 
-    pooled = call(
-        functools.partial(finish_kernel, plan),
-        [table],
-        [pooled_own, *pooled_halo],
-        [own_spec, *back_specs],
-        [f32(channels, n_out)],
-        [cot_spec],
-        [cot_held, pltpu.VMEM((plan["back_halo"] + 1, 2 * UNIT, LANES), jnp.float32)],
-        steps,
-    )[0]
-    bias_new = [small_new[k, :per_dev] for k in range(6)]
+    conv_new, (head_new, head_average), bias_new = new[:4], new[4:6], new[6:]
     return (
         pooled.T[None],
         class_out[None],
@@ -1037,7 +1143,7 @@
         bias_first,
         bias_second,
         *bias_new[4:],
-        small_new[6, :4],
+        trust,
     )
 
 

time: 145 us -> 130 us (0.90)
  waiting for transfers between devices: 36.3 us -> 25.7 us
  Pallas kernels: 69.3 us -> 63 us
  starting transfers between devices: 24.3 us -> 27.8 us
    ppermute x10, waiting for transfers between devices: 28.3 us -> 7.07 us  [swap(): return lax.ppermute(x, axis, [(k, k ^ bit) for k in range(size)])]
    ppermute x1, waiting for transfers between devices: 0.01 us -> 7.4 us  [per_device(): pooled_halo[n] = lax.ppermute(partials[n], 'chan', op['pairs'])]
    pallas_call x10 -> x11, Pallas kernels: 69.3 us -> 63 us  [call(): pl.pallas_call(kernel, grid_spec=pltpu.PrefetchScalarGridSpec(num_scalar_...]
    ppermute x2, waiting for transfers between devices: 0.01 us -> 5.28 us  [per_device(): pooled_halo[n] = lax.ppermute(v, 'chan', plan['back_ops'][n]['pairs'])]
    unnamed x22 -> x26, local copies, waits for them, and re-layouts: 1.21 us -> 3.9 us
    squeeze x2 -> x0, local copies, waits for them, and re-layouts: 2.63 us -> none  [the longest x1 1.43 us: per_device(): bias_new = [small_new[k, :per_dev] for k in range(6)]]
    ppermute x3, waiting for transfers between devices: 8 us -> 5.9 us  [per_device(): cot_halo[n] = lax.ppermute(sends[n], 'chan', op['pairs'])]
  transfers between devices with their start and end apart: 16 -> 16, of which waited for: 8 -> 8; matrix products, arithmetic and copies ran while one was open for 8% -> 5% of each run, Pallas kernels for 42% -> 46%
where the time goes in v3:
time: 130 us; the launch traced here: 129 us
  Pallas kernels  63 us (48%)
  starting transfers between devices  27.8 us (21%)
  waiting for transfers between devices  25.7 us (20%)
  other arithmetic  6.12 us (5%)
  local copies, waits for them, and re-layouts  5.44 us (4%)
    pallas_call x11, Pallas kernels, call(): pl.pallas_call(kernel, grid_spec=pltpu.PrefetchScalarGridSpec(num_scalar_...  63 us
    ppermute x10, starting transfers between devices, swap(): return lax.ppermute(x, axis, [(k, k ^ bit) for k in range(size)])  14.8 us
    ppermute x1, waiting for transfers between devices, per_device(): pooled_halo[n] = lax.ppermute(partials[n], 'chan', op['pairs'])  7.4 us
    ppermute x10, waiting for transfers between devices, swap(): return lax.ppermute(x, axis, [(k, k ^ bit) for k in range(size)])  7.07 us
    ppermute x3, waiting for transfers between devices, per_device(): cot_halo[n] = lax.ppermute(sends[n], 'chan', op['pairs'])  5.9 us
    ppermute x3, starting transfers between devices, per_device(): cot_halo[n] = lax.ppermute(sends[n], 'chan', op['pairs'])  5.35 us
    ppermute x2, waiting for transfers between devices, per_device(): pooled_halo[n] = lax.ppermute(v, 'chan', plan['back_ops'][n]['pairs'])  5.28 us
    ppermute x1, starting transfers between devices, per_device(): pooled_halo[n] = lax.ppermute(partials[n], 'chan', op['pairs'])  4.4 us
  transfers between devices with their start and end apart: 16, of which 8 were waited for; matrix products, arithmetic and copies ran while one was open for 5% of the time, Pallas kernels for 46%

profile of v3, /device:TPU:9, one launch (start us, length us, event | category | flops | bytes accessed | tf_op | source)
XLA Modules:
  0.0 128.9 jit_solution(2996069736279960049)
XLA Ops:
  0.7 1.6 %shard_map.364.after = f32[144,128]{1,0:T(8,128)} custom-call(f32[9,36]{1,0:T(8,128)} %bitcast.80, f32[1,36]{1,0:T(1,128)} %bitcast.89, f32[9,36]{1,0:T(8,128)} %bitcast.82, f32[1,36]{1,0:T(1,128)} %bitcast.91, f32[9,36]{1,0:T(8,128)} %bitcast.84, f32[1,36]{1,0:T(1,128)} %bitcast.93, f32[1,36]{1,0:T(1,128)} %bitcast.87, f32[36,144]{1,0:T(8,128)} %bitcast.73, ...), custom_call_target="tpu_custom_call" | custom-call | flops 1 | bytes 1 | tf_op jit(solution)/shard_map/pallas_call | solution.py:771
  2.3 1.2 collective-permute-start
  3.5 1.4 %constant_dynamic-slice_fusion = s32[1,926]{1,0:T(1,128)} fusion(s32[8,926]{1,0:T(8,128)} %constant.12.clone, s32[]{:T(128)S(6)} %select_n.11), kind=kLoop, calls=%fused_computation.20 | loop fusion | bytes 7412 | tf_op jit(solution)/shard_map/jit(dynamic_index_in_dim)/dynamic_slice | solution.py:869
  4.9 6.2 %shard_map.365 = (f32[11,144,128]{2,1,0:T(8,128)}, f32[10,144,128]{2,1,0:T(8,128)}, f32[15,144,128]{2,1,0:T(8,128)}) custom-call(s32[926]{0:T(1024)} %bitcast.58, f32[288,3136]{1,0:T(8,128)} %bitcast.66, f32[144,128]{1,0:T(8,128)} %shard_map.364.after), custom_call_target="tpu_custom_call" | custom-call | flops 1 | bytes 1 | tf_op jit(solution)/shard_map/pallas_call | solution.py:771
  11.0 0.0 collective-permute-done
  11.0 0.0 copy-done.5
  11.1 0.3 collective-permute-start.3
  11.3 2.3 %collective-permute-start.1 = (f32[2,144,128]{2,1,0:T(8,128)S(1)}, f32[2,144,128]{2,1,0:T(8,128)S(1)}, u32[]{:S(2)}, u32[]{:S(2)}) collective-permute-start(f32[2,144,128]{2,1,0:T(8,128)S(1)} %pad_maximum_fusion.2), channel_id=1, source_target_pairs={{0,4},{1,5},{2,6},{3,7},{4,0},{5,1},{6,2},{7,3},{8,12},{9,13},{10,... | collective-permute-start | bytes 442376 | tf_op jit(solution)/shard_map/ppermute | solution.py:804
  13.7 8.7 %shard_map.366.after.x_ref = f32[93,144,128]{2,1,0:T(8,128)} custom-call(s32[926]{0:T(1024)} %bitcast.59, f32[144,11664]{1,0:T(8,128)} %bitcast.68, f32[11,144,128]{2,1,0:T(8,128)} %get-tuple-element.85.after), custom_call_target="tpu_custom_call" | custom-call | flops 1 | bytes 1 | tf_op jit(solution)/shard_map/pallas_call | solution.py:771
  22.3 0.0 collective-permute-done.1
  22.3 0.0 copy-start.12
  22.3 0.2 collective-permute-start.2
  22.6 6.6 %shard_map.367.cot_ref = f32[25,2,144,128]{3,2,1,0:T(8,128)} custom-call(s32[926]{0:T(1024)} %bitcast.60, f32[288,3136]{1,0:T(8,128)} %bitcast.67, f32[93,144,128]{2,1,0:T(8,128)} %shard_map.366.after.x_ref), custom_call_target="tpu_custom_call" | custom-call | flops 1 | bytes 1 | tf_op jit(solution)/shard_map/pallas_call | solution.py:771
  29.1 0.3 collective-permute-done.2
  29.4 0.9 pad_maximum_fusion.parts
  30.3 0.0 collective-permute-done.3.refs_0_
  30.3 0.0 copy-done.12
  30.3 3.8 %collective-permute-start.5 = (f32[15,144,128]{2,1,0:T(8,128)S(1)}, f32[15,144,128]{2,1,0:T(8,128)S(1)}, u32[]{:S(2)}, u32[]{:S(2)}) collective-permute-start(f32[15,144,128]{2,1,0:T(8,128)S(1)} %copy-done.12), channel_id=1, source_target_pairs={{3,4},{4,3},{1,2},{2,1},{5,6},{6,5},{11,12},{12,11},{9,10},{10,9},... | collective-permute-start | bytes 3317768 | tf_op jit(solution)/shard_map/ppermute | solution.py:978
  34.1 1.3 %collective-permute-start.4 = (f32[10,144,128]{2,1,0:T(8,128)}, f32[10,144,128]{2,1,0:T(8,128)S(1)}, u32[]{:S(2)}, u32[]{:S(2)}) collective-permute-start(f32[10,144,128]{2,1,0:T(8,128)} %get-tuple-element.86), channel_id=1, source_target_pairs={{3,2},{4,5},{1,0},{6,7},{11,10},{12,13},{9,8},{14,15},{19,18},{20,... | collective-permute-start | bytes 2211848 | tf_op jit(solution)/shard_map/ppermute | solution.py:971
  35.4 0.0 copy-start.4
  35.4 2.9 %shard_map.368 = (f32[288,128]{1,0:T(8,128)}, f32[128,384]{1,0:T(8,128)}, f32[16,288]{1,0:T(8,128)}, f32[16,144]{1,0:T(8,128)}, f32[40,256]{1,0:T(8,128)}, /*index=5*/f32[8,128]{1,0:T(8,128)}) custom-call(s32[1]{0:T(128)} %bitcast.16.me, f32[8,144,128]{2,1,0:T(8,128)} %pad_maximum_fusion.parts, f32[16,144]{1,0:T(8,128)} %bitcast.78, f32[16,288]{1,0:T(8,128)} %bitcast.76, ...), custom_call_target="tpu_custom_call" | custom-call | flops 1 | bytes 1 | tf_op jit(solution)/shard_map/pallas_call | solution.py:771
  38.3 0.0 copy-start.8
  38.3 1.3 collective-permute-start.6
  39.6 2.1 %collective-permute-done.6 = f32[40,256]{1,0:T(8,128)S(1)} collective-permute-done((f32[40,256]{1,0:T(8,128)}, f32[40,256]{1,0:T(8,128)S(1)}, u32[]{:S(2)}, u32[]{:S(2)}) %collective-permute-start.6) | collective-permute-done | bytes 40992 | tf_op jit(solution)/shard_map/ppermute | solution.py:804
  41.8 0.8 add.56
  42.5 2.9 %collective-permute-start.7 = (f32[40,256]{1,0:T(8,128)S(1)}, f32[40,256]{1,0:T(8,128)S(1)}, u32[]{:S(2)}, u32[]{:S(2)}) collective-permute-start(f32[40,256]{1,0:T(8,128)S(1)} %add.56), channel_id=1, source_target_pairs={{0,8},{8,0},{16,24},{24,16},{1,9},{9,1},{17,25},{25,17},{2,10},{10... | collective-permute-start | bytes 122888 | tf_op jit(solution)/shard_map/ppermute | solution.py:804
  45.5 0.0 copy-done.4
  45.5 2.9 %copy-done = f32[93,144,128]{2,1,0:T(8,128)S(1)} copy-done((f32[93,144,128]{2,1,0:T(8,128)S(1)}, f32[93,144,128]{2,1,0:T(8,128)}, u32[]{:S(2)}) %copy-start) | copy-done | bytes 6856728
  48.4 0.9 copy-done.2
  49.3 5.8 %shard_map.369 = (f32[21,144,128]{2,1,0:T(8,128)S(1)}, f32[15,144,128]{2,1,0:T(8,128)S(1)}, f32[11,144,128]{2,1,0:T(8,128)S(1)}) custom-call(s32[926]{0:T(1024)S(1)} %bitcast.61, f32[93,144,128]{2,1,0:T(8,128)S(1)} %copy-done, f32[288,128]{1,0:T(8,128)S(1)} %copy-done.2), custom_call_target="tpu_custom_call" | custom-call | flops 1 | bytes 1 | tf_op jit(solution)/shard_map/pallas_call | solution.py:771
  55.1 4.4 %collective-permute-start.13 = (f32[21,144,128]{2,1,0:T(8,128)S(1)}, f32[21,144,128]{2,1,0:T(8,128)S(1)}, u32[]{:S(2)}, u32[]{:S(2)}) collective-permute-start(f32[21,144,128]{2,1,0:T(8,128)S(1)} %get-tuple-element.104), channel_id=1, source_target_pairs={{2,3},{5,4},{0,1},{7,6},{10,11},{13,12},{8,9},{15,14},{18,19},{21,... | collective-permute-start | bytes 4644872 | tf_op jit(solution)/shard_map/ppermute | solution.py:1025
  59.5 0.0 collective-permute-done.7
  59.6 0.0 copy-done.6
  59.6 0.0 copy-done.7
  59.6 0.0 copy-done.8
  59.6 1.3 multiply_reduce_fusion
  60.9 7.1 %shard_map.370.own_ref = f32[25,288,128]{2,1,0:T(8,128)S(1)} custom-call(s32[926]{0:T(1024)S(1)} %bitcast.62, f32[93,144,128]{2,1,0:T(8,128)S(1)} %copy-done, f32[288,128]{1,0:T(8,128)S(1)} %copy-done.2, f32[36,144]{1,0:T(8,128)S(1)} %get-tuple-element.132.after.hu), custom_call_target="tpu_custom_call" | custom-call | flops 1 | bytes 1 | tf_op jit(solution)/shard_map/pallas_call | solution.py:771
  68.0 0.0 copy-done.3
  68.0 0.2 slice_reduce_fusion
  68.2 0.0 copy-done.9
  68.2 1.1 multiply_reduce_fusion.1
  69.3 5.9 %collective-permute-done.4.refs_1_ = f32[10,144,128]{2,1,0:T(8,128)S(1)} collective-permute-done((f32[10,144,128]{2,1,0:T(8,128)}, f32[10,144,128]{2,1,0:T(8,128)S(1)}, u32[]{:S(2)}, u32[]{:S(2)}) %collective-permute-start.4) | collective-permute-done | bytes 737312 | tf_op jit(solution)/shard_map/ppermute | solution.py:971
  75.2 0.0 collective-permute-done.5.refs_2_
  75.2 1.9 %collective-permute-start.14 = (f32[15,144,128]{2,1,0:T(8,128)S(1)}, f32[15,144,128]{2,1,0:T(8,128)S(1)}, u32[]{:S(2)}, u32[]{:S(2)}) collective-permute-start(f32[15,144,128]{2,1,0:T(8,128)S(1)} %get-tuple-element.105), channel_id=1, source_target_pairs={{3,4},{4,3},{1,2},{2,1},{5,6},{6,5},{11,12},{12,11},{9,10},{10,9},... | collective-permute-start | bytes 3317768 | tf_op jit(solution)/shard_map/ppermute | solution.py:1055
  77.1 1.3 %collective-permute-start.15 = (f32[11,144,128]{2,1,0:T(8,128)S(1)}, f32[11,144,128]{2,1,0:T(8,128)S(1)}, u32[]{:S(2)}, u32[]{:S(2)}) collective-permute-start(f32[11,144,128]{2,1,0:T(8,128)S(1)} %get-tuple-element.106), channel_id=1, source_target_pairs={{1,0},{6,7},{3,2},{4,5},{9,8},{14,15},{11,10},{12,13},{17,16},{22,... | collective-permute-start | bytes 2433032 | tf_op jit(solution)/shard_map/ppermute | solution.py:1055
  78.4 6.3 %shard_map.371.after = f32[16,384]{1,0:T(8,128)S(1)} custom-call(s32[926]{0:T(1024)S(1)} %bitcast.63, f32[93,144,128]{2,1,0:T(8,128)S(1)} %copy-done, f32[25,2,144,128]{3,2,1,0:T(8,128)S(1)} %copy-done.1, f32[11,144,128]{2,1,0:T(8,128)S(1)} %collective-permute-done.3.refs_0_, f32[10,144,128]{2,1,0:T(8,128)S(1)} %collective-permute-done.4.refs_1_, ...), custom_call_target="tpu_custom_call" | custom-call | flops 1 | bytes 1 | tf_op jit(solution)/shard_map/pallas_call | solution.py:771
  84.8 1.3 collective-permute-start.8
  86.1 1.8 %collective-permute-done.8 = f32[16,384]{1,0:T(8,128)S(1)} collective-permute-done((f32[16,384]{1,0:T(8,128)S(1)}, f32[16,384]{1,0:T(8,128)S(1)}, u32[]{:S(2)}, u32[]{:S(2)}) %collective-permute-start.8) | collective-permute-done | bytes 24608 | tf_op jit(solution)/shard_map/ppermute | solution.py:804
  87.8 1.3 %collective-permute-start.9 = (f32[16,384]{1,0:T(8,128)S(1)}, f32[16,384]{1,0:T(8,128)S(1)}, u32[]{:S(2)}, u32[]{:S(2)}) collective-permute-start(f32[16,384]{1,0:T(8,128)S(1)} %add.68), channel_id=1, source_target_pairs={{0,8},{8,0},{16,24},{24,16},{1,9},{9,1},{17,25},{25,17},{2,10},{10... | collective-permute-start | bytes 73736 | tf_op jit(solution)/shard_map/ppermute | solution.py:804
  89.2 0.8 collective-permute-done.9
  90.0 1.4 %select_select_fusion = f32[16,384]{1,0:T(8,128)S(1)} fusion(f32[16,384]{1,0:T(8,128)S(1)} %add.68, f32[16,384]{1,0:T(8,128)S(1)} %collective-permute-done.9, f32[]{:T(128)} %get-tuple-element.97, f32[]{:T(128)} %get-tuple-element.96, pred[384]{0:T(512)(128)(4,1)S(1)} %get-tuple-element.135, pred[384]{0:T(512)(128)(4,1)S(1)} %get-tuple-element.136, ...), kind=kLoop, calls=%fused_computation.8 | loop fusion | flops 30720 | bytes 74520 | tf_op jit(solution)/shard_map/jit(_where)/select_n | solution.py:1083
  91.4 3.2 %collective-permute-start.10 = (f32[16,384]{1,0:T(8,128)S(1)}, f32[16,384]{1,0:T(8,128)S(1)}, u32[]{:S(2)}, u32[]{:S(2)}) collective-permute-start(f32[16,384]{1,0:T(8,128)S(1)} %select_select_fusion), channel_id=1, source_target_pairs={{0,4},{1,5},{2,6},{3,7},{4,0},{5,1},{6,2},{7,3},{8,12},{9,13},{10,... | collective-permute-start | bytes 73736 | tf_op jit(solution)/shard_map/ppermute | solution.py:804
  94.6 11.3 %shard_map.372 = f32[144,11664]{1,0:T(8,128)} custom-call(s32[926]{0:T(1024)S(1)} %bitcast.64, f32[25,2,144,128]{3,2,1,0:T(8,128)S(1)} %copy-done.1, f32[288,128]{1,0:T(8,128)S(1)} %copy-done.2, f32[16,384]{1,0:T(8,128)S(1)} %shard_map.371.after, f32[11,144,128]{2,1,0:T(8,128)S(1)} %collective-permute-done.3.refs_0_, ...), custom_call_target="tpu_custom_call" | custom-call | flops 1 | bytes 1 | tf_op jit(solution)/shard_map/pallas_call | solution.py:771
  106.0 0.0 collective-permute-done.10
  106.0 1.0 collective-permute-start.11
  106.9 2.1 %collective-permute-done.11 = f32[16,384]{1,0:T(8,128)S(1)} collective-permute-done((f32[16,384]{1,0:T(8,128)S(1)}, f32[16,384]{1,0:T(8,128)S(1)}, u32[]{:S(2)}, u32[]{:S(2)}) %collective-permute-start.11) | collective-permute-done | bytes 24608 | tf_op jit(solution)/shard_map/ppermute | solution.py:804
  109.0 0.0 collective-permute-start.12
  109.0 7.4 %collective-permute-done.13.refs_0_ = f32[21,144,128]{2,1,0:T(8,128)S(1)} collective-permute-done((f32[21,144,128]{2,1,0:T(8,128)S(1)}, f32[21,144,128]{2,1,0:T(8,128)S(1)}, u32[]{:S(2)}, u32[]{:S(2)}) %collective-permute-start.13) | collective-permute-done | bytes 1548320 | tf_op jit(solution)/shard_map/ppermute | solution.py:1025
  116.4 5.3 %collective-permute-done.15.refs_2_ = f32[11,144,128]{2,1,0:T(8,128)S(1)} collective-permute-done((f32[11,144,128]{2,1,0:T(8,128)S(1)}, f32[11,144,128]{2,1,0:T(8,128)S(1)}, u32[]{:S(2)}, u32[]{:S(2)}) %collective-permute-start.15) | collective-permute-done | bytes 811040 | tf_op jit(solution)/shard_map/ppermute | solution.py:1055
  121.7 0.0 collective-permute-done.14.refs_1_
  121.7 4.6 %shard_map.373 = f32[288,3136]{1,0:T(8,128)} custom-call(s32[926]{0:T(1024)S(1)} %bitcast.65, f32[25,288,128]{2,1,0:T(8,128)S(1)} %shard_map.370.own_ref, f32[21,144,128]{2,1,0:T(8,128)S(1)} %collective-permute-done.13.refs_0_, f32[15,144,128]{2,1,0:T(8,128)S(1)} %collective-permute-done.14.refs_1_, f32[11,144,128]{2,1,0:T(8,128)S(1)} %collective-permute-done.15.refs_2_), custom_call_target="tpu_custom_call" | custom-call | flops 1 | bytes 1 | tf_op jit(solution)/shard_map/pallas_call | solution.py:771
  126.3 0.0 collective-permute-done.12
  126.3 0.6 add.72.sums
  126.9 2.0 %shard_map.374 = (f32[9,36]{1,0:T(8,128)}, f32[9,36]{1,0:T(8,128)}, f32[9,36]{1,0:T(8,128)}, f32[9,36]{1,0:T(8,128)}, f32[36,144]{1,0:T(8,128)}, /*index=5*/f32[...) custom-call(s32[1]{0:T(128)} %bitcast.16.me, ...), custom_call_target="tpu_custom_call" | custom-call | flops 1 | bytes 1 | tf_op jit(solution)/shard_map/pallas_call | solution.py:771
  (21 shorter events, 0.1 us)
Async XLA Ops:
  2.3 8.8 %copy-start.5 = (f32[144,128]{1,0:T(8,128)S(1)}, f32[144,128]{1,0:T(8,128)}, u32[]{:S(2)}) copy-start(f32[144,128]{1,0:T(8,128)} %shard_map.364.after) | copy-start | bytes 221188
  2.3 8.8 %collective-permute-start = (f32[1,144,128]{2,1,0:T(8,128)}, f32[1,144,128]{2,1,0:T(8,128)S(1)}, u32[]{:S(2)}, u32[]{:S(2)}) collective-permute-start(f32[1,144,128]{2,1,0:T(8,128)} %bitcast.71), channel_id=1, source_target_pairs={{0,1},{1,0},{2,3},{3,2},{4,5},{5,4},{6,7},{7,6},{8,9},{9,8},{10,11... | collective-permute-start | bytes 221192 | tf_op jit(solution)/shard_map/ppermute | solution.py:804
  11.1 19.3 %collective-permute-start.3 = (f32[11,144,128]{2,1,0:T(8,128)}, f32[11,144,128]{2,1,0:T(8,128)S(1)}, u32[]{:S(2)}, u32[]{:S(2)}) collective-permute-start(f32[11,144,128]{2,1,0:T(8,128)} %get-tuple-element.85.after), channel_id=1, source_target_pairs={{0,1},{1,0},{3,2},{4,5},{6,7},{7,6},{2,3},{5,4},{8,9},{9,8},{11,10... | collective-permute-start | bytes 2433032 | tf_op jit(solution)/shard_map/ppermute | solution.py:971
  11.3 11.0 %collective-permute-start.1 = (f32[2,144,128]{2,1,0:T(8,128)S(1)}, f32[2,144,128]{2,1,0:T(8,128)S(1)}, u32[]{:S(2)}, u32[]{:S(2)}) collective-permute-start(f32[2,144,128]{2,1,0:T(8,128)S(1)} %pad_maximum_fusion.2), channel_id=1, source_target_pairs={{0,4},{1,5},{2,6},{3,7},{4,0},{5,1},{6,2},{7,3},{8,12},{9,13},{10,... | collective-permute-start | bytes 442376 | tf_op jit(solution)/shard_map/ppermute | solution.py:804
  22.3 8.0 %copy-start.12 = (f32[15,144,128]{2,1,0:T(8,128)S(1)}, f32[15,144,128]{2,1,0:T(8,128)}, u32[]{:S(2)}) copy-start(f32[15,144,128]{2,1,0:T(8,128)} %get-tuple-element.94) | copy-start | bytes 3317764
  22.3 7.0 %collective-permute-start.2 = (f32[4,144,128]{2,1,0:T(8,128)S(1)}, f32[4,144,128]{2,1,0:T(8,128)S(1)}, u32[]{:S(2)}, u32[]{:S(2)}) collective-permute-start(f32[4,144,128]{2,1,0:T(8,128)S(1)} %pad_maximum_fusion.1), channel_id=1, source_target_pairs={{0,2},{1,3},{2,0},{3,1},{4,6},{5,7},{6,4},{7,5},{8,10},{9,11},{10,... | collective-permute-start | bytes 884744 | tf_op jit(solution)/shard_map/ppermute | solution.py:804
  30.3 44.9 %collective-permute-start.5 = (f32[15,144,128]{2,1,0:T(8,128)S(1)}, f32[15,144,128]{2,1,0:T(8,128)S(1)}, u32[]{:S(2)}, u32[]{:S(2)}) collective-permute-start(f32[15,144,128]{2,1,0:T(8,128)S(1)} %copy-done.12), channel_id=1, source_target_pairs={{3,4},{4,3},{1,2},{2,1},{5,6},{6,5},{11,12},{12,11},{9,10},{10,9},... | collective-permute-start | bytes 3317768 | tf_op jit(solution)/shard_map/ppermute | solution.py:978
  34.1 41.1 %collective-permute-start.4 = (f32[10,144,128]{2,1,0:T(8,128)}, f32[10,144,128]{2,1,0:T(8,128)S(1)}, u32[]{:S(2)}, u32[]{:S(2)}) collective-permute-start(f32[10,144,128]{2,1,0:T(8,128)} %get-tuple-element.86), channel_id=1, source_target_pairs={{3,2},{4,5},{1,0},{6,7},{11,10},{12,13},{9,8},{14,15},{19,18},{20,... | collective-permute-start | bytes 2211848 | tf_op jit(solution)/shard_map/ppermute | solution.py:971
  35.4 10.1 %copy-start.4 = (s32[1,926]{1,0:T(1,128)S(1)}, s32[1,926]{1,0:T(1,128)}, u32[]{:S(2)}) copy-start(s32[1,926]{1,0:T(1,128)} %constant_dynamic-slice_fusion) | copy-start | bytes 11116
  38.3 21.3 %copy-start.6 = (f32[144,36]{0,1:T(8,128)S(1)}, f32[144,36]{0,1:T(8,128)}, u32[]{:S(2)}) copy-start(f32[144,36]{0,1:T(8,128)} %param.25) | copy-start | bytes 62212
  38.3 21.3 %copy-start.7 = (f32[144,36]{0,1:T(8,128)S(1)}, f32[144,36]{0,1:T(8,128)}, u32[]{:S(2)}) copy-start(f32[144,36]{0,1:T(8,128)} %param.33) | copy-start | bytes 62212
  38.3 21.3 %copy-start.8 = (f32[144,36]{0,1:T(8,128)S(1)}, f32[144,36]{0,1:T(8,128)}, u32[]{:S(2)}) copy-start(f32[144,36]{0,1:T(8,128)} %param.29) | copy-start | bytes 62212
  38.3 3.4 %collective-permute-start.6 = (f32[40,256]{1,0:T(8,128)}, f32[40,256]{1,0:T(8,128)S(1)}, u32[]{:S(2)}, u32[]{:S(2)}) collective-permute-start(f32[40,256]{1,0:T(8,128)} %get-tuple-element.95), channel_id=1, source_target_pairs={{0,16},{8,24},{16,0},{24,8},{1,17},{9,25},{17,1},{25,9},{2,18},{10... | collective-permute-start | bytes 122888 | tf_op jit(solution)/shard_map/ppermute | solution.py:804
  42.5 17.0 %collective-permute-start.7 = (f32[40,256]{1,0:T(8,128)S(1)}, f32[40,256]{1,0:T(8,128)S(1)}, u32[]{:S(2)}, u32[]{:S(2)}) collective-permute-start(f32[40,256]{1,0:T(8,128)S(1)} %add.56), channel_id=1, source_target_pairs={{0,8},{8,0},{16,24},{24,16},{1,9},{9,1},{17,25},{25,17},{2,10},{10... | collective-permute-start | bytes 122888 | tf_op jit(solution)/shard_map/ppermute | solution.py:804
  45.5 2.9 %copy-start = (f32[93,144,128]{2,1,0:T(8,128)S(1)}, f32[93,144,128]{2,1,0:T(8,128)}, u32[]{:S(2)}) copy-start(f32[93,144,128]{2,1,0:T(8,128)} %shard_map.366.after.x_ref) | copy-start | bytes 20570116
  48.4 0.9 copy-start.2
  55.1 61.3 %collective-permute-start.13 = (f32[21,144,128]{2,1,0:T(8,128)S(1)}, f32[21,144,128]{2,1,0:T(8,128)S(1)}, u32[]{:S(2)}, u32[]{:S(2)}) collective-permute-start(f32[21,144,128]{2,1,0:T(8,128)S(1)} %get-tuple-element.104), channel_id=1, source_target_pairs={{2,3},{5,4},{0,1},{7,6},{10,11},{13,12},{8,9},{15,14},{18,19},{21,... | collective-permute-start | bytes 4644872 | tf_op jit(solution)/shard_map/ppermute | solution.py:1025
  60.9 7.1 %copy-start.3 = (f32[36,144]{1,0:T(8,128)}, f32[36,144]{1,0:T(8,128)S(1)}, u32[]{:S(2)}) copy-start(f32[36,144]{1,0:T(8,128)S(1)} %get-tuple-element.132.after.hu) | copy-start | bytes 62212
  60.9 7.3 %copy-start.9 = (f32[36]{0:T(128)S(1)}, f32[36]{0:T(128)}, u32[]{:S(2)}) copy-start(f32[36]{0:T(128)} %param.26) | copy-start | bytes 436
  60.9 7.3 %copy-start.10 = (f32[36]{0:T(128)S(1)}, f32[36]{0:T(128)}, u32[]{:S(2)}) copy-start(f32[36]{0:T(128)} %param.30) | copy-start | bytes 436
  60.9 7.3 %copy-start.11 = (f32[36]{0:T(128)S(1)}, f32[36]{0:T(128)}, u32[]{:S(2)}) copy-start(f32[36]{0:T(128)} %param.34) | copy-start | bytes 436
  60.9 17.6 %copy-start.1 = (f32[25,2,144,128]{3,2,1,0:T(8,128)S(1)}, f32[25,2,144,128]{3,2,1,0:T(8,128)}, u32[]{:S(2)}) copy-start(f32[25,2,144,128]{3,2,1,0:T(8,128)} %shard_map.367.cot_ref) | copy-start | bytes 11059204
  75.2 46.5 %collective-permute-start.14 = (f32[15,144,128]{2,1,0:T(8,128)S(1)}, f32[15,144,128]{2,1,0:T(8,128)S(1)}, u32[]{:S(2)}, u32[]{:S(2)}) collective-permute-start(f32[15,144,128]{2,1,0:T(8,128)S(1)} %get-tuple-element.105), channel_id=1, source_target_pairs={{3,4},{4,3},{1,2},{2,1},{5,6},{6,5},{11,12},{12,11},{9,10},{10,9},... | collective-permute-start | bytes 3317768 | tf_op jit(solution)/shard_map/ppermute | solution.py:1055
  77.1 44.6 %collective-permute-start.15 = (f32[11,144,128]{2,1,0:T(8,128)S(1)}, f32[11,144,128]{2,1,0:T(8,128)S(1)}, u32[]{:S(2)}, u32[]{:S(2)}) collective-permute-start(f32[11,144,128]{2,1,0:T(8,128)S(1)} %get-tuple-element.106), channel_id=1, source_target_pairs={{1,0},{6,7},{3,2},{4,5},{9,8},{14,15},{11,10},{12,13},{17,16},{22,... | collective-permute-start | bytes 2433032 | tf_op jit(solution)/shard_map/ppermute | solution.py:1055
  84.8 3.0 %collective-permute-start.8 = (f32[16,384]{1,0:T(8,128)S(1)}, f32[16,384]{1,0:T(8,128)S(1)}, u32[]{:S(2)}, u32[]{:S(2)}) collective-permute-start(f32[16,384]{1,0:T(8,128)S(1)} %shard_map.371.after), channel_id=1, source_target_pairs={{0,16},{8,24},{16,0},{24,8},{1,17},{9,25},{17,1},{25,9},{2,18},{10... | collective-permute-start | bytes 73736 | tf_op jit(solution)/shard_map/ppermute | solution.py:804
  87.8 2.2 %collective-permute-start.9 = (f32[16,384]{1,0:T(8,128)S(1)}, f32[16,384]{1,0:T(8,128)S(1)}, u32[]{:S(2)}, u32[]{:S(2)}) collective-permute-start(f32[16,384]{1,0:T(8,128)S(1)} %add.68), channel_id=1, source_target_pairs={{0,8},{8,0},{16,24},{24,16},{1,9},{9,1},{17,25},{25,17},{2,10},{10... | collective-permute-start | bytes 73736 | tf_op jit(solution)/shard_map/ppermute | solution.py:804
  91.4 14.6 %collective-permute-start.10 = (f32[16,384]{1,0:T(8,128)S(1)}, f32[16,384]{1,0:T(8,128)S(1)}, u32[]{:S(2)}, u32[]{:S(2)}) collective-permute-start(f32[16,384]{1,0:T(8,128)S(1)} %select_select_fusion), channel_id=1, source_target_pairs={{0,4},{1,5},{2,6},{3,7},{4,0},{5,1},{6,2},{7,3},{8,12},{9,13},{10,... | collective-permute-start | bytes 73736 | tf_op jit(solution)/shard_map/ppermute | solution.py:804
  106.0 3.0 %collective-permute-start.11 = (f32[16,384]{1,0:T(8,128)S(1)}, f32[16,384]{1,0:T(8,128)S(1)}, u32[]{:S(2)}, u32[]{:S(2)}) collective-permute-start(f32[16,384]{1,0:T(8,128)S(1)} %add.70), channel_id=1, source_target_pairs={{0,2},{1,3},{2,0},{3,1},{4,6},{5,7},{6,4},{7,5},{8,10},{9,11},{10,... | collective-permute-start | bytes 73736 | tf_op jit(solution)/shard_map/ppermute | solution.py:804
  109.0 17.3 %collective-permute-start.12 = (f32[16,384]{1,0:T(8,128)S(1)}, f32[16,384]{1,0:T(8,128)S(1)}, u32[]{:S(2)}, u32[]{:S(2)}) collective-permute-start(f32[16,384]{1,0:T(8,128)S(1)} %add.71), channel_id=1, source_target_pairs={{0,1},{1,0},{2,3},{3,2},{4,5},{5,4},{6,7},{7,6},{8,9},{9,8},{10,11... | collective-permute-start | bytes 73736 | tf_op jit(solution)/shard_map/ppermute | solution.py:804

commit v4 on v3

--- a/solution.py
+++ b/solution.py
@@ -25,31 +25,73 @@
 highest = lax.Precision.HIGHEST
 
 
+def sized(parts):
+    full = max(len(f) for _, (f, _) in parts)
+    half = max(len(h) for _, (_, h) in parts)
+    return {
+        "full": full,
+        "half": half,
+        "size": full + half,
+        "parts": parts,
+        "pairs": [pair for pair, _ in parts],
+        "tiles": [
+            [(j, *v) for j, v in enumerate(f)] + [(full + j, *v) for j, v in enumerate(h)]
+            for _, (f, h) in parts
+        ],
+        "near": all(src ^ dst == 1 for (src, dst), _ in parts),
+    }
+
+
+def halves(message):
+    return 2 * len(message[0]) + len(message[1])
+
+
+def free_in(parts, pair):
+    return all(pair[0] != s and pair[1] != d for (s, d), _ in parts)
+
+
 def grouped(messages, spare):
-    ops = []
-    for (src, dst), (full, half) in sorted(
-        messages, key=lambda kv: (-2 * len(kv[1][0]) - len(kv[1][1]), kv[0])
-    ):
-        for op in ops:
-            waste = op["full"] + op["half"] / 2 - len(full) - len(half) / 2
+    groups = []
+    for pair, message in sorted(messages, key=lambda kv: (-halves(kv[1]), kv[0])):
+        for parts in groups:
+            first = parts[0][1]
             if (
-                len(full) <= op["full"]
-                and len(half) <= op["half"]
-                and waste <= spare
-                and all(src != s and dst != d for s, d in op["pairs"])
+                len(message[0]) <= len(first[0])
+                and len(message[1]) <= len(first[1])
+                and halves(first) - halves(message) <= 2 * spare
+                and free_in(parts, pair)
             ):
                 break
         else:
-            op = {"full": len(full), "half": len(half), "pairs": [], "tiles": []}
-            op["size"] = op["full"] + op["half"]
-            ops.append(op)
-        op["pairs"].append((src, dst))
-        op["tiles"].append(
-            [(j, *v) for j, v in enumerate(full)]
-            + [(op["full"] + j, *v) for j, v in enumerate(half)]
-        )
+            parts = []
+            groups.append(parts)
+        parts.append((pair, message))
+    return [sized(parts) for parts in groups]
+
+
+def loads(ops, groups):
+    got = np.zeros(groups, np.int64)
     for op in ops:
-        op["near"] = all(src ^ dst == 1 for src, dst in op["pairs"])
+        for _, dst in op["pairs"]:
+            got[dst] += 2 * op["full"] + op["half"]
+    return got
+
+
+def joined(ops, others, groups):
+    for n in range(1, len(ops)):
+        for m in range(n):
+            if not (ops[n]["near"] and ops[m]["near"]):
+                continue
+            for pair, message in list(ops[n]["parts"]):
+                got = loads(ops + others, groups)
+                more = halves(ops[m]["parts"][0][1]) - 2 * ops[n]["full"] - ops[n]["half"]
+                if (
+                    len(ops[n]["parts"]) > 1
+                    and free_in(ops[m]["parts"], pair)
+                    and got[pair[1]] + more < 0.9 * max(got)
+                ):
+                    ops[n] = sized([v for v in ops[n]["parts"] if v[0] != pair])
+                    ops[m] = sized(ops[m]["parts"] + [(pair, message)])
     return ops
 
 
@@ -97,6 +139,7 @@
     ops = grouped(begin, even) + grouped(rest, 2)
     ops += grouped([(p, t) for p, t in wanted.items() if p[0] ^ p[1] != 1], 2)
     back_ops = grouped([((d, s), t) for (s, d), t in wanted.items()], 2)
+    back_ops = joined(back_ops, ops, groups)
     longest = max(op["size"] for op in back_ops)
     for op in back_ops:
         op["early"] = op["near"] and 4 * op["size"] > 3 * longest
@@ -929,24 +972,24 @@
         [cot_held],
         steps,
     )
+    cot_split = call(
+        functools.partial(align_cot_kernel, plan),
+        [table],
+        [cot, sends[0]],
+        [cot_spec, anywhere],
+        [f32(tiles, 2, channels_in, LANES)],
+        [split_spec],
+        [cot_held],
+        steps,
+    )[0]
     x_held = call(
         functools.partial(align_patches_kernel, plan),
         [table],
-        [x, sends[0]],
+        [x, cot_split],
         [x_spec, anywhere],
         [f32(in_tiles + 1, channels_in, LANES)],
         [held_spec],
         [],
-        steps,
-    )[0]
-    cot_split = call(
-        functools.partial(align_cot_kernel, plan),
-        [table],
-        [cot, x_held],
-        [cot_spec, anywhere],
-        [f32(tiles, 2, channels_in, LANES)],
-        [split_spec],
-        [cot_held],
         steps,
     )[0]
 
@@ -959,9 +1002,9 @@
         got = swap(parts, "chan", bit)
         if bit == 1:
             got, sends = tied(got, sends)
+        elif bit == rounds[-1]:
+            got, (x_held,) = tied(got, [x_held])
         elif bit == rounds[1]:
-            got, (x_held,) = tied(got, [x_held])
-        elif bit == rounds[-1]:
             got, (cot_split,) = tied(got, [cot_split])
         parts = jnp.concatenate([parts, got], axis=0)
         if bit == 1:

time: 130 us -> 126 us (0.969)
  waiting for transfers between devices: 25.7 us -> 18.7 us
  starting transfers between devices: 27.8 us -> 29.5 us
    ppermute x2, waiting for transfers between devices: 5.28 us -> 0.01 us  [per_device(): pooled_halo[n] = lax.ppermute(v, 'chan', plan['back_ops'][n]['pairs'])]
    unnamed x26 -> x30, local copies, waits for them, and re-layouts: 3.9 us -> 3.91 us
  transfers between devices with their start and end apart: 16 -> 16, of which waited for: 8 -> 7; matrix products, arithmetic and copies ran while one was open for 5% -> 6% of each run, Pallas kernels for 46% -> 48%
where the time goes in v4:
time: 126 us; the launch traced here: 124 us
  Pallas kernels  63 us (50%)
  starting transfers between devices  29.5 us (23%)
  waiting for transfers between devices  18.7 us (15%)
  other arithmetic  6.12 us (5%)
  local copies, waits for them, and re-layouts  5.45 us (4%)
    pallas_call x11, Pallas kernels, call(): pl.pallas_call(kernel, grid_spec=pltpu.PrefetchScalarGridSpec(num_scalar_...  63 us
    ppermute x10, starting transfers between devices, swap(): return lax.ppermute(x, axis, [(k, k ^ bit) for k in range(size)])  16.1 us
    ppermute x10, waiting for transfers between devices, swap(): return lax.ppermute(x, axis, [(k, k ^ bit) for k in range(size)])  6.59 us
    ppermute x1, waiting for transfers between devices, per_device(): pooled_halo[n] = lax.ppermute(partials[n], 'chan', op['pairs'])  6.53 us
    ppermute x3, starting transfers between devices, per_device(): cot_halo[n] = lax.ppermute(sends[n], 'chan', op['pairs'])  5.87 us
    ppermute x3, waiting for transfers between devices, per_device(): cot_halo[n] = lax.ppermute(sends[n], 'chan', op['pairs'])  5.54 us
    ppermute x1, starting transfers between devices, per_device(): pooled_halo[n] = lax.ppermute(partials[n], 'chan', op['pairs'])  4.4 us
    unnamed x30, local copies, waits for them, and re-layouts  3.91 us
  transfers between devices with their start and end apart: 16, of which 7 were waited for; matrix products, arithmetic and copies ran while one was open for 6% of the time, Pallas kernels for 48%

profile of v4, /device:TPU:9, one launch (start us, length us, event | category | flops | bytes accessed | tf_op | source)
XLA Modules:
  0.0 123.7 jit_solution(15189001014539230983)
XLA Ops:
  0.7 1.6 %shard_map.364.after = f32[144,128]{1,0:T(8,128)} custom-call(f32[9,36]{1,0:T(8,128)} %bitcast.82, f32[1,36]{1,0:T(1,128)} %bitcast.91, f32[9,36]{1,0:T(8,128)} %bitcast.84, f32[1,36]{1,0:T(1,128)} %bitcast.93, f32[9,36]{1,0:T(8,128)} %bitcast.86, f32[1,36]{1,0:T(1,128)} %bitcast.95, f32[1,36]{1,0:T(1,128)} %bitcast.89, f32[36,144]{1,0:T(8,128)} %bitcast.75, ...), custom_call_target="tpu_custom_call" | custom-call | flops 1 | bytes 1 | tf_op jit(solution)/shard_map/pallas_call | solution.py:814
  2.3 1.2 %collective-permute-start = (f32[1,144,128]{2,1,0:T(8,128)}, f32[1,144,128]{2,1,0:T(8,128)S(1)}, u32[]{:S(2)}, u32[]{:S(2)}) collective-permute-start(f32[1,144,128]{2,1,0:T(8,128)} %bitcast.73), channel_id=1, source_target_pairs={{0,1},{1,0},{2,3},{3,2},{4,5},{5,4},{6,7},{7,6},{8,9},{9,8},{10,11... | collective-permute-start | bytes 221192 | tf_op jit(solution)/shard_map/ppermute | solution.py:847
  3.5 1.4 %constant_dynamic-slice_fusion = s32[1,916]{1,0:T(1,128)} fusion(s32[8,916]{1,0:T(8,128)} %constant.12.clone, s32[]{:T(128)S(6)} %select_n.11), kind=kLoop, calls=%fused_computation.20 | loop fusion | bytes 7332 | tf_op jit(solution)/shard_map/jit(dynamic_index_in_dim)/dynamic_slice | solution.py:912
  4.9 6.2 %shard_map.365 = (f32[11,144,128]{2,1,0:T(8,128)}, f32[10,144,128]{2,1,0:T(8,128)}, f32[15,144,128]{2,1,0:T(8,128)}) custom-call(s32[916]{0:T(1024)} %bitcast.60, f32[288,3136]{1,0:T(8,128)} %bitcast.68, f32[144,128]{1,0:T(8,128)} %shard_map.364.after), custom_call_target="tpu_custom_call" | custom-call | flops 1 | bytes 1 | tf_op jit(solution)/shard_map/pallas_call | solution.py:814
  11.0 0.0 collective-permute-done
  11.0 0.0 copy-done.5
  11.1 0.3 collective-permute-start.3
  11.3 2.3 %collective-permute-start.1 = (f32[2,144,128]{2,1,0:T(8,128)S(1)}, f32[2,144,128]{2,1,0:T(8,128)S(1)}, u32[]{:S(2)}, u32[]{:S(2)}) collective-permute-start(f32[2,144,128]{2,1,0:T(8,128)S(1)} %pad_maximum_fusion.2), channel_id=1, source_target_pairs={{0,4},{1,5},{2,6},{3,7},{4,0},{5,1},{6,2},{7,3},{8,12},{9,13},{10,... | collective-permute-start | bytes 442376 | tf_op jit(solution)/shard_map/ppermute | solution.py:847
  13.7 6.4 %shard_map.366.after.cot_ref = f32[25,2,144,128]{3,2,1,0:T(8,128)} custom-call(s32[916]{0:T(1024)} %bitcast.61, f32[288,3136]{1,0:T(8,128)} %bitcast.69, f32[11,144,128]{2,1,0:T(8,128)} %get-tuple-element.85.after), custom_call_target="tpu_custom_call" | custom-call | flops 1 | bytes 1 | tf_op jit(solution)/shard_map/pallas_call | solution.py:814
  20.1 0.2 collective-permute-done.1
  20.3 0.1 collective-permute-start.2
  20.4 0.0 copy-start.12
  20.4 8.8 %shard_map.367.after.x_ref = f32[93,144,128]{2,1,0:T(8,128)} custom-call(s32[916]{0:T(1024)} %bitcast.62, f32[144,11664]{1,0:T(8,128)} %bitcast.70, f32[25,2,144,128]{3,2,1,0:T(8,128)} %shard_map.366.after.cot_ref), custom_call_target="tpu_custom_call" | custom-call | flops 1 | bytes 1 | tf_op jit(solution)/shard_map/pallas_call | solution.py:814
  29.1 0.0 collective-permute-done.2
  29.1 0.9 pad_maximum_fusion.parts
  30.0 0.0 collective-permute-done.3.refs_0_
  30.0 0.0 copy-done.12
  30.0 4.3 %collective-permute-start.5 = (f32[15,144,128]{2,1,0:T(8,128)S(1)}, f32[15,144,128]{2,1,0:T(8,128)S(1)}, u32[]{:S(2)}, u32[]{:S(2)}) collective-permute-start(f32[15,144,128]{2,1,0:T(8,128)S(1)} %copy-done.12), channel_id=1, source_target_pairs={{3,4},{4,3},{1,2},{2,1},{5,6},{6,5},{11,12},{12,11},{9,10},{10,9},... | collective-permute-start | bytes 3317768 | tf_op jit(solution)/shard_map/ppermute | solution.py:1021
  34.3 1.3 %collective-permute-start.4 = (f32[10,144,128]{2,1,0:T(8,128)}, f32[10,144,128]{2,1,0:T(8,128)S(1)}, u32[]{:S(2)}, u32[]{:S(2)}) collective-permute-start(f32[10,144,128]{2,1,0:T(8,128)} %get-tuple-element.86), channel_id=1, source_target_pairs={{3,2},{4,5},{1,0},{6,7},{11,10},{12,13},{9,8},{14,15},{19,18},{20,... | collective-permute-start | bytes 2211848 | tf_op jit(solution)/shard_map/ppermute | solution.py:1014
  35.6 0.0 copy-start.4
  35.7 2.9 %shard_map.368 = (f32[288,128]{1,0:T(8,128)}, f32[128,384]{1,0:T(8,128)}, f32[16,288]{1,0:T(8,128)}, f32[16,144]{1,0:T(8,128)}, f32[40,256]{1,0:T(8,128)}, /*index=5*/f32[8,128]{1,0:T(8,128)}) custom-call(s32[1]{0:T(128)} %bitcast.17.me, f32[8,144,128]{2,1,0:T(8,128)} %pad_maximum_fusion.parts, f32[16,144]{1,0:T(8,128)} %bitcast.80, f32[16,288]{1,0:T(8,128)} %bitcast.78, ...), custom_call_target="tpu_custom_call" | custom-call | flops 1 | bytes 1 | tf_op jit(solution)/shard_map/pallas_call | solution.py:814
  38.6 0.0 copy-start.8
  38.6 1.3 %collective-permute-start.6 = (f32[40,256]{1,0:T(8,128)}, f32[40,256]{1,0:T(8,128)S(1)}, u32[]{:S(2)}, u32[]{:S(2)}) collective-permute-start(f32[40,256]{1,0:T(8,128)} %get-tuple-element.95), channel_id=1, source_target_pairs={{0,16},{8,24},{16,0},{24,8},{1,17},{9,25},{17,1},{25,9},{2,18},{10... | collective-permute-start | bytes 122888 | tf_op jit(solution)/shard_map/ppermute | solution.py:847
  39.9 2.1 %collective-permute-done.6 = f32[40,256]{1,0:T(8,128)S(1)} collective-permute-done((f32[40,256]{1,0:T(8,128)}, f32[40,256]{1,0:T(8,128)S(1)}, u32[]{:S(2)}, u32[]{:S(2)}) %collective-permute-start.6) | collective-permute-done | bytes 40992 | tf_op jit(solution)/shard_map/ppermute | solution.py:847
  42.0 0.8 add.56
  42.8 2.8 %collective-permute-start.7 = (f32[40,256]{1,0:T(8,128)S(1)}, f32[40,256]{1,0:T(8,128)S(1)}, u32[]{:S(2)}, u32[]{:S(2)}) collective-permute-start(f32[40,256]{1,0:T(8,128)S(1)} %add.56), channel_id=1, source_target_pairs={{0,8},{8,0},{16,24},{24,16},{1,9},{9,1},{17,25},{25,17},{2,10},{10... | collective-permute-start | bytes 122888 | tf_op jit(solution)/shard_map/ppermute | solution.py:847
  45.6 0.0 copy-done.4
  45.6 2.9 %copy-done = f32[93,144,128]{2,1,0:T(8,128)S(1)} copy-done((f32[93,144,128]{2,1,0:T(8,128)S(1)}, f32[93,144,128]{2,1,0:T(8,128)}, u32[]{:S(2)}) %copy-start) | copy-done | bytes 6856728
  48.5 0.9 copy-done.2
  49.4 5.8 %shard_map.369 = (f32[21,144,128]{2,1,0:T(8,128)S(1)}, f32[15,144,128]{2,1,0:T(8,128)S(1)}, f32[7,144,128]{2,1,0:T(8,128)S(1)}) custom-call(s32[916]{0:T(1024)S(1)} %bitcast.63, f32[93,144,128]{2,1,0:T(8,128)S(1)} %copy-done, f32[288,128]{1,0:T(8,128)S(1)} %copy-done.2), custom_call_target="tpu_custom_call" | custom-call | flops 1 | bytes 1 | tf_op jit(solution)/shard_map/pallas_call | solution.py:814
  55.2 4.4 %collective-permute-start.13 = (f32[21,144,128]{2,1,0:T(8,128)S(1)}, f32[21,144,128]{2,1,0:T(8,128)S(1)}, u32[]{:S(2)}, u32[]{:S(2)}) collective-permute-start(f32[21,144,128]{2,1,0:T(8,128)S(1)} %get-tuple-element.104), channel_id=1, source_target_pairs={{2,3},{5,4},{0,1},{7,6},{1,0},{6,7},{10,11},{13,12},{8,9},{15,14},... | collective-permute-start | bytes 4644872 | tf_op jit(solution)/shard_map/ppermute | solution.py:1068
  59.6 0.0 collective-permute-done.7
  59.7 0.0 copy-done.6
  59.7 1.3 %multiply_reduce_fusion = (f32[]{:T(128)}, f32[36,144]{1,0:T(8,128)S(1)}, f32[144,36]{0,1:T(8,128)}, f32[144,36]{0,1:T(8,128)}) fusion(f32[144,36]{0,1:T(8,128)S(1)} %copy-done.6, f32[144,36]{0,1:T(8,128)S(1)} %copy-done.7, f32[40,256]{1,0:T(8,128)S(1)} %add.57, f32[144,36]{0,1:T(8,128)S(1)} %copy-done.8), kind=kLoop, calls=%fused_computation.6 | loop fusion | flops 77759 | bytes 145156 | tf_op jit(solution)/shard_map/reduce_sum | solution.py:1079
  61.0 0.0 copy-start.1
  61.0 7.1 %shard_map.370.own_ref = f32[25,288,128]{2,1,0:T(8,128)S(1)} custom-call(s32[916]{0:T(1024)S(1)} %bitcast.64, f32[93,144,128]{2,1,0:T(8,128)S(1)} %copy-done, f32[288,128]{1,0:T(8,128)S(1)} %copy-done.2, f32[36,144]{1,0:T(8,128)S(1)} %get-tuple-element.132.after.hu), custom_call_target="tpu_custom_call" | custom-call | flops 1 | bytes 1 | tf_op jit(solution)/shard_map/pallas_call | solution.py:814
  68.1 0.2 slice_reduce_fusion
  68.3 1.1 multiply_reduce_fusion.1
  69.4 5.5 %collective-permute-done.4.refs_1_ = f32[10,144,128]{2,1,0:T(8,128)S(1)} collective-permute-done((f32[10,144,128]{2,1,0:T(8,128)}, f32[10,144,128]{2,1,0:T(8,128)S(1)}, u32[]{:S(2)}, u32[]{:S(2)}) %collective-permute-start.4) | collective-permute-done | bytes 737312 | tf_op jit(solution)/shard_map/ppermute | solution.py:1014
  75.0 0.0 collective-permute-done.5.refs_2_
  75.0 1.9 %collective-permute-start.14 = (f32[15,144,128]{2,1,0:T(8,128)S(1)}, f32[15,144,128]{2,1,0:T(8,128)S(1)}, u32[]{:S(2)}, u32[]{:S(2)}) collective-permute-start(f32[15,144,128]{2,1,0:T(8,128)S(1)} %get-tuple-element.105), channel_id=1, source_target_pairs={{3,4},{4,3},{1,2},{2,1},{5,6},{6,5},{11,12},{12,11},{9,10},{10,9},... | collective-permute-start | bytes 3317768 | tf_op jit(solution)/shard_map/ppermute | solution.py:1098
  76.9 0.0 slice-done
  76.9 0.0 slice-done.1
  76.9 0.0 copy-done.1
  76.9 6.3 %shard_map.371.after = f32[16,384]{1,0:T(8,128)S(1)} custom-call(s32[916]{0:T(1024)S(1)} %bitcast.65, f32[93,144,128]{2,1,0:T(8,128)S(1)} %bitcast.59, f32[25,2,144,128]{3,2,1,0:T(8,128)S(1)} %copy-done.1, f32[11,144,128]{2,1,0:T(8,128)S(1)} %collective-permute-done.3.refs_0_, f32[10,144,128]{2,1,0:T(8,128)S(1)} %collective-permute-done.4.refs_1_, ...), custom_call_target="tpu_custom_call" | custom-call | flops 1 | bytes 1 | tf_op jit(solution)/shard_map/pallas_call | solution.py:814
  83.3 1.3 %collective-permute-start.8 = (f32[16,384]{1,0:T(8,128)S(1)}, f32[16,384]{1,0:T(8,128)S(1)}, u32[]{:S(2)}, u32[]{:S(2)}) collective-permute-start(f32[16,384]{1,0:T(8,128)S(1)} %shard_map.371.after), channel_id=1, source_target_pairs={{0,16},{8,24},{16,0},{24,8},{1,17},{9,25},{17,1},{25,9},{2,18},{10... | collective-permute-start | bytes 73736 | tf_op jit(solution)/shard_map/ppermute | solution.py:847
  84.5 1.3 %collective-permute-start.15 = (f32[7,144,128]{2,1,0:T(8,128)S(1)}, f32[7,144,128]{2,1,0:T(8,128)S(1)}, u32[]{:S(2)}, u32[]{:S(2)}) collective-permute-start(f32[7,144,128]{2,1,0:T(8,128)S(1)} %get-tuple-element.106), channel_id=1, source_target_pairs={{3,2},{4,5},{11,10},{12,13},{19,18},{20,21},{27,26},{28,29}} | collective-permute-start | bytes 1548296 | tf_op jit(solution)/shard_map/ppermute | solution.py:1098
  85.8 0.5 collective-permute-done.8
  86.3 1.3 %collective-permute-start.9 = (f32[16,384]{1,0:T(8,128)S(1)}, f32[16,384]{1,0:T(8,128)S(1)}, u32[]{:S(2)}, u32[]{:S(2)}) collective-permute-start(f32[16,384]{1,0:T(8,128)S(1)} %add.68), channel_id=1, source_target_pairs={{0,8},{8,0},{16,24},{24,16},{1,9},{9,1},{17,25},{25,17},{2,10},{10... | collective-permute-start | bytes 73736 | tf_op jit(solution)/shard_map/ppermute | solution.py:847
  87.7 0.8 collective-permute-done.9
  88.5 1.4 %select_select_fusion = f32[16,384]{1,0:T(8,128)S(1)} fusion(f32[16,384]{1,0:T(8,128)S(1)} %add.68, f32[16,384]{1,0:T(8,128)S(1)} %collective-permute-done.9, f32[]{:T(128)} %get-tuple-element.97, f32[]{:T(128)} %get-tuple-element.96, pred[384]{0:T(512)(128)(4,1)S(1)} %get-tuple-element.135, pred[384]{0:T(512)(128)(4,1)S(1)} %get-tuple-element.136, ...), kind=kLoop, calls=%fused_computation.8 | loop fusion | flops 30720 | bytes 74520 | tf_op jit(solution)/shard_map/jit(_where)/select_n | solution.py:1126
  89.9 5.7 %collective-permute-start.10 = (f32[16,384]{1,0:T(8,128)S(1)}, f32[16,384]{1,0:T(8,128)S(1)}, u32[]{:S(2)}, u32[]{:S(2)}) collective-permute-start(f32[16,384]{1,0:T(8,128)S(1)} %select_select_fusion), channel_id=1, source_target_pairs={{0,4},{1,5},{2,6},{3,7},{4,0},{5,1},{6,2},{7,3},{8,12},{9,13},{10,... | collective-permute-start | bytes 73736 | tf_op jit(solution)/shard_map/ppermute | solution.py:847
  95.6 11.3 %shard_map.372 = f32[144,11664]{1,0:T(8,128)} custom-call(s32[916]{0:T(1024)S(1)} %bitcast.66, f32[25,2,144,128]{3,2,1,0:T(8,128)S(1)} %copy-done.1, f32[288,128]{1,0:T(8,128)S(1)} %copy-done.2, f32[16,384]{1,0:T(8,128)S(1)} %shard_map.371.after, f32[11,144,128]{2,1,0:T(8,128)S(1)} %collective-permute-done.3.refs_0_, ...), custom_call_target="tpu_custom_call" | custom-call | flops 1 | bytes 1 | tf_op jit(solution)/shard_map/pallas_call | solution.py:814
  106.9 0.0 collective-permute-done.10
  106.9 0.1 collective-permute-start.11
  107.0 3.0 %collective-permute-done.11 = f32[16,384]{1,0:T(8,128)S(1)} collective-permute-done((f32[16,384]{1,0:T(8,128)S(1)}, f32[16,384]{1,0:T(8,128)S(1)}, u32[]{:S(2)}, u32[]{:S(2)}) %collective-permute-start.11) | collective-permute-done | bytes 24608 | tf_op jit(solution)/shard_map/ppermute | solution.py:847
  110.0 0.0 collective-permute-start.12
  110.0 6.5 %collective-permute-done.13.refs_0_ = f32[21,144,128]{2,1,0:T(8,128)S(1)} collective-permute-done((f32[21,144,128]{2,1,0:T(8,128)S(1)}, f32[21,144,128]{2,1,0:T(8,128)S(1)}, u32[]{:S(2)}, u32[]{:S(2)}) %collective-permute-start.13) | collective-permute-done | bytes 1548320 | tf_op jit(solution)/shard_map/ppermute | solution.py:1068
  116.5 0.0 collective-permute-done.15.refs_2_
  116.5 0.0 collective-permute-done.14.refs_1_
  116.5 4.5 %shard_map.373 = f32[288,3136]{1,0:T(8,128)} custom-call(s32[916]{0:T(1024)S(1)} %bitcast.67, f32[25,288,128]{2,1,0:T(8,128)S(1)} %shard_map.370.own_ref, f32[21,144,128]{2,1,0:T(8,128)S(1)} %collective-permute-done.13.refs_0_, f32[15,144,128]{2,1,0:T(8,128)S(1)} %collective-permute-done.14.refs_1_, f32[7,144,128]{2,1,0:T(8,128)S(1)} %collective-permute-done.15.refs_2_), custom_call_target="tpu_custom_call" | custom-call | flops 1 | bytes 1 | tf_op jit(solution)/shard_map/pallas_call | solution.py:814
  121.1 0.0 collective-permute-done.12
  121.1 0.6 add.72.sums
  121.7 2.0 %shard_map.374 = (f32[9,36]{1,0:T(8,128)}, f32[9,36]{1,0:T(8,128)}, f32[9,36]{1,0:T(8,128)}, f32[9,36]{1,0:T(8,128)}, f32[36,144]{1,0:T(8,128)}, /*index=5*/f32[...) custom-call(s32[1]{0:T(128)} %bitcast.17.me, ...), custom_call_target="tpu_custom_call" | custom-call | flops 1 | bytes 1 | tf_op jit(solution)/shard_map/pallas_call | solution.py:814
  (26 shorter events, 0.1 us)
Async XLA Ops:
  2.3 8.8 %copy-start.5 = (f32[144,128]{1,0:T(8,128)S(1)}, f32[144,128]{1,0:T(8,128)}, u32[]{:S(2)}) copy-start(f32[144,128]{1,0:T(8,128)} %shard_map.364.after) | copy-start | bytes 221188
  2.3 8.8 %collective-permute-start = (f32[1,144,128]{2,1,0:T(8,128)}, f32[1,144,128]{2,1,0:T(8,128)S(1)}, u32[]{:S(2)}, u32[]{:S(2)}) collective-permute-start(f32[1,144,128]{2,1,0:T(8,128)} %bitcast.73), channel_id=1, source_target_pairs={{0,1},{1,0},{2,3},{3,2},{4,5},{5,4},{6,7},{7,6},{8,9},{9,8},{10,11... | collective-permute-start | bytes 221192 | tf_op jit(solution)/shard_map/ppermute | solution.py:847
  11.1 19.0 %collective-permute-start.3 = (f32[11,144,128]{2,1,0:T(8,128)}, f32[11,144,128]{2,1,0:T(8,128)S(1)}, u32[]{:S(2)}, u32[]{:S(2)}) collective-permute-start(f32[11,144,128]{2,1,0:T(8,128)} %get-tuple-element.85.after), channel_id=1, source_target_pairs={{0,1},{1,0},{3,2},{4,5},{6,7},{7,6},{2,3},{5,4},{8,9},{9,8},{11,10... | collective-permute-start | bytes 2433032 | tf_op jit(solution)/shard_map/ppermute | solution.py:1014
  11.3 8.9 %collective-permute-start.1 = (f32[2,144,128]{2,1,0:T(8,128)S(1)}, f32[2,144,128]{2,1,0:T(8,128)S(1)}, u32[]{:S(2)}, u32[]{:S(2)}) collective-permute-start(f32[2,144,128]{2,1,0:T(8,128)S(1)} %pad_maximum_fusion.2), channel_id=1, source_target_pairs={{0,4},{1,5},{2,6},{3,7},{4,0},{5,1},{6,2},{7,3},{8,12},{9,13},{10,... | collective-permute-start | bytes 442376 | tf_op jit(solution)/shard_map/ppermute | solution.py:847
  20.3 8.9 %collective-permute-start.2 = (f32[4,144,128]{2,1,0:T(8,128)S(1)}, f32[4,144,128]{2,1,0:T(8,128)S(1)}, u32[]{:S(2)}, u32[]{:S(2)}) collective-permute-start(f32[4,144,128]{2,1,0:T(8,128)S(1)} %pad_maximum_fusion.1), channel_id=1, source_target_pairs={{0,2},{1,3},{2,0},{3,1},{4,6},{5,7},{6,4},{7,5},{8,10},{9,11},{10,... | collective-permute-start | bytes 884744 | tf_op jit(solution)/shard_map/ppermute | solution.py:847
  20.4 9.7 %copy-start.12 = (f32[15,144,128]{2,1,0:T(8,128)S(1)}, f32[15,144,128]{2,1,0:T(8,128)}, u32[]{:S(2)}) copy-start(f32[15,144,128]{2,1,0:T(8,128)} %get-tuple-element.94) | copy-start | bytes 3317764
  30.0 44.9 %collective-permute-start.5 = (f32[15,144,128]{2,1,0:T(8,128)S(1)}, f32[15,144,128]{2,1,0:T(8,128)S(1)}, u32[]{:S(2)}, u32[]{:S(2)}) collective-permute-start(f32[15,144,128]{2,1,0:T(8,128)S(1)} %copy-done.12), channel_id=1, source_target_pairs={{3,4},{4,3},{1,2},{2,1},{5,6},{6,5},{11,12},{12,11},{9,10},{10,9},... | collective-permute-start | bytes 3317768 | tf_op jit(solution)/shard_map/ppermute | solution.py:1021
  34.3 40.6 %collective-permute-start.4 = (f32[10,144,128]{2,1,0:T(8,128)}, f32[10,144,128]{2,1,0:T(8,128)S(1)}, u32[]{:S(2)}, u32[]{:S(2)}) collective-permute-start(f32[10,144,128]{2,1,0:T(8,128)} %get-tuple-element.86), channel_id=1, source_target_pairs={{3,2},{4,5},{1,0},{6,7},{11,10},{12,13},{9,8},{14,15},{19,18},{20,... | collective-permute-start | bytes 2211848 | tf_op jit(solution)/shard_map/ppermute | solution.py:1014
  35.6 9.9 %copy-start.4 = (s32[1,916]{1,0:T(1,128)S(1)}, s32[1,916]{1,0:T(1,128)}, u32[]{:S(2)}) copy-start(s32[1,916]{1,0:T(1,128)} %constant_dynamic-slice_fusion) | copy-start | bytes 10996
  38.6 21.1 %copy-start.6 = (f32[144,36]{0,1:T(8,128)S(1)}, f32[144,36]{0,1:T(8,128)}, u32[]{:S(2)}) copy-start(f32[144,36]{0,1:T(8,128)} %param.25) | copy-start | bytes 62212
  38.6 21.1 %copy-start.7 = (f32[144,36]{0,1:T(8,128)S(1)}, f32[144,36]{0,1:T(8,128)}, u32[]{:S(2)}) copy-start(f32[144,36]{0,1:T(8,128)} %param.33) | copy-start | bytes 62212
  38.6 21.1 %copy-start.8 = (f32[144,36]{0,1:T(8,128)S(1)}, f32[144,36]{0,1:T(8,128)}, u32[]{:S(2)}) copy-start(f32[144,36]{0,1:T(8,128)} %param.29) | copy-start | bytes 62212
  38.6 3.4 %collective-permute-start.6 = (f32[40,256]{1,0:T(8,128)}, f32[40,256]{1,0:T(8,128)S(1)}, u32[]{:S(2)}, u32[]{:S(2)}) collective-permute-start(f32[40,256]{1,0:T(8,128)} %get-tuple-element.95), channel_id=1, source_target_pairs={{0,16},{8,24},{16,0},{24,8},{1,17},{9,25},{17,1},{25,9},{2,18},{10... | collective-permute-start | bytes 122888 | tf_op jit(solution)/shard_map/ppermute | solution.py:847
  42.8 16.8 %collective-permute-start.7 = (f32[40,256]{1,0:T(8,128)S(1)}, f32[40,256]{1,0:T(8,128)S(1)}, u32[]{:S(2)}, u32[]{:S(2)}) collective-permute-start(f32[40,256]{1,0:T(8,128)S(1)} %add.56), channel_id=1, source_target_pairs={{0,8},{8,0},{16,24},{24,16},{1,9},{9,1},{17,25},{25,17},{2,10},{10... | collective-permute-start | bytes 122888 | tf_op jit(solution)/shard_map/ppermute | solution.py:847
  45.6 2.9 %copy-start = (f32[93,144,128]{2,1,0:T(8,128)S(1)}, f32[93,144,128]{2,1,0:T(8,128)}, u32[]{:S(2)}) copy-start(f32[93,144,128]{2,1,0:T(8,128)} %shard_map.367.after.x_ref) | copy-start | bytes 20570116
  48.5 0.9 copy-start.2
  49.4 27.5 %slice-start = ((s8[6856704]{0:T(1024)(128)(4,1)}), s8[4194304]{0:T(1024)(128)(4,1)S(1)}, s32[]{:S(2)}) async-start(s8[6856704]{0:T(1024)(128)(4,1)} %bitcast.58), calls=%async_computation | async-start | bytes 8388608
  55.2 61.3 %collective-permute-start.13 = (f32[21,144,128]{2,1,0:T(8,128)S(1)}, f32[21,144,128]{2,1,0:T(8,128)S(1)}, u32[]{:S(2)}, u32[]{:S(2)}) collective-permute-start(f32[21,144,128]{2,1,0:T(8,128)S(1)} %get-tuple-element.104), channel_id=1, source_target_pairs={{2,3},{5,4},{0,1},{7,6},{1,0},{6,7},{10,11},{13,12},{8,9},{15,14},... | collective-permute-start | bytes 4644872 | tf_op jit(solution)/shard_map/ppermute | solution.py:1068
  61.0 7.1 %copy-start.3 = (f32[36,144]{1,0:T(8,128)}, f32[36,144]{1,0:T(8,128)S(1)}, u32[]{:S(2)}) copy-start(f32[36,144]{1,0:T(8,128)S(1)} %get-tuple-element.132.after.hu) | copy-start | bytes 62212
  61.0 7.3 %copy-start.9 = (f32[36]{0:T(128)S(1)}, f32[36]{0:T(128)}, u32[]{:S(2)}) copy-start(f32[36]{0:T(128)} %param.26) | copy-start | bytes 436
  61.0 7.3 %copy-start.10 = (f32[36]{0:T(128)S(1)}, f32[36]{0:T(128)}, u32[]{:S(2)}) copy-start(f32[36]{0:T(128)} %param.30) | copy-start | bytes 436
  61.0 7.3 %copy-start.11 = (f32[36]{0:T(128)S(1)}, f32[36]{0:T(128)}, u32[]{:S(2)}) copy-start(f32[36]{0:T(128)} %param.34) | copy-start | bytes 436
  61.0 16.0 %slice-start.1 = ((s8[6856704]{0:T(1024)(128)(4,1)}), s8[2662400]{0:T(1024)(128)(4,1)S(1)}, s32[]{:S(2)}) async-start(s8[6856704]{0:T(1024)(128)(4,1)} %bitcast.58), calls=%async_computation.1 | async-start | bytes 5324800
  61.0 16.0 %copy-start.1 = (f32[25,2,144,128]{3,2,1,0:T(8,128)S(1)}, f32[25,2,144,128]{3,2,1,0:T(8,128)}, u32[]{:S(2)}) copy-start(f32[25,2,144,128]{3,2,1,0:T(8,128)} %shard_map.366.after.cot_ref) | copy-start | bytes 11059204
  75.0 41.5 %collective-permute-start.14 = (f32[15,144,128]{2,1,0:T(8,128)S(1)}, f32[15,144,128]{2,1,0:T(8,128)S(1)}, u32[]{:S(2)}, u32[]{:S(2)}) collective-permute-start(f32[15,144,128]{2,1,0:T(8,128)S(1)} %get-tuple-element.105), channel_id=1, source_target_pairs={{3,4},{4,3},{1,2},{2,1},{5,6},{6,5},{11,12},{12,11},{9,10},{10,9},... | collective-permute-start | bytes 3317768 | tf_op jit(solution)/shard_map/ppermute | solution.py:1098
  83.3 3.0 %collective-permute-start.8 = (f32[16,384]{1,0:T(8,128)S(1)}, f32[16,384]{1,0:T(8,128)S(1)}, u32[]{:S(2)}, u32[]{:S(2)}) collective-permute-start(f32[16,384]{1,0:T(8,128)S(1)} %shard_map.371.after), channel_id=1, source_target_pairs={{0,16},{8,24},{16,0},{24,8},{1,17},{9,25},{17,1},{25,9},{2,18},{10... | collective-permute-start | bytes 73736 | tf_op jit(solution)/shard_map/ppermute | solution.py:847
  84.5 32.0 %collective-permute-start.15 = (f32[7,144,128]{2,1,0:T(8,128)S(1)}, f32[7,144,128]{2,1,0:T(8,128)S(1)}, u32[]{:S(2)}, u32[]{:S(2)}) collective-permute-start(f32[7,144,128]{2,1,0:T(8,128)S(1)} %get-tuple-element.106), channel_id=1, source_target_pairs={{3,2},{4,5},{11,10},{12,13},{19,18},{20,21},{27,26},{28,29}} | collective-permute-start | bytes 1548296 | tf_op jit(solution)/shard_map/ppermute | solution.py:1098
  86.3 2.2 %collective-permute-start.9 = (f32[16,384]{1,0:T(8,128)S(1)}, f32[16,384]{1,0:T(8,128)S(1)}, u32[]{:S(2)}, u32[]{:S(2)}) collective-permute-start(f32[16,384]{1,0:T(8,128)S(1)} %add.68), channel_id=1, source_target_pairs={{0,8},{8,0},{16,24},{24,16},{1,9},{9,1},{17,25},{25,17},{2,10},{10... | collective-permute-start | bytes 73736 | tf_op jit(solution)/shard_map/ppermute | solution.py:847
  89.9 17.0 %collective-permute-start.10 = (f32[16,384]{1,0:T(8,128)S(1)}, f32[16,384]{1,0:T(8,128)S(1)}, u32[]{:S(2)}, u32[]{:S(2)}) collective-permute-start(f32[16,384]{1,0:T(8,128)S(1)} %select_select_fusion), channel_id=1, source_target_pairs={{0,4},{1,5},{2,6},{3,7},{4,0},{5,1},{6,2},{7,3},{8,12},{9,13},{10,... | collective-permute-start | bytes 73736 | tf_op jit(solution)/shard_map/ppermute | solution.py:847
  106.9 3.0 %collective-permute-start.11 = (f32[16,384]{1,0:T(8,128)S(1)}, f32[16,384]{1,0:T(8,128)S(1)}, u32[]{:S(2)}, u32[]{:S(2)}) collective-permute-start(f32[16,384]{1,0:T(8,128)S(1)} %add.70), channel_id=1, source_target_pairs={{0,2},{1,3},{2,0},{3,1},{4,6},{5,7},{6,4},{7,5},{8,10},{9,11},{10,... | collective-permute-start | bytes 73736 | tf_op jit(solution)/shard_map/ppermute | solution.py:847
  110.0 11.1 %collective-permute-start.12 = (f32[16,384]{1,0:T(8,128)S(1)}, f32[16,384]{1,0:T(8,128)S(1)}, u32[]{:S(2)}, u32[]{:S(2)}) collective-permute-start(f32[16,384]{1,0:T(8,128)S(1)} %add.71), channel_id=1, source_target_pairs={{0,1},{1,0},{2,3},{3,2},{4,5},{5,4},{6,7},{7,6},{8,9},{9,8},{10,11... | collective-permute-start | bytes 73736 | tf_op jit(solution)/shard_map/ppermute | solution.py:847

commit v5 on v4

--- a/solution.py
+++ b/solution.py
@@ -1,4 +1,5 @@
 import functools
+import types
 
 import jax
 import jax.numpy as jnp
@@ -13,6 +14,7 @@
 OUTG = 14
 LANES = 128
 SUBL = 8
+CHAN = "chan"
 UNIT = 16
 
 beta_one = 0.9
@@ -28,18 +30,18 @@
 def sized(parts):
     full = max(len(f) for _, (f, _) in parts)
     half = max(len(h) for _, (_, h) in parts)
-    return {
-        "full": full,
-        "half": half,
-        "size": full + half,
-        "parts": parts,
-        "pairs": [pair for pair, _ in parts],
-        "tiles": [
+    return types.SimpleNamespace(
+        full=full,
+        half=half,
+        size=full + half,
+        parts=parts,
+        pairs=[pair for pair, _ in parts],
+        tiles=[
             [(j, *v) for j, v in enumerate(f)] + [(full + j, *v) for j, v in enumerate(h)]
             for _, (f, h) in parts
         ],
-        "near": all(src ^ dst == 1 for (src, dst), _ in parts),
-    }
+        near=all(src ^ dst == 1 for (src, dst), _ in parts),
+    )
 
 
 def halves(message):
@@ -72,26 +74,26 @@
 def loads(ops, groups):
     got = np.zeros(groups, np.int64)
     for op in ops:
-        for _, dst in op["pairs"]:
-            got[dst] += 2 * op["full"] + op["half"]
+        for _, dst in op.pairs:
+            got[dst] += 2 * op.full + op.half
     return got
 
 
 def joined(ops, others, groups):
     for n in range(1, len(ops)):
         for m in range(n):
-            if not (ops[n]["near"] and ops[m]["near"]):
+            if not (ops[n].near and ops[m].near):
                 continue
-            for pair, message in list(ops[n]["parts"]):
+            for pair, message in list(ops[n].parts):
                 got = loads(ops + others, groups)
-                more = halves(ops[m]["parts"][0][1]) - 2 * ops[n]["full"] - ops[n]["half"]
+                more = halves(ops[m].parts[0][1]) - 2 * ops[n].full - ops[n].half
                 if (
-                    len(ops[n]["parts"]) > 1
-                    and free_in(ops[m]["parts"], pair)
+                    len(ops[n].parts) > 1
+                    and free_in(ops[m].parts, pair)
                     and got[pair[1]] + more < 0.9 * max(got)
                 ):
-                    ops[n] = sized([v for v in ops[n]["parts"] if v[0] != pair])
-                    ops[m] = sized(ops[m]["parts"] + [(pair, message)])
+                    ops[n] = sized([v for v in ops[n].parts if v[0] != pair])
+                    ops[m] = sized(ops[m].parts + [(pair, message)])
     return ops
 
 
@@ -140,18 +142,18 @@
     ops += grouped([(p, t) for p, t in wanted.items() if p[0] ^ p[1] != 1], 2)
     back_ops = grouped([((d, s), t) for (s, d), t in wanted.items()], 2)
     back_ops = joined(back_ops, ops, groups)
-    longest = max(op["size"] for op in back_ops)
+    longest = max(op.size for op in back_ops)
     for op in back_ops:
-        op["early"] = op["near"] and 4 * op["size"] > 3 * longest
+        op.early = op.near and 4 * op.size > 3 * longest
     in_base = np.arange(groups) * n_in // LANES
     in_shift = np.arange(groups) * n_in % LANES
     out_base = np.arange(groups) * n_out // LANES
     out_shift = np.arange(groups) * n_out % LANES
     in_tiles = int(max(-(-(in_shift + n_in) // LANES)))
     out_tiles = int(max(-(-(out_shift + n_out) // LANES)))
-    sizes = [op["size"] for op in ops]
+    sizes = [op.size for op in ops]
     halo = sum(sizes)
-    back_sizes = [op["size"] for op in back_ops]
+    back_sizes = [op.size for op in back_ops]
     back_halo = sum(back_sizes)
     owned = [
         range(int(out_base[k]), int(out_base[k]) - (-(int(out_shift[k]) + n_out) // LANES))
@@ -163,12 +165,12 @@
     upper = np.zeros((4, groups, max(halo, back_halo)), np.int64)
     start = 0
     for op in ops:
-        for (src, dst), tiles in zip(op["pairs"], op["tiles"]):
+        for (src, dst), tiles in zip(op.pairs, op.tiles):
             for j, p, high in tiles:
                 own_slot[src, start + j] = p - out_base[src]
                 got[dst].append((p, start + j))
                 upper[0, src, start + j] = upper[1, dst, start + j] = high
-        start += op["size"]
+        start += op.size
     most = max(len(v) for v in got)
 
     def tap_rows(device, p):
@@ -201,13 +203,13 @@
                 slot_of[k][p] = out_tiles + place
     start = 0
     for op in back_ops:
-        for (src, dst), tiles in zip(op["pairs"], op["tiles"]):
+        for (src, dst), tiles in zip(op.pairs, op.tiles):
             names = [p for p, _ in got[src]]
             for j, p, high in tiles:
                 from_got[src, start + j] = names.index(p)
                 adds[dst][p - out_base[dst]].append(start + j)
                 upper[2, src, start + j] = upper[3, dst, start + j] = high
-        start += op["size"]
+        start += op.size
     n_merges = max(len(v) for v in merges)
     merges = np.array([v + [[none, none]] * (n_merges - len(v)) for v in merges], np.int64)
     n_adds = max(len(v) for per_dev in adds for v in per_dev)
@@ -238,40 +240,44 @@
         reach_tables.append(
             np.array([v + [filler] * (size - len(v)) for v in per_device_lists]).reshape(groups, -1)
         )
-    parts = [
-        ("shifts", np.stack([in_shift, out_shift], axis=1)),
-        ("own_slot", own_slot),
-        ("own_taps", own_taps.reshape(groups, -1)),
-        ("got_taps", got_taps.reshape(groups, -1)),
-        ("from_got", from_got),
-        ("merges", merges.reshape(groups, -1)),
-        ("adds", adds.reshape(groups, -1)),
-        *((f"upper{q}", v) for q, v in enumerate(upper)),
-        *((f"kind{q}", v) for q, v in enumerate(reach_tables)),
-    ]
-    at, total = {}, 0
-    for name, v in parts:
-        at[name] = total
-        total += v.shape[1]
-    return {
-        "ops": ops,
-        "sizes": sizes,
-        "halo": halo,
-        "back_ops": back_ops,
-        "back_sizes": back_sizes,
-        "back_halo": back_halo,
-        "in_tiles": in_tiles,
-        "out_tiles": out_tiles,
-        "most": most,
-        "n_merges": n_merges,
-        "n_adds": n_adds,
-        "n_in": n_in,
-        "n_out": n_out,
-        "kinds": [[3 * a + e for a, e in kind] for kind in kinds],
-        "kind_sizes": kind_sizes,
-        "at": at,
-        "table": np.concatenate([v for _, v in parts], axis=1).astype(np.int32),
-    }
+    parts = types.SimpleNamespace(
+        shifts=np.stack([in_shift, out_shift], axis=1),
+        own_slot=own_slot,
+        own_taps=own_taps.reshape(groups, -1),
+        got_taps=got_taps.reshape(groups, -1),
+        from_got=from_got,
+        merges=merges.reshape(groups, -1),
+        adds=adds.reshape(groups, -1),
+        upper=list(upper),
+        kinds=reach_tables,
+    )
+    at, total, columns = types.SimpleNamespace(), 0, []
+    for name, v in vars(parts).items():
+        places = []
+        for one in v if isinstance(v, list) else [v]:
+            places.append(total)
+            total += one.shape[1]
+            columns.append(one)
+        setattr(at, name, places if isinstance(v, list) else places[0])
+    return types.SimpleNamespace(
+        ops=ops,
+        sizes=sizes,
+        halo=halo,
+        back_ops=back_ops,
+        back_sizes=back_sizes,
+        back_halo=back_halo,
+        in_tiles=in_tiles,
+        out_tiles=out_tiles,
+        most=most,
+        n_merges=n_merges,
+        n_adds=n_adds,
+        n_in=n_in,
+        n_out=n_out,
+        kinds=[[3 * a + e for a, e in kind] for kind in kinds],
+        kind_sizes=kind_sizes,
+        at=at,
+        table=np.concatenate(columns, axis=1).astype(np.int32),
+    )
 
 
 def lane_ids():
@@ -328,8 +334,8 @@
         align_into(
             lambda t: cot_ref[rows_at(unit, part, 2), tile_lanes(t)],
             lambda t, v: held.__setitem__((t, slice(part * UNIT, (part + 1) * UNIT)), v),
-            plan["n_out"],
-            plan["out_tiles"],
+            plan.n_out,
+            plan.out_tiles,
             shift,
         )
 
@@ -365,7 +371,8 @@
 HEAD_LANE = 96
 
 
-def small_kernel(per_dev, cw, cb, fw, fb, sw, sb, hb, hw, ci, cc, out, square):
+def small_kernel(per_dev, me, cw, cb, fw, fb, sw, sb, hb, hw, ci, cc, row, out, row_out, square):
+    row_out[...] = row[...]
     square[...] = jnp.zeros_like(square)
     for part, (w, b) in enumerate(((cw, cb), (fw, fb), (sw, sb))):
         square[2 * SUBL * part : 2 * SUBL * part + TAPS, :per_dev] = w[...]
@@ -392,8 +399,8 @@
         align_into(
             lambda t: x_ref[rows_at(unit), tile_lanes(t)],
             lambda t, v: x_out.__setitem__((t, rows_at(unit)), v),
-            plan["n_in"],
-            plan["in_tiles"],
+            plan.n_in,
+            plan.in_tiles,
             tab[0],
         )
 
@@ -403,7 +410,7 @@
 def align_cot_kernel(plan, tab, cot_ref, after, cot_out, held):
     def body(unit):
         align_cot(cot_ref, unit, held, plan, tab[1])
-        for j in range(plan["out_tiles"]):
+        for j in range(plan.out_tiles):
             for half in range(2):
                 cot_out[j, half, rows_at(unit)] = held[j, of_half(half)]
 
@@ -416,17 +423,17 @@
     def body(unit):
         align_cot(cot_ref, unit, held, plan, tab[1])
         at = 0
-        for op, out in zip(plan["ops"], outs):
+        for op, out in zip(plan.ops, outs):
             send_tiles(
                 op,
                 lambda j, at=at: [
-                    held[tab[plan["at"]["own_slot"] + at + j], of_half(half)] for half in range(2)
+                    held[tab[plan.at.own_slot + at + j], of_half(half)] for half in range(2)
                 ],
-                lambda j, at=at: tab[plan["at"]["upper0"] + at + j],
+                lambda j, at=at: tab[plan.at.upper[0] + at + j],
                 out,
                 unit,
             )
-            at += op["size"]
+            at += op.size
 
     over_units(cot_ref, 2 * UNIT, body)
 
@@ -451,26 +458,26 @@
         for half, v in enumerate(pair):
             out[2 * j + half, rows_at(unit)] = v
 
-    in_turn(op["full"], 6, load, store)
+    in_turn(op.full, 6, load, store)
     low = lane_ids() < LANES // 2
-    for j in range(op["full"], op["size"]):
+    for j in range(op.full, op.size):
         even, odd = load(j)
         high = upper(j) > 0
         left = jnp.where(high, pltpu.roll(even, LANES // 2, 1), even)
         right = jnp.where(high, odd, pltpu.roll(odd, LANES // 2, 1))
-        out[op["full"] + j, rows_at(unit)] = jnp.where(low, left, right)
+        out[op.full + j, rows_at(unit)] = jnp.where(low, left, right)
 
 
 def received_tiles(op, ref, upper, keep, unit):
     in_turn(
-        op["full"],
+        op.full,
         5,
         lambda j: [ref[2 * j + half, rows_at(unit)] for half in range(2)],
         keep,
     )
     low = lane_ids() < LANES // 2
-    for j in range(op["full"], op["size"]):
-        plane = ref[op["full"] + j, rows_at(unit)]
+    for j in range(op.full, op.size):
+        plane = ref[op.full + j, rows_at(unit)]
         turned = pltpu.roll(plane, LANES // 2, 1)
         high = upper(j) > 0
         even = jnp.where(high, jnp.where(low, 0.0, turned), jnp.where(low, plane, 0.0))
@@ -487,24 +494,24 @@
 
         weights = [tap_weights(w_ref, unit, half, range(TAPS)) for half in range(2)]
         in_turn(
-            plan["most"],
+            plan.most,
             4,
-            lambda n: tap_sums(tab, plan["at"]["got_taps"] + (1 + TAPS) * n + 1, held, weights),
+            lambda n: tap_sums(tab, plan.at.got_taps + (1 + TAPS) * n + 1, held, weights),
             lambda n, totals: keep_split_all(done, n, totals),
         )
-        done[plan["most"]] = jnp.zeros(done.shape[1:], jnp.float32)
+        done[plan.most] = jnp.zeros(done.shape[1:], jnp.float32)
         at = 0
-        for op, out in zip(plan["back_ops"], outs):
+        for op, out in zip(plan.back_ops, outs):
             send_tiles(
                 op,
                 lambda j, at=at: [
-                    done[tab[plan["at"]["from_got"] + at + j], half] for half in range(2)
+                    done[tab[plan.at.from_got + at + j], half] for half in range(2)
                 ],
-                lambda j, at=at: tab[plan["at"]["upper2"] + at + j],
+                lambda j, at=at: tab[plan.at.upper[2] + at + j],
                 out,
                 unit,
             )
-            at += op["size"]
+            at += op.size
 
     over_units(w_ref, 2 * UNIT, body)
 
@@ -518,9 +525,9 @@
             tap_weights(w_ref, unit, half, [*range(TAPS), BIAS_LANE]) for half in range(2)
         ]
         in_turn(
-            plan["out_tiles"],
+            plan.out_tiles,
             4,
-            lambda j: tap_sums(tab, plan["at"]["own_taps"] + TAPS * j, held, weights),
+            lambda j: tap_sums(tab, plan.at.own_taps + TAPS * j, held, weights),
             lambda j, totals: keep_halves(
                 out, j, unit, [totals[half] + weights[half][TAPS] for half in range(2)]
             ),
@@ -530,7 +537,7 @@
 
 
 def take_cots(plan, tab, unit, cot_ref, halos, cots):
-    own = plan["out_tiles"]
+    own = plan.out_tiles
     in_turn(
         own,
         5,
@@ -538,15 +545,15 @@
         lambda j, v: keep_split_all(cots, j, v),
     )
     at = 0
-    for op, ref in zip(plan["ops"], halos):
+    for op, ref in zip(plan.ops, halos):
         received_tiles(
             op,
             ref,
-            lambda j, at=at: tab[plan["at"]["upper1"] + at + j],
+            lambda j, at=at: tab[plan.at.upper[1] + at + j],
             lambda j, v, at=at: keep_split_all(cots, own + at + j, v),
             unit,
         )
-        at += op["size"]
+        at += op.size
     cots[own + at] = jnp.zeros(cots.shape[1:], jnp.float32)
 
 
@@ -556,15 +563,15 @@
 
 
 def merge_cots(plan, tab, cots):
-    for n in range(plan["n_merges"]):
-        at = plan["at"]["merges"] + 2 * n
+    for n in range(plan.n_merges):
+        at = plan.at.merges + 2 * n
         for half in range(2):
             cots[tab[at], half] = cots[tab[at], half] + cots[tab[at + 1], half]
 
 
 def weights_kernel(plan, tab, x_ref, cot_ref, *refs):
-    halos = refs[: len(plan["sizes"])]
-    sums_ref, cots, rows = refs[len(plan["sizes"]) :]
+    halos = refs[: len(plan.sizes)]
+    sums_ref, cots, rows = refs[len(plan.sizes) :]
     step = pl.program_id(0)
     per = x_ref.shape[1] // UNIT
     zero = jnp.zeros((UNIT, LANES), jnp.float32)
@@ -578,15 +585,15 @@
         here = step * per + unit
         for half in range(2):
             bias = cots[0, half]
-            for j in range(1, plan["out_tiles"]):
+            for j in range(1, plan.out_tiles):
                 bias = bias + cots[j, half]
             rows[TAPS, of_half(half, here), :] = bias
         merge_cots(plan, tab, cots)
-        for q, (kind, size) in enumerate(zip(plan["kinds"], plan["kind_sizes"])):
+        for q, (kind, size) in enumerate(zip(plan.kinds, plan.kind_sizes)):
             width = 1 + len(kind)
             total = [[zero] * len(kind) for _ in range(2)]
             for j in range(size):
-                at = plan["at"][f"kind{q}"] + width * j
+                at = plan.at.kinds[q] + width * j
                 tile = x_ref[tab[at], rows_at(unit)]
                 for n in range(len(kind)):
                     slot = tab[at + 1 + n]
@@ -615,18 +622,18 @@
 
 
 def patches_kernel(plan, tab, cot_ref, w_ref, after, *refs):
-    halos = refs[: len(plan["sizes"])]
-    grad_ref, cots, back = refs[len(plan["sizes"]) :]
+    halos = refs[: len(plan.sizes)]
+    grad_ref, cots, back = refs[len(plan.sizes) :]
 
     def body(unit):
         take_cots(plan, tab, unit, cot_ref, halos, cots)
         merge_cots(plan, tab, cots)
-        for q, (kind, size) in enumerate(zip(plan["kinds"], plan["kind_sizes"])):
+        for q, (kind, size) in enumerate(zip(plan.kinds, plan.kind_sizes)):
             weights = [tap_weights(w_ref, unit, half, kind) for half in range(2)]
             width = 1 + len(kind)
 
             def one(j, q=q, kind=kind, weights=weights, width=width):
-                at = plan["at"][f"kind{q}"] + width * j
+                at = plan.at.kinds[q] + width * j
                 items = []
                 for n in range(len(kind)):
                     slot = tab[at + 1 + n]
@@ -637,8 +644,8 @@
         unalign_from(
             lambda t: back[t],
             lambda t, v: grad_ref.__setitem__((rows_at(unit), tile_lanes(t)), v),
-            plan["n_in"],
-            plan["in_tiles"],
+            plan.n_in,
+            plan.in_tiles,
             tab[0],
         )
 
@@ -646,28 +653,28 @@
 
 
 def finish_kernel(plan, tab, own_ref, *refs):
-    n_ops = len(plan["back_sizes"])
+    n_ops = len(plan.back_sizes)
     halos = refs[:n_ops]
     out_ref, held, got = refs[n_ops:]
-    tiles = plan["out_tiles"]
+    tiles = plan.out_tiles
 
     def body(unit):
         at = 0
-        for op, halo in zip(plan["back_ops"], halos):
+        for op, halo in zip(plan.back_ops, halos):
             received_tiles(
                 op,
                 halo,
-                lambda j, at=at: tab[plan["at"]["upper3"] + at + j],
+                lambda j, at=at: tab[plan.at.upper[3] + at + j],
                 lambda j, v, at=at: keep_halves(got, at + j, 0, v),
                 unit,
             )
-            at += op["size"]
+            at += op.size
         got[at] = jnp.zeros(got.shape[1:], jnp.float32)
 
         def whole_sum(j):
             total = own_ref[j, both_at(unit)]
-            for n in range(plan["n_adds"]):
-                total = total + got[tab[plan["at"]["adds"] + plan["n_adds"] * j + n]]
+            for n in range(plan.n_adds):
+                total = total + got[tab[plan.at.adds + plan.n_adds * j + n]]
             return total
 
         in_turn(tiles, 5, whole_sum, held.__setitem__)
@@ -675,7 +682,7 @@
             unalign_from(
                 lambda t: held[t, part * UNIT : (part + 1) * UNIT],
                 lambda t, v: out_ref.__setitem__((rows_at(unit, part, 2), tile_lanes(t)), v),
-                plan["n_out"],
+                plan.n_out,
                 tiles,
                 tab[1],
             )
@@ -801,10 +808,20 @@
     ha_out[...] = keep_rate * ha[...] + (1.0 - keep_rate) * w_new
 
 
+class Row:
+    def __init__(self, ref):
+        self.ref = ref
+
+    def __getitem__(self, place):
+        return self.ref[0, place]
+
+
 def call(kernel, tables, operands, in_specs, outs, out_specs, scratch, steps, fills=False, tight=False):
     moved = sum(4 * int(np.prod(a.shape)) for a in operands) + sum(
         4 * int(np.prod(o.shape)) for o in outs
     )
+    if tables[0].ndim == 2:
+        by_place, kernel = kernel, lambda tab, *refs: by_place(Row(tab), *refs)
     limit = 60
     if tight:
         blocks = [s.block_shape for s in [*in_specs, *out_specs] if s.block_shape]
@@ -899,8 +916,8 @@
     pooled_cot,
     class_cot,
 ):
-    groups = lax.axis_size("chan")
-    me = lax.axis_index("chan")
+    groups = lax.axis_size(CHAN)
+    me = lax.axis_index(CHAN)
     my_id = me.astype(jnp.int32)[None]
     per_dev = conv_weight.shape[0]
     n_in, channels_in = patches.shape[1:]
@@ -908,8 +925,8 @@
     local_images = class_in.shape[1]
     images = local_images * groups
     plan = make_plan(groups, images, n_in, n_out)
-    tiles, in_tiles = plan["out_tiles"], plan["in_tiles"]
-    table = lax.dynamic_index_in_dim(jnp.asarray(plan["table"]), me, 0, keepdims=False)
+    tiles, in_tiles = plan.out_tiles, plan.in_tiles
+    width = plan.table.shape[1]
     per = 3
     steps = channels_in // (UNIT * per)
     x = patches[0].T
@@ -918,10 +935,10 @@
     rows, wide_rows = UNIT * per, 2 * UNIT * per
     x_spec = pl.BlockSpec((rows, in_lanes), lambda g, tab: (g, 0))
     cot_spec = pl.BlockSpec((wide_rows, out_lanes), lambda g, tab: (g, 0))
-    planes = [2 * op["full"] + op["half"] for op in plan["ops"]]
+    planes = [2 * op.full + op.half for op in plan.ops]
     halo_specs = [pl.BlockSpec((n, rows, LANES), lambda g, tab: (0, g, 0)) for n in planes]
     halo_outs = [f32(n, channels_in, LANES) for n in planes]
-    planes = [2 * op["full"] + op["half"] for op in plan["back_ops"]]
+    planes = [2 * op.full + op.half for op in plan.back_ops]
     back_specs = [pl.BlockSpec((n, rows, LANES), lambda g, tab: (0, g, 0)) for n in planes]
     back_outs = [f32(n, channels_in, LANES) for n in planes]
     held_spec = pl.BlockSpec((in_tiles + 1, rows, LANES), lambda g, tab: (0, g, 0))
@@ -951,16 +968,16 @@
         whole(local_images, 2 * LANES),
         whole(local_images, 3 * LANES),
     ]
-    small = call(
+    small, table = call(
         functools.partial(small_kernel, per_dev),
-        [],
-        pieces,
-        own_specs,
-        [f32(small_rows, LANES)],
-        [whole(small_rows, LANES)],
+        [my_id],
+        [*pieces, jnp.asarray(plan.table)[:, None]],
+        [*own_specs, pl.BlockSpec((None, 1, width), lambda g, tab: (tab[0], 0, 0))],
+        [f32(small_rows, LANES), jax.ShapeDtypeStruct((1, width), jnp.int32)],
+        [whole(small_rows, LANES), whole(1, width)],
         [pltpu.VMEM((LANES, LANES), jnp.float32)],
         1,
-    )[0]
+    )
 
     sends = call(
         functools.partial(pack_kernel, plan),
@@ -996,10 +1013,10 @@
     sends = list(sends)
     cot_halo = [None] * len(sends)
     parts = small[None]
-    rounds = bits_of("chan")
+    rounds = bits_of(CHAN)
     rounds = rounds[:1] + rounds[:0:-1]
     for bit in rounds:
-        got = swap(parts, "chan", bit)
+        got = swap(parts, CHAN, bit)
         if bit == 1:
             got, sends = tied(got, sends)
         elif bit == rounds[-1]:
@@ -1009,16 +1026,16 @@
         parts = jnp.concatenate([parts, got], axis=0)
         if bit == 1:
             parts, sends = tied(parts, sends)
-            for n, op in enumerate(plan["ops"]):
-                if op["near"]:
-                    cot_halo[n] = lax.ppermute(sends[n], "chan", op["pairs"])
+            for n, op in enumerate(plan.ops):
+                if op.near:
+                    cot_halo[n] = lax.ppermute(sends[n], CHAN, op.pairs)
     parts, sends = tied(parts, sends)
-    near = [n for n, op in enumerate(plan["ops"]) if op["near"]]
+    near = [n for n, op in enumerate(plan.ops) if op.near]
     if near:
         cot_halo[near[0]], sends = tied(cot_halo[near[0]], sends)
-    for n, op in enumerate(plan["ops"]):
-        if not op["near"]:
-            cot_halo[n] = lax.ppermute(sends[n], "chan", op["pairs"])
+    for n, op in enumerate(plan.ops):
+        if not op.near:
+            cot_halo[n] = lax.ppermute(sends[n], CHAN, op.pairs)
     padded = round_up(channels, LANES)
     wide, turned, class_out, class_grad, grad_h, weight_norms = call(
         functools.partial(spread_kernel, groups, per_dev, rounds),
@@ -1057,15 +1074,15 @@
         [held_spec, w_spec],
         back_outs,
         back_specs,
-        [pltpu.VMEM((plan["most"] + 1, 2, UNIT, LANES), jnp.float32)],
+        [pltpu.VMEM((plan.most + 1, 2, UNIT, LANES), jnp.float32)],
         steps,
         tight=True,
     )
     partials, late = list(partials), []
     pooled_halo = [None] * len(partials)
-    for n, op in enumerate(plan["back_ops"]):
-        if op["early"]:
-            pooled_halo[n] = lax.ppermute(partials[n], "chan", op["pairs"])
+    for n, op in enumerate(plan.back_ops):
+        if op.early:
+            pooled_halo[n] = lax.ppermute(partials[n], CHAN, op.pairs)
         else:
             late.append(n)
     grad_h = sum_over(grad_h, "dp")
@@ -1095,8 +1112,8 @@
         (waiting, cot_halo, pooled_own, norms)
     )
     for n, v in zip(late, waiting):
-        pooled_halo[n] = lax.ppermute(v, "chan", plan["back_ops"][n]["pairs"])
-    cots_held = pltpu.VMEM((tiles + plan["halo"] + 1, 2, UNIT, LANES), jnp.float32)
+        pooled_halo[n] = lax.ppermute(v, CHAN, plan.back_ops[n].pairs)
+    cots_held = pltpu.VMEM((tiles + plan.halo + 1, 2, UNIT, LANES), jnp.float32)
     sums = call(
         functools.partial(weights_kernel, plan),
         [table],
@@ -1131,13 +1148,13 @@
         [own_spec, *back_specs],
         [f32(channels, n_out)],
         [cot_spec],
-        [cot_held, pltpu.VMEM((plan["back_halo"] + 1, 2 * UNIT, LANES), jnp.float32)],
+        [cot_held, pltpu.VMEM((plan.back_halo + 1, 2 * UNIT, LANES), jnp.float32)],
         steps,
         tight=True,
     )[0]
-    for bit in bits_of("chan")[::-1]:
-        got = swap(sums, "chan", bit)
-        if bit == bits_of("chan")[-1]:
+    for bit in bits_of(CHAN)[::-1]:
+        got = swap(sums, CHAN, bit)
+        if bit == bits_of(CHAN)[-1]:
             got, (x_grad,) = tied(got, [x_grad])
         if bit == 1:
             got, (pooled,) = tied(got, [pooled])
@@ -1191,52 +1208,54 @@
 
 
 def solution(mesh):
+    by_row, by_column = P("dp", CHAN, None), P(None, CHAN)
+    by_channel, by_name = P(CHAN, None), P(CHAN)
     return jax.shard_map(
         per_device,
         mesh=mesh,
         in_specs=(
-            P("dp", "chan", None),
-            P("dp", "chan", None),
-            P("chan", None),
-            P("chan"),
-            P(None, "chan"),
-            P("chan"),
-            P("chan", None),
-            P("chan"),
-            P(None, "chan"),
-            P("chan"),
-            P("chan", None),
-            P("chan"),
-            P(None, "chan"),
-            P("chan"),
-            P("chan", None),
-            P("chan"),
-            P(None, "chan"),
-            P("chan"),
-            P("dp", "chan", None),
-            P("dp", "chan", None),
+            by_row,
+            by_row,
+            by_channel,
+            by_name,
+            by_column,
+            by_name,
+            by_channel,
+            by_name,
+            by_column,
+            by_name,
+            by_channel,
+            by_name,
+            by_column,
+            by_name,
+            by_channel,
+            by_name,
+            by_column,
+            by_name,
+            by_row,
+            by_row,
         ),
         out_specs=(
-            P("dp", "chan", None),
-            P("dp", "chan", None),
-            P("dp", "chan", None),
-            P("dp", "chan", None),
-            P("chan", None),
-            P("chan", None),
-            P("chan", None),
-            P("chan", None),
-            P("chan"),
-            P("chan"),
-            P("chan"),
-            P("chan"),
-            P(None, "chan"),
-            P(None, "chan"),
-            P(None, "chan"),
-            P(None, "chan"),
-            P("chan"),
-            P("chan"),
-            P("chan"),
-            P("chan"),
+            by_row,
+            by_row,
+            by_row,
+            by_row,
+            by_channel,
+            by_channel,
+            by_channel,
+            by_channel,
+            by_name,
+            by_name,
+            by_name,
+            by_name,
+            by_column,
+            by_column,
+            by_column,
+            by_column,
+            by_name,
+            by_name,
+            by_name,
+            by_name,
             P(),
         ),
         check_vma=False,

time: 126 us -> 125 us (level)
  local copies, waits for them, and re-layouts: 5.45 us -> 4.08 us
    dynamic_slice x1 -> x0, local copies, waits for them, and re-layouts: 1.36 us -> none  [per_device(): lax.dynamic_index_in_dim(jnp.asarray(plan['table']), me, 0, keepdims=False)]
  transfers between devices with their start and end apart: 16 -> 16, of which waited for: 7 -> 7; matrix products, arithmetic and copies ran while one was open for 6% -> 5% of each run, Pallas kernels for 48% -> 49%
where the time goes in v5:
time: 125 us; the launch traced here: 123 us
  Pallas kernels  63.1 us (50%)
  starting transfers between devices  29.7 us (24%)
  waiting for transfers between devices  18.6 us (15%)
  other arithmetic  6.19 us (5%)
  local copies, waits for them, and re-layouts  4.08 us (3%)
    pallas_call x11, Pallas kernels, call(): pl.pallas_call(kernel, grid_spec=pltpu.PrefetchScalarGridSpec(num_scalar_...  63.1 us
    ppermute x10, starting transfers between devices, swap(): return lax.ppermute(x, axis, [(k, k ^ bit) for k in range(size)])  16.1 us
    ppermute x1, waiting for transfers between devices, per_device(): pooled_halo[n] = lax.ppermute(partials[n], CHAN, op.pairs)  6.7 us
    ppermute x10, waiting for transfers between devices, swap(): return lax.ppermute(x, axis, [(k, k ^ bit) for k in range(size)])  6.58 us
    ppermute x3, starting transfers between devices, per_device(): cot_halo[n] = lax.ppermute(sends[n], CHAN, op.pairs)  6.01 us
    ppermute x3, waiting for transfers between devices, per_device(): cot_halo[n] = lax.ppermute(sends[n], CHAN, op.pairs)  5.33 us
    ppermute x1, starting transfers between devices, per_device(): pooled_halo[n] = lax.ppermute(partials[n], CHAN, op.pairs)  4.4 us
    unnamed x30, local copies, waits for them, and re-layouts  3.91 us
  transfers between devices with their start and end apart: 16, of which 7 were waited for; matrix products, arithmetic and copies ran while one was open for 5% of the time, Pallas kernels for 49%

profile of v5, /device:TPU:9, one launch (start us, length us, event | category | flops | bytes accessed | tf_op | source)
XLA Modules:
  0.0 122.6 jit_solution(13030458415453385497)
XLA Ops:
  0.7 1.6 %shard_map.364 = (f32[144,128]{1,0:T(8,128)}, s32[1,916]{1,0:T(1,128)}) custom-call(s32[1]{0:T(128)} %bitcast.me, f32[9,36]{1,0:T(8,128)} %bitcast.73, f32[1,36]{1,0:T(1,128)} %bitcast.82, f32[9,36]{1,0:T(8,128)} %bitcast.75, f32[1,36]{1,0:T(1,128)} %bitcast.84, f32[9,36]{1,0:T(8,128)} %bitcast.77, f32[1,36]{1,0:T(1,128)} %bitcast.86, f32[1,36]{1,0:T(1,128)} %bitcast.80, ...), custom_call_target="tpu_custom_call" | custom-call | flops 1 | bytes 1 | tf_op jit(solution)/shard_map/pallas_call | solution.py:831
  2.3 1.2 %collective-permute-start = (f32[1,144,128]{2,1,0:T(8,128)}, f32[1,144,128]{2,1,0:T(8,128)S(1)}, u32[]{:S(2)}, u32[]{:S(2)}) collective-permute-start(f32[1,144,128]{2,1,0:T(8,128)} %bitcast.66), channel_id=1, source_target_pairs={{0,1},{1,0},{2,3},{3,2},{4,5},{5,4},{6,7},{7,6},{8,9},{9,8},{10,11... | collective-permute-start | bytes 221192 | tf_op jit(solution)/shard_map/ppermute | solution.py:864
  3.5 6.2 %shard_map.365 = (f32[11,144,128]{2,1,0:T(8,128)}, f32[10,144,128]{2,1,0:T(8,128)}, f32[15,144,128]{2,1,0:T(8,128)}) custom-call(s32[1,916]{1,0:T(1,128)} %get-tuple-element.76.tab, f32[288,3136]{1,0:T(8,128)} %bitcast.59, f32[144,128]{1,0:T(8,128)} %get-tuple-element.77.refs_1_), custom_call_target="tpu_custom_call" | custom-call | flops 1 | bytes 1 | tf_op jit(solution)/shard_map/pallas_call | solution.py:831
  9.7 0.0 collective-permute-done
  9.7 0.0 copy-done.6
  9.7 0.3 collective-permute-start.3
  10.0 2.3 %collective-permute-start.1 = (f32[2,144,128]{2,1,0:T(8,128)S(1)}, f32[2,144,128]{2,1,0:T(8,128)S(1)}, u32[]{:S(2)}, u32[]{:S(2)}) collective-permute-start(f32[2,144,128]{2,1,0:T(8,128)S(1)} %pad_maximum_fusion.2), channel_id=1, source_target_pairs={{0,4},{1,5},{2,6},{3,7},{4,0},{5,1},{6,2},{7,3},{8,12},{9,13},{10,... | collective-permute-start | bytes 442376 | tf_op jit(solution)/shard_map/ppermute | solution.py:864
  12.3 6.4 %shard_map.366.refs_1_.refs_0_ = f32[25,2,144,128]{3,2,1,0:T(8,128)} custom-call(s32[1,916]{1,0:T(1,128)} %get-tuple-element.76.tab, f32[288,3136]{1,0:T(8,128)} %bitcast.60, f32[11,144,128]{2,1,0:T(8,128)} %get-tuple-element.89.refs_1_), custom_call_target="tpu_custom_call" | custom-call | flops 1 | bytes 1 | tf_op jit(solution)/shard_map/pallas_call | solution.py:831
  18.7 0.2 collective-permute-done.1
  18.9 0.1 collective-permute-start.2
  19.0 0.0 copy-start.12
  19.0 8.8 %shard_map.367.after.refs_0_ = f32[93,144,128]{2,1,0:T(8,128)} custom-call(s32[1,916]{1,0:T(1,128)} %get-tuple-element.76.tab, f32[144,11664]{1,0:T(8,128)} %bitcast.61, f32[25,2,144,128]{3,2,1,0:T(8,128)} %shard_map.366.refs_1_.refs_0_), custom_call_target="tpu_custom_call" | custom-call | flops 1 | bytes 1 | tf_op jit(solution)/shard_map/pallas_call | solution.py:831
  27.8 0.0 collective-permute-done.2
  27.8 0.9 pad_maximum_fusion.parts
  28.7 0.0 collective-permute-done.3.refs_2_.refs_3_
  28.7 0.0 copy-done.12
  28.7 4.4 %collective-permute-start.5 = (f32[15,144,128]{2,1,0:T(8,128)S(1)}, f32[15,144,128]{2,1,0:T(8,128)S(1)}, u32[]{:S(2)}, u32[]{:S(2)}) collective-permute-start(f32[15,144,128]{2,1,0:T(8,128)S(1)} %copy-done.12), channel_id=1, source_target_pairs={{3,4},{4,3},{1,2},{2,1},{5,6},{6,5},{11,12},{12,11},{9,10},{10,9},... | collective-permute-start | bytes 3317768 | tf_op jit(solution)/shard_map/ppermute | solution.py:1038
  33.1 1.3 %collective-permute-start.4 = (f32[10,144,128]{2,1,0:T(8,128)}, f32[10,144,128]{2,1,0:T(8,128)S(1)}, u32[]{:S(2)}, u32[]{:S(2)}) collective-permute-start(f32[10,144,128]{2,1,0:T(8,128)} %get-tuple-element.90), channel_id=1, source_target_pairs={{3,2},{4,5},{1,0},{6,7},{11,10},{12,13},{9,8},{14,15},{19,18},{20,... | collective-permute-start | bytes 2211848 | tf_op jit(solution)/shard_map/ppermute | solution.py:1031
  34.4 2.9 %shard_map.368 = (f32[288,128]{1,0:T(8,128)}, f32[128,384]{1,0:T(8,128)}, f32[16,288]{1,0:T(8,128)}, f32[16,144]{1,0:T(8,128)}, f32[40,256]{1,0:T(8,128)}, /*index=5*/f32[8,128]{1,0:T(8,128)}) custom-call(s32[1]{0:T(128)} %bitcast.me, f32[8,144,128]{2,1,0:T(8,128)} %pad_maximum_fusion.parts, f32[16,144]{1,0:T(8,128)} %bitcast.71, f32[16,288]{1,0:T(8,128)} %bitcast.69, ...), custom_call_target="tpu_custom_call" | custom-call | flops 1 | bytes 1 | tf_op jit(solution)/shard_map/pallas_call | solution.py:831
  37.4 1.3 %collective-permute-start.6 = (f32[40,256]{1,0:T(8,128)}, f32[40,256]{1,0:T(8,128)S(1)}, u32[]{:S(2)}, u32[]{:S(2)}) collective-permute-start(f32[40,256]{1,0:T(8,128)} %get-tuple-element.99), channel_id=1, source_target_pairs={{0,16},{8,24},{16,0},{24,8},{1,17},{9,25},{17,1},{25,9},{2,18},{10... | collective-permute-start | bytes 122888 | tf_op jit(solution)/shard_map/ppermute | solution.py:864
  38.6 2.1 %collective-permute-done.6 = f32[40,256]{1,0:T(8,128)S(1)} collective-permute-done((f32[40,256]{1,0:T(8,128)}, f32[40,256]{1,0:T(8,128)S(1)}, u32[]{:S(2)}, u32[]{:S(2)}) %collective-permute-start.6) | collective-permute-done | bytes 40992 | tf_op jit(solution)/shard_map/ppermute | solution.py:864
  40.8 0.8 add.51
  41.6 2.8 %collective-permute-start.7 = (f32[40,256]{1,0:T(8,128)S(1)}, f32[40,256]{1,0:T(8,128)S(1)}, u32[]{:S(2)}, u32[]{:S(2)}) collective-permute-start(f32[40,256]{1,0:T(8,128)S(1)} %add.51), channel_id=1, source_target_pairs={{0,8},{8,0},{16,24},{24,16},{1,9},{9,1},{17,25},{25,17},{2,10},{10... | collective-permute-start | bytes 122888 | tf_op jit(solution)/shard_map/ppermute | solution.py:864
  44.4 0.0 copy-done.4
  44.4 2.9 %copy-done = f32[93,144,128]{2,1,0:T(8,128)S(1)} copy-done((f32[93,144,128]{2,1,0:T(8,128)S(1)}, f32[93,144,128]{2,1,0:T(8,128)}, u32[]{:S(2)}) %copy-start) | copy-done | bytes 6856728
  47.3 0.9 copy-done.2
  48.2 6.0 %shard_map.369 = (f32[21,144,128]{2,1,0:T(8,128)S(1)}, f32[15,144,128]{2,1,0:T(8,128)S(1)}, f32[7,144,128]{2,1,0:T(8,128)S(1)}) custom-call(s32[1,916]{1,0:T(1,128)S(1)} %copy-done.4, f32[93,144,128]{2,1,0:T(8,128)S(1)} %copy-done, f32[288,128]{1,0:T(8,128)S(1)} %copy-done.2), custom_call_target="tpu_custom_call" | custom-call | flops 1 | bytes 1 | tf_op jit(solution)/shard_map/pallas_call | solution.py:831
  54.2 4.4 %collective-permute-start.13 = (f32[21,144,128]{2,1,0:T(8,128)S(1)}, f32[21,144,128]{2,1,0:T(8,128)S(1)}, u32[]{:S(2)}, u32[]{:S(2)}) collective-permute-start(f32[21,144,128]{2,1,0:T(8,128)S(1)} %get-tuple-element.108), channel_id=1, source_target_pairs={{2,3},{5,4},{0,1},{7,6},{1,0},{6,7},{10,11},{13,12},{8,9},{15,14},... | collective-permute-start | bytes 4644872 | tf_op jit(solution)/shard_map/ppermute | solution.py:1085
  58.6 0.0 collective-permute-done.7
  58.6 0.0 copy-done.5
  58.6 0.0 copy-done.7
  58.7 1.3 %multiply_reduce_fusion = (f32[]{:T(128)}, f32[36,144]{1,0:T(8,128)S(1)}, f32[144,36]{0,1:T(8,128)}, f32[144,36]{0,1:T(8,128)}) fusion(f32[144,36]{0,1:T(8,128)S(1)} %copy-done.5, f32[144,36]{0,1:T(8,128)S(1)} %copy-done.7, f32[40,256]{1,0:T(8,128)S(1)} %add.52, f32[144,36]{0,1:T(8,128)S(1)} %copy-done.8), kind=kLoop, calls=%fused_computation.6 | loop fusion | flops 77759 | bytes 145156 | tf_op jit(solution)/shard_map/reduce_sum | solution.py:1096
  59.9 0.0 copy-start.1
  59.9 7.1 %shard_map.370.refs_0_ = f32[25,288,128]{2,1,0:T(8,128)S(1)} custom-call(s32[1,916]{1,0:T(1,128)S(1)} %copy-done.4, f32[93,144,128]{2,1,0:T(8,128)S(1)} %copy-done, f32[288,128]{1,0:T(8,128)S(1)} %copy-done.2, f32[36,144]{1,0:T(8,128)S(1)} %get-tuple-element.136.refs_2_.hu), custom_call_target="tpu_custom_call" | custom-call | flops 1 | bytes 1 | tf_op jit(solution)/shard_map/pallas_call | solution.py:831
  67.1 0.2 slice_reduce_fusion
  67.2 0.0 copy-done.10
  67.3 0.0 copy-done.11
  67.3 1.2 multiply_reduce_fusion.1
  68.4 5.3 %collective-permute-done.4.refs_3_.refs_4_ = f32[10,144,128]{2,1,0:T(8,128)S(1)} collective-permute-done((f32[10,144,128]{2,1,0:T(8,128)}, f32[10,144,128]{2,1,0:T(8,128)S(1)}, u32[]{:S(2)}, u32[]{:S(2)}) %collective-permute-start.4) | collective-permute-done | bytes 737312 | tf_op jit(solution)/shard_map/ppermute | solution.py:1031
  73.8 0.0 collective-permute-done.5.refs_4_.refs_5_
  73.8 1.9 %collective-permute-start.14 = (f32[15,144,128]{2,1,0:T(8,128)S(1)}, f32[15,144,128]{2,1,0:T(8,128)S(1)}, u32[]{:S(2)}, u32[]{:S(2)}) collective-permute-start(f32[15,144,128]{2,1,0:T(8,128)S(1)} %get-tuple-element.109), channel_id=1, source_target_pairs={{3,4},{4,3},{1,2},{2,1},{5,6},{6,5},{11,12},{12,11},{9,10},{10,9},... | collective-permute-start | bytes 3317768 | tf_op jit(solution)/shard_map/ppermute | solution.py:1115
  75.7 0.0 slice-done
  75.7 0.0 slice-done.1
  75.7 0.0 copy-done.1
  75.7 6.3 %shard_map.371.refs_2_ = f32[16,384]{1,0:T(8,128)S(1)} custom-call(s32[1,916]{1,0:T(1,128)S(1)} %copy-done.4, f32[93,144,128]{2,1,0:T(8,128)S(1)} %bitcast.58, f32[25,2,144,128]{3,2,1,0:T(8,128)S(1)} %copy-done.1, f32[11,144,128]{2,1,0:T(8,128)S(1)} %collective-permute-done.3.refs_2_.refs_3_, f32[10,144,128]{2,1,0:T(8,128)S(1)} %collective-permute-done.4.refs_3_.refs_4_, ...), custom_call_target="tpu_custom_call" | custom-call | flops 1 | bytes 1 | tf_op jit(solution)/shard_map/pallas_call | solution.py:831
  82.1 1.3 %collective-permute-start.8 = (f32[16,384]{1,0:T(8,128)S(1)}, f32[16,384]{1,0:T(8,128)S(1)}, u32[]{:S(2)}, u32[]{:S(2)}) collective-permute-start(f32[16,384]{1,0:T(8,128)S(1)} %shard_map.371.refs_2_), channel_id=1, source_target_pairs={{0,16},{8,24},{16,0},{24,8},{1,17},{9,25},{17,1},{25,9},{2,18},{10... | collective-permute-start | bytes 73736 | tf_op jit(solution)/shard_map/ppermute | solution.py:864
  83.3 1.3 %collective-permute-start.15 = (f32[7,144,128]{2,1,0:T(8,128)S(1)}, f32[7,144,128]{2,1,0:T(8,128)S(1)}, u32[]{:S(2)}, u32[]{:S(2)}) collective-permute-start(f32[7,144,128]{2,1,0:T(8,128)S(1)} %get-tuple-element.110), channel_id=1, source_target_pairs={{3,2},{4,5},{11,10},{12,13},{19,18},{20,21},{27,26},{28,29}} | collective-permute-start | bytes 1548296 | tf_op jit(solution)/shard_map/ppermute | solution.py:1115
  84.6 0.5 collective-permute-done.8
  85.1 1.3 %collective-permute-start.9 = (f32[16,384]{1,0:T(8,128)S(1)}, f32[16,384]{1,0:T(8,128)S(1)}, u32[]{:S(2)}, u32[]{:S(2)}) collective-permute-start(f32[16,384]{1,0:T(8,128)S(1)} %add.63), channel_id=1, source_target_pairs={{0,8},{8,0},{16,24},{24,16},{1,9},{9,1},{17,25},{25,17},{2,10},{10... | collective-permute-start | bytes 73736 | tf_op jit(solution)/shard_map/ppermute | solution.py:864
  86.5 0.8 collective-permute-done.9
  87.3 1.4 %select_select_fusion = f32[16,384]{1,0:T(8,128)S(1)} fusion(f32[16,384]{1,0:T(8,128)S(1)} %add.63, f32[16,384]{1,0:T(8,128)S(1)} %collective-permute-done.9, f32[]{:T(128)} %get-tuple-element.101, f32[]{:T(128)} %get-tuple-element.100, pred[384]{0:T(512)(128)(4,1)S(1)} %get-tuple-element.139, pred[384]{0:T(512)(128)(4,1)S(1)} %get-tuple-element.140, ...), kind=kLoop, calls=%fused_computation.8 | loop fusion | flops 30720 | bytes 74520 | tf_op jit(solution)/shard_map/jit(_where)/select_n | solution.py:1143
  88.7 5.7 %collective-permute-start.10 = (f32[16,384]{1,0:T(8,128)S(1)}, f32[16,384]{1,0:T(8,128)S(1)}, u32[]{:S(2)}, u32[]{:S(2)}) collective-permute-start(f32[16,384]{1,0:T(8,128)S(1)} %select_select_fusion), channel_id=1, source_target_pairs={{0,4},{1,5},{2,6},{3,7},{4,0},{5,1},{6,2},{7,3},{8,12},{9,13},{10,... | collective-permute-start | bytes 73736 | tf_op jit(solution)/shard_map/ppermute | solution.py:864
  94.4 11.3 %shard_map.372 = f32[144,11664]{1,0:T(8,128)} custom-call(s32[1,916]{1,0:T(1,128)S(1)} %copy-done.4, f32[25,2,144,128]{3,2,1,0:T(8,128)S(1)} %copy-done.1, f32[288,128]{1,0:T(8,128)S(1)} %copy-done.2, f32[16,384]{1,0:T(8,128)S(1)} %shard_map.371.refs_2_, f32[11,144,128]{2,1,0:T(8,128)S(1)} %collective-permute-done.3.refs_2_.refs_3_, ...), custom_call_target="tpu_custom_call" | custom-call | flops 1 | bytes 1 | tf_op jit(solution)/shard_map/pallas_call | solution.py:831
  105.7 0.0 collective-permute-done.10
  105.7 0.1 collective-permute-start.11
  105.8 3.0 %collective-permute-done.11 = f32[16,384]{1,0:T(8,128)S(1)} collective-permute-done((f32[16,384]{1,0:T(8,128)S(1)}, f32[16,384]{1,0:T(8,128)S(1)}, u32[]{:S(2)}, u32[]{:S(2)}) %collective-permute-start.11) | collective-permute-done | bytes 24608 | tf_op jit(solution)/shard_map/ppermute | solution.py:864
  108.8 0.0 collective-permute-start.12
  108.8 6.7 %collective-permute-done.13.refs_1_ = f32[21,144,128]{2,1,0:T(8,128)S(1)} collective-permute-done((f32[21,144,128]{2,1,0:T(8,128)S(1)}, f32[21,144,128]{2,1,0:T(8,128)S(1)}, u32[]{:S(2)}, u32[]{:S(2)}) %collective-permute-start.13) | collective-permute-done | bytes 1548320 | tf_op jit(solution)/shard_map/ppermute | solution.py:1085
  115.5 0.0 collective-permute-done.15.refs_3_
  115.5 0.0 collective-permute-done.14.refs_2_
  115.5 4.5 %shard_map.373 = f32[288,3136]{1,0:T(8,128)} custom-call(s32[1,916]{1,0:T(1,128)S(1)} %copy-done.4, f32[25,288,128]{2,1,0:T(8,128)S(1)} %shard_map.370.refs_0_, f32[21,144,128]{2,1,0:T(8,128)S(1)} %collective-permute-done.13.refs_1_, f32[15,144,128]{2,1,0:T(8,128)S(1)} %collective-permute-done.14.refs_2_, f32[7,144,128]{2,1,0:T(8,128)S(1)} %collective-permute-done.15.refs_3_), custom_call_target="tpu_custom_call" | custom-call | flops 1 | bytes 1 | tf_op jit(solution)/shard_map/pallas_call | solution.py:831
  120.0 0.0 collective-permute-done.12
  120.0 0.6 add.67.sums
  120.6 2.0 %shard_map.374 = (f32[9,36]{1,0:T(8,128)}, f32[9,36]{1,0:T(8,128)}, f32[9,36]{1,0:T(8,128)}, f32[9,36]{1,0:T(8,128)}, f32[36,144]{1,0:T(8,128)}, /*index=5*/f32[...) custom-call(s32[1]{0:T(128)} %bitcast.me, ...), custom_call_target="tpu_custom_call" | custom-call | flops 1 | bytes 1 | tf_op jit(solution)/shard_map/pallas_call | solution.py:831
  (25 shorter events, 0.1 us)
Async XLA Ops:
  2.3 7.4 %copy-start.6 = (f32[144,128]{1,0:T(8,128)S(1)}, f32[144,128]{1,0:T(8,128)}, u32[]{:S(2)}) copy-start(f32[144,128]{1,0:T(8,128)} %get-tuple-element.77.refs_1_) | copy-start | bytes 221188
  2.3 7.4 %collective-permute-start = (f32[1,144,128]{2,1,0:T(8,128)}, f32[1,144,128]{2,1,0:T(8,128)S(1)}, u32[]{:S(2)}, u32[]{:S(2)}) collective-permute-start(f32[1,144,128]{2,1,0:T(8,128)} %bitcast.66), channel_id=1, source_target_pairs={{0,1},{1,0},{2,3},{3,2},{4,5},{5,4},{6,7},{7,6},{8,9},{9,8},{10,11... | collective-permute-start | bytes 221192 | tf_op jit(solution)/shard_map/ppermute | solution.py:864
  9.7 19.0 %collective-permute-start.3 = (f32[11,144,128]{2,1,0:T(8,128)}, f32[11,144,128]{2,1,0:T(8,128)S(1)}, u32[]{:S(2)}, u32[]{:S(2)}) collective-permute-start(f32[11,144,128]{2,1,0:T(8,128)} %get-tuple-element.89.refs_1_), channel_id=1, source_target_pairs={{0,1},{1,0},{3,2},{4,5},{6,7},{7,6},{2,3},{5,4},{8,9},{9,8},{11,10... | collective-permute-start | bytes 2433032 | tf_op jit(solution)/shard_map/ppermute | solution.py:1031
  10.0 8.9 %collective-permute-start.1 = (f32[2,144,128]{2,1,0:T(8,128)S(1)}, f32[2,144,128]{2,1,0:T(8,128)S(1)}, u32[]{:S(2)}, u32[]{:S(2)}) collective-permute-start(f32[2,144,128]{2,1,0:T(8,128)S(1)} %pad_maximum_fusion.2), channel_id=1, source_target_pairs={{0,4},{1,5},{2,6},{3,7},{4,0},{5,1},{6,2},{7,3},{8,12},{9,13},{10,... | collective-permute-start | bytes 442376 | tf_op jit(solution)/shard_map/ppermute | solution.py:864
  18.9 8.9 %collective-permute-start.2 = (f32[4,144,128]{2,1,0:T(8,128)S(1)}, f32[4,144,128]{2,1,0:T(8,128)S(1)}, u32[]{:S(2)}, u32[]{:S(2)}) collective-permute-start(f32[4,144,128]{2,1,0:T(8,128)S(1)} %pad_maximum_fusion.1), channel_id=1, source_target_pairs={{0,2},{1,3},{2,0},{3,1},{4,6},{5,7},{6,4},{7,5},{8,10},{9,11},{10,... | collective-permute-start | bytes 884744 | tf_op jit(solution)/shard_map/ppermute | solution.py:864
  19.0 9.7 %copy-start.12 = (f32[15,144,128]{2,1,0:T(8,128)S(1)}, f32[15,144,128]{2,1,0:T(8,128)}, u32[]{:S(2)}) copy-start(f32[15,144,128]{2,1,0:T(8,128)} %get-tuple-element.98) | copy-start | bytes 3317764
  28.7 15.7 %copy-start.4 = (s32[1,916]{1,0:T(1,128)S(1)}, s32[1,916]{1,0:T(1,128)}, u32[]{:S(2)}) copy-start(s32[1,916]{1,0:T(1,128)} %get-tuple-element.76.tab) | copy-start | bytes 10996
  28.7 45.1 %collective-permute-start.5 = (f32[15,144,128]{2,1,0:T(8,128)S(1)}, f32[15,144,128]{2,1,0:T(8,128)S(1)}, u32[]{:S(2)}, u32[]{:S(2)}) collective-permute-start(f32[15,144,128]{2,1,0:T(8,128)S(1)} %copy-done.12), channel_id=1, source_target_pairs={{3,4},{4,3},{1,2},{2,1},{5,6},{6,5},{11,12},{12,11},{9,10},{10,9},... | collective-permute-start | bytes 3317768 | tf_op jit(solution)/shard_map/ppermute | solution.py:1038
  33.1 40.6 %collective-permute-start.4 = (f32[10,144,128]{2,1,0:T(8,128)}, f32[10,144,128]{2,1,0:T(8,128)S(1)}, u32[]{:S(2)}, u32[]{:S(2)}) collective-permute-start(f32[10,144,128]{2,1,0:T(8,128)} %get-tuple-element.90), channel_id=1, source_target_pairs={{3,2},{4,5},{1,0},{6,7},{11,10},{12,13},{9,8},{14,15},{19,18},{20,... | collective-permute-start | bytes 2211848 | tf_op jit(solution)/shard_map/ppermute | solution.py:1031
  37.4 21.3 %copy-start.5 = (f32[144,36]{0,1:T(8,128)S(1)}, f32[144,36]{0,1:T(8,128)}, u32[]{:S(2)}) copy-start(f32[144,36]{0,1:T(8,128)} %param.25) | copy-start | bytes 62212
  37.4 21.3 %copy-start.7 = (f32[144,36]{0,1:T(8,128)S(1)}, f32[144,36]{0,1:T(8,128)}, u32[]{:S(2)}) copy-start(f32[144,36]{0,1:T(8,128)} %param.33) | copy-start | bytes 62212
  37.4 21.3 %copy-start.8 = (f32[144,36]{0,1:T(8,128)S(1)}, f32[144,36]{0,1:T(8,128)}, u32[]{:S(2)}) copy-start(f32[144,36]{0,1:T(8,128)} %param.29) | copy-start | bytes 62212
  37.4 3.4 %collective-permute-start.6 = (f32[40,256]{1,0:T(8,128)}, f32[40,256]{1,0:T(8,128)S(1)}, u32[]{:S(2)}, u32[]{:S(2)}) collective-permute-start(f32[40,256]{1,0:T(8,128)} %get-tuple-element.99), channel_id=1, source_target_pairs={{0,16},{8,24},{16,0},{24,8},{1,17},{9,25},{17,1},{25,9},{2,18},{10... | collective-permute-start | bytes 122888 | tf_op jit(solution)/shard_map/ppermute | solution.py:864
  41.6 17.0 %collective-permute-start.7 = (f32[40,256]{1,0:T(8,128)S(1)}, f32[40,256]{1,0:T(8,128)S(1)}, u32[]{:S(2)}, u32[]{:S(2)}) collective-permute-start(f32[40,256]{1,0:T(8,128)S(1)} %add.51), channel_id=1, source_target_pairs={{0,8},{8,0},{16,24},{24,16},{1,9},{9,1},{17,25},{25,17},{2,10},{10... | collective-permute-start | bytes 122888 | tf_op jit(solution)/shard_map/ppermute | solution.py:864
  44.4 2.9 %copy-start = (f32[93,144,128]{2,1,0:T(8,128)S(1)}, f32[93,144,128]{2,1,0:T(8,128)}, u32[]{:S(2)}) copy-start(f32[93,144,128]{2,1,0:T(8,128)} %shard_map.367.after.refs_0_) | copy-start | bytes 20570116
  47.3 0.9 copy-start.2
  48.2 27.5 %slice-start = ((s8[6856704]{0:T(1024)(128)(4,1)}), s8[4194304]{0:T(1024)(128)(4,1)S(1)}, s32[]{:S(2)}) async-start(s8[6856704]{0:T(1024)(128)(4,1)} %bitcast.57), calls=%async_computation | async-start | bytes 8388608
  54.2 61.3 %collective-permute-start.13 = (f32[21,144,128]{2,1,0:T(8,128)S(1)}, f32[21,144,128]{2,1,0:T(8,128)S(1)}, u32[]{:S(2)}, u32[]{:S(2)}) collective-permute-start(f32[21,144,128]{2,1,0:T(8,128)S(1)} %get-tuple-element.108), channel_id=1, source_target_pairs={{2,3},{5,4},{0,1},{7,6},{1,0},{6,7},{10,11},{13,12},{8,9},{15,14},... | collective-permute-start | bytes 4644872 | tf_op jit(solution)/shard_map/ppermute | solution.py:1085
  59.9 7.1 %copy-start.3 = (f32[36,144]{1,0:T(8,128)}, f32[36,144]{1,0:T(8,128)S(1)}, u32[]{:S(2)}) copy-start(f32[36,144]{1,0:T(8,128)S(1)} %get-tuple-element.136.refs_2_.hu) | copy-start | bytes 62212
  59.9 7.3 %copy-start.9 = (f32[36]{0:T(128)S(1)}, f32[36]{0:T(128)}, u32[]{:S(2)}) copy-start(f32[36]{0:T(128)} %param.26) | copy-start | bytes 436
  59.9 7.3 %copy-start.10 = (f32[36]{0:T(128)S(1)}, f32[36]{0:T(128)}, u32[]{:S(2)}) copy-start(f32[36]{0:T(128)} %param.30) | copy-start | bytes 436
  59.9 7.3 %copy-start.11 = (f32[36]{0:T(128)S(1)}, f32[36]{0:T(128)}, u32[]{:S(2)}) copy-start(f32[36]{0:T(128)} %param.34) | copy-start | bytes 436
  59.9 15.8 %slice-start.1 = ((s8[6856704]{0:T(1024)(128)(4,1)}), s8[2662400]{0:T(1024)(128)(4,1)S(1)}, s32[]{:S(2)}) async-start(s8[6856704]{0:T(1024)(128)(4,1)} %bitcast.57), calls=%async_computation.1 | async-start | bytes 5324800
  59.9 15.8 %copy-start.1 = (f32[25,2,144,128]{3,2,1,0:T(8,128)S(1)}, f32[25,2,144,128]{3,2,1,0:T(8,128)}, u32[]{:S(2)}) copy-start(f32[25,2,144,128]{3,2,1,0:T(8,128)} %shard_map.366.refs_1_.refs_0_) | copy-start | bytes 11059204
  73.8 41.7 %collective-permute-start.14 = (f32[15,144,128]{2,1,0:T(8,128)S(1)}, f32[15,144,128]{2,1,0:T(8,128)S(1)}, u32[]{:S(2)}, u32[]{:S(2)}) collective-permute-start(f32[15,144,128]{2,1,0:T(8,128)S(1)} %get-tuple-element.109), channel_id=1, source_target_pairs={{3,4},{4,3},{1,2},{2,1},{5,6},{6,5},{11,12},{12,11},{9,10},{10,9},... | collective-permute-start | bytes 3317768 | tf_op jit(solution)/shard_map/ppermute | solution.py:1115
  82.1 3.0 %collective-permute-start.8 = (f32[16,384]{1,0:T(8,128)S(1)}, f32[16,384]{1,0:T(8,128)S(1)}, u32[]{:S(2)}, u32[]{:S(2)}) collective-permute-start(f32[16,384]{1,0:T(8,128)S(1)} %shard_map.371.refs_2_), channel_id=1, source_target_pairs={{0,16},{8,24},{16,0},{24,8},{1,17},{9,25},{17,1},{25,9},{2,18},{10... | collective-permute-start | bytes 73736 | tf_op jit(solution)/shard_map/ppermute | solution.py:864
  83.3 32.1 %collective-permute-start.15 = (f32[7,144,128]{2,1,0:T(8,128)S(1)}, f32[7,144,128]{2,1,0:T(8,128)S(1)}, u32[]{:S(2)}, u32[]{:S(2)}) collective-permute-start(f32[7,144,128]{2,1,0:T(8,128)S(1)} %get-tuple-element.110), channel_id=1, source_target_pairs={{3,2},{4,5},{11,10},{12,13},{19,18},{20,21},{27,26},{28,29}} | collective-permute-start | bytes 1548296 | tf_op jit(solution)/shard_map/ppermute | solution.py:1115
  85.1 2.2 %collective-permute-start.9 = (f32[16,384]{1,0:T(8,128)S(1)}, f32[16,384]{1,0:T(8,128)S(1)}, u32[]{:S(2)}, u32[]{:S(2)}) collective-permute-start(f32[16,384]{1,0:T(8,128)S(1)} %add.63), channel_id=1, source_target_pairs={{0,8},{8,0},{16,24},{24,16},{1,9},{9,1},{17,25},{25,17},{2,10},{10... | collective-permute-start | bytes 73736 | tf_op jit(solution)/shard_map/ppermute | solution.py:864
  88.7 17.0 %collective-permute-start.10 = (f32[16,384]{1,0:T(8,128)S(1)}, f32[16,384]{1,0:T(8,128)S(1)}, u32[]{:S(2)}, u32[]{:S(2)}) collective-permute-start(f32[16,384]{1,0:T(8,128)S(1)} %select_select_fusion), channel_id=1, source_target_pairs={{0,4},{1,5},{2,6},{3,7},{4,0},{5,1},{6,2},{7,3},{8,12},{9,13},{10,... | collective-permute-start | bytes 73736 | tf_op jit(solution)/shard_map/ppermute | solution.py:864
  105.7 3.0 %collective-permute-start.11 = (f32[16,384]{1,0:T(8,128)S(1)}, f32[16,384]{1,0:T(8,128)S(1)}, u32[]{:S(2)}, u32[]{:S(2)}) collective-permute-start(f32[16,384]{1,0:T(8,128)S(1)} %add.65), channel_id=1, source_target_pairs={{0,2},{1,3},{2,0},{3,1},{4,6},{5,7},{6,4},{7,5},{8,10},{9,11},{10,... | collective-permute-start | bytes 73736 | tf_op jit(solution)/shard_map/ppermute | solution.py:864
  108.8 11.3 %collective-permute-start.12 = (f32[16,384]{1,0:T(8,128)S(1)}, f32[16,384]{1,0:T(8,128)S(1)}, u32[]{:S(2)}, u32[]{:S(2)}) collective-permute-start(f32[16,384]{1,0:T(8,128)S(1)} %add.66), channel_id=1, source_target_pairs={{0,1},{1,0},{2,3},{3,2},{4,5},{5,4},{6,7},{7,6},{8,9},{9,8},{10,11... | collective-permute-start | bytes 73736 | tf_op jit(solution)/shard_map/ppermute | solution.py:864

commit v6 on v5

--- a/solution.py
+++ b/solution.py
@@ -808,6 +808,19 @@
     ha_out[...] = keep_rate * ha[...] + (1.0 - keep_rate) * w_new
 
 
+def last_kernel(plan, channels, per_dev, count, tab, me, own_ref, *refs):
+    n_ops = len(plan.back_sizes)
+    halos, refs = refs[:n_ops], refs[n_ops:]
+    small, refs = refs[:count], refs[count:]
+    out_ref, new, scratch = refs[0], refs[1:-2], refs[-2:]
+
+    @pl.when(pl.program_id(0) == 0)
+    def _():
+        update_kernel(channels, per_dev, me, *small, *new)
+
+    finish_kernel(plan, tab, own_ref, *halos, out_ref, *scratch)
+
+
 class Row:
     def __init__(self, ref):
         self.ref = ref
@@ -933,18 +946,18 @@
     cot = pooled_cot[0].T
     in_lanes, out_lanes = round_up(n_in, LANES), round_up(n_out, LANES)
     rows, wide_rows = UNIT * per, 2 * UNIT * per
-    x_spec = pl.BlockSpec((rows, in_lanes), lambda g, tab: (g, 0))
-    cot_spec = pl.BlockSpec((wide_rows, out_lanes), lambda g, tab: (g, 0))
+    x_spec = pl.BlockSpec((rows, in_lanes), lambda g, *tab: (g, 0))
+    cot_spec = pl.BlockSpec((wide_rows, out_lanes), lambda g, *tab: (g, 0))
     planes = [2 * op.full + op.half for op in plan.ops]
-    halo_specs = [pl.BlockSpec((n, rows, LANES), lambda g, tab: (0, g, 0)) for n in planes]
+    halo_specs = [pl.BlockSpec((n, rows, LANES), lambda g, *tab: (0, g, 0)) for n in planes]
     halo_outs = [f32(n, channels_in, LANES) for n in planes]
     planes = [2 * op.full + op.half for op in plan.back_ops]
-    back_specs = [pl.BlockSpec((n, rows, LANES), lambda g, tab: (0, g, 0)) for n in planes]
+    back_specs = [pl.BlockSpec((n, rows, LANES), lambda g, *tab: (0, g, 0)) for n in planes]
     back_outs = [f32(n, channels_in, LANES) for n in planes]
-    held_spec = pl.BlockSpec((in_tiles + 1, rows, LANES), lambda g, tab: (0, g, 0))
-    split_spec = pl.BlockSpec((tiles, 2, rows, LANES), lambda g, tab: (0, 0, g, 0))
-    own_spec = pl.BlockSpec((tiles, wide_rows, LANES), lambda g, tab: (0, g, 0))
-    w_spec = pl.BlockSpec((wide_rows, LANES), lambda g, tab: (g, 0))
+    held_spec = pl.BlockSpec((in_tiles + 1, rows, LANES), lambda g, *tab: (0, g, 0))
+    split_spec = pl.BlockSpec((tiles, 2, rows, LANES), lambda g, *tab: (0, 0, g, 0))
+    own_spec = pl.BlockSpec((tiles, wide_rows, LANES), lambda g, *tab: (0, g, 0))
+    w_spec = pl.BlockSpec((wide_rows, LANES), lambda g, *tab: (g, 0))
     anywhere = pl.BlockSpec(memory_space=pl.ANY)
     cot_held = pltpu.VMEM((tiles + 1, 2 * UNIT, LANES), jnp.float32)
 
@@ -1141,23 +1154,10 @@
     lane = lax.broadcasted_iota(jnp.int32, sums.shape, 1)
     for k, v in enumerate(norms):
         sums = jnp.where((row == TAPS + 1) & (lane == k), v, sums)
-    pooled = call(
-        functools.partial(finish_kernel, plan),
-        [table],
-        [pooled_own, *pooled_halo],
-        [own_spec, *back_specs],
-        [f32(channels, n_out)],
-        [cot_spec],
-        [cot_held, pltpu.VMEM((plan.back_halo + 1, 2 * UNIT, LANES), jnp.float32)],
-        steps,
-        tight=True,
-    )[0]
     for bit in bits_of(CHAN)[::-1]:
         got = swap(sums, CHAN, bit)
         if bit == bits_of(CHAN)[-1]:
             got, (x_grad,) = tied(got, [x_grad])
-        if bit == 1:
-            got, (pooled,) = tied(got, [pooled])
         sums = sums + got
     conv_shapes = [f32(TAPS, per_dev)] * 4
     head_shapes = [f32(per_dev, channels_in)] * 2
@@ -1177,17 +1177,17 @@
     ]
     specs = [whole(*v.shape) for v in operands]
     out_shapes = [*conv_shapes, *head_shapes, *[f32(per_dev)] * 6, f32(4)]
-    *new, trust = call(
-        functools.partial(update_kernel, channels, per_dev),
-        [my_id],
-        operands,
-        specs,
-        out_shapes,
-        [whole(*v.shape) for v in out_shapes],
-        [],
-        1,
-    )
-
+    pooled, *new, trust = call(
+        functools.partial(last_kernel, plan, channels, per_dev, len(operands)),
+        [table, my_id],
+        [pooled_own, *pooled_halo, *operands],
+        [own_spec, *back_specs, *specs],
+        [f32(channels, n_out), *out_shapes],
+        [cot_spec, *[whole(*v.shape) for v in out_shapes]],
+        [cot_held, pltpu.VMEM((plan.back_halo + 1, 2 * UNIT, LANES), jnp.float32)],
+        steps,
+        tight=True,
+    )
     conv_new, (head_new, head_average), bias_new = new[:4], new[4:6], new[6:]
     return (
         pooled.T[None],

time: 125 us -> 123 us (0.984)
  Pallas kernels: 63.1 us -> 61.2 us
    ppermute x10, waiting for transfers between devices: 6.58 us -> 13.7 us  [swap(): return lax.ppermute(x, axis, [(k, k ^ bit) for k in range(size)])]
    ppermute x1, waiting for transfers between devices: 6.7 us -> 0.01 us  [per_device(): pooled_halo[n] = lax.ppermute(partials[n], CHAN, op.pairs)]
    pallas_call x11 -> x10, Pallas kernels: 63.1 us -> 61.2 us  [call(): pl.pallas_call(kernel, grid_spec=pltpu.PrefetchScalarGridSpec(num_scalar_...]
    unnamed x30 -> x52, local copies, waits for them, and re-layouts: 3.91 us -> 3.97 us
  transfers between devices with their start and end apart: 16 -> 16, of which waited for: 7 -> 7; matrix products, arithmetic and copies ran while one was open for 5% -> 5% of each run, Pallas kernels for 49% -> 45%
where the time goes in v6:
time: 123 us; the launch traced here: 121 us
  Pallas kernels  61.2 us (50%)
  starting transfers between devices  29.8 us (24%)
  waiting for transfers between devices  19.3 us (16%)
  other arithmetic  5.47 us (4%)
  local copies, waits for them, and re-layouts  4.15 us (3%)
    pallas_call x10, Pallas kernels, call(): pl.pallas_call(kernel, grid_spec=pltpu.PrefetchScalarGridSpec(num_scalar_...  61.2 us
    ppermute x10, starting transfers between devices, swap(): return lax.ppermute(x, axis, [(k, k ^ bit) for k in range(size)])  16.2 us
    ppermute x10, waiting for transfers between devices, swap(): return lax.ppermute(x, axis, [(k, k ^ bit) for k in range(size)])  13.7 us
    ppermute x3, starting transfers between devices, per_device(): cot_halo[n] = lax.ppermute(sends[n], CHAN, op.pairs)  6.01 us
    ppermute x3, waiting for transfers between devices, per_device(): cot_halo[n] = lax.ppermute(sends[n], CHAN, op.pairs)  5.61 us
    ppermute x1, starting transfers between devices, per_device(): pooled_halo[n] = lax.ppermute(partials[n], CHAN, op.pairs)  4.41 us
    unnamed x52, local copies, waits for them, and re-layouts  3.97 us
    ppermute x2, starting transfers between devices, per_device(): pooled_halo[n] = lax.ppermute(v, CHAN, plan.back_ops[n].pairs)  3.19 us
  transfers between devices with their start and end apart: 16, of which 7 were waited for; matrix products, arithmetic and copies ran while one was open for 5% of the time, Pallas kernels for 45%

profile of v6, /device:TPU:9, one launch (start us, length us, event | category | flops | bytes accessed | tf_op | source)
XLA Modules:
  0.0 121.0 jit_solution(2316283746556537588)
XLA Ops:
  0.7 1.6 %shard_map.364 = (f32[144,128]{1,0:T(8,128)}, s32[1,916]{1,0:T(1,128)}) custom-call(s32[1]{0:T(128)} %bitcast.me.refs_0_, f32[9,36]{1,0:T(8,128)} %bitcast.62, f32[1,36]{1,0:T(1,128)} %bitcast.71, f32[9,36]{1,0:T(8,128)} %bitcast.64, f32[1,36]{1,0:T(1,128)} %bitcast.73, f32[9,36]{1,0:T(8,128)} %bitcast.66, f32[1,36]{1,0:T(1,128)} %bitcast.75, ...), custom_call_target="tpu_custom_call" | custom-call | flops 1 | bytes 1 | tf_op jit(solution)/shard_map/pallas_call | solution.py:844
  2.3 1.2 %collective-permute-start = (f32[1,144,128]{2,1,0:T(8,128)}, f32[1,144,128]{2,1,0:T(8,128)S(1)}, u32[]{:S(2)}, u32[]{:S(2)}) collective-permute-start(f32[1,144,128]{2,1,0:T(8,128)} %bitcast.84), channel_id=1, source_target_pairs={{0,1},{1,0},{2,3},{3,2},{4,5},{5,4},{6,7},{7,6},{8,9},{9,8},{10,11... | collective-permute-start | bytes 221192 | tf_op jit(solution)/shard_map/ppermute | solution.py:877
  3.5 6.2 %shard_map.365 = (f32[11,144,128]{2,1,0:T(8,128)}, f32[10,144,128]{2,1,0:T(8,128)}, f32[15,144,128]{2,1,0:T(8,128)}) custom-call(s32[1,916]{1,0:T(1,128)} %get-tuple-element.75.tab, f32[288,3136]{1,0:T(8,128)} %bitcast.80, f32[144,128]{1,0:T(8,128)} %get-tuple-element.76.refs_1_), custom_call_target="tpu_custom_call" | custom-call | flops 1 | bytes 1 | tf_op jit(solution)/shard_map/pallas_call | solution.py:844
  9.7 0.0 collective-permute-done
  9.7 0.0 copy-done.18
  9.7 0.3 collective-permute-start.3
  10.0 2.3 %collective-permute-start.1 = (f32[2,144,128]{2,1,0:T(8,128)S(1)}, f32[2,144,128]{2,1,0:T(8,128)S(1)}, u32[]{:S(2)}, u32[]{:S(2)}) collective-permute-start(f32[2,144,128]{2,1,0:T(8,128)S(1)} %pad_maximum_fusion.2), channel_id=1, source_target_pairs={{0,4},{1,5},{2,6},{3,7},{4,0},{5,1},{6,2},{7,3},{8,12},{9,13},{10,... | collective-permute-start | bytes 442376 | tf_op jit(solution)/shard_map/ppermute | solution.py:877
  12.3 6.4 %shard_map.366.refs_1_.refs_0_ = f32[25,2,144,128]{3,2,1,0:T(8,128)} custom-call(s32[1,916]{1,0:T(1,128)} %get-tuple-element.75.tab, f32[288,3136]{1,0:T(8,128)} %bitcast.81, f32[11,144,128]{2,1,0:T(8,128)} %get-tuple-element.88.refs_1_), custom_call_target="tpu_custom_call" | custom-call | flops 1 | bytes 1 | tf_op jit(solution)/shard_map/pallas_call | solution.py:844
  18.7 0.2 collective-permute-done.1
  18.9 0.1 collective-permute-start.2
  19.0 0.0 copy-start.23
  19.0 8.8 %shard_map.367.after.refs_0_ = f32[93,144,128]{2,1,0:T(8,128)} custom-call(s32[1,916]{1,0:T(1,128)} %get-tuple-element.75.tab, f32[144,11664]{1,0:T(8,128)} %bitcast.82, f32[25,2,144,128]{3,2,1,0:T(8,128)} %shard_map.366.refs_1_.refs_0_), custom_call_target="tpu_custom_call" | custom-call | flops 1 | bytes 1 | tf_op jit(solution)/shard_map/pallas_call | solution.py:844
  27.8 0.0 collective-permute-done.2
  27.8 0.9 pad_maximum_fusion.parts
  28.7 0.0 collective-permute-done.3.refs_2_.refs_3_
  28.7 0.0 copy-done.23
  28.7 4.4 %collective-permute-start.5 = (f32[15,144,128]{2,1,0:T(8,128)S(1)}, f32[15,144,128]{2,1,0:T(8,128)S(1)}, u32[]{:S(2)}, u32[]{:S(2)}) collective-permute-start(f32[15,144,128]{2,1,0:T(8,128)S(1)} %copy-done.23), channel_id=1, source_target_pairs={{3,4},{4,3},{1,2},{2,1},{5,6},{6,5},{11,12},{12,11},{9,10},{10,9},... | collective-permute-start | bytes 3317768 | tf_op jit(solution)/shard_map/ppermute | solution.py:1051
  33.1 1.3 %collective-permute-start.4 = (f32[10,144,128]{2,1,0:T(8,128)}, f32[10,144,128]{2,1,0:T(8,128)S(1)}, u32[]{:S(2)}, u32[]{:S(2)}) collective-permute-start(f32[10,144,128]{2,1,0:T(8,128)} %get-tuple-element.89), channel_id=1, source_target_pairs={{3,2},{4,5},{1,0},{6,7},{11,10},{12,13},{9,8},{14,15},{19,18},{20,... | collective-permute-start | bytes 2211848 | tf_op jit(solution)/shard_map/ppermute | solution.py:1044
  34.4 2.9 %shard_map.368 = (f32[288,128]{1,0:T(8,128)}, f32[128,384]{1,0:T(8,128)}, f32[16,288]{1,0:T(8,128)}, f32[16,144]{1,0:T(8,128)}, f32[40,256]{1,0:T(8,128)}, /*index=5*/f32[8,128]{1,0:T(8,128)}) custom-call(s32[1]{0:T(128)} %bitcast.me.refs_0_, f32[8,144,128]{2,1,0:T(8,128)} %pad_maximum_fusion.parts, f32[16,144]{1,0:T(8,128)} %bitcast.89, ...), custom_call_target="tpu_custom_call" | custom-call | flops 1 | bytes 1 | tf_op jit(solution)/shard_map/pallas_call | solution.py:844
  37.4 1.3 %collective-permute-start.6 = (f32[40,256]{1,0:T(8,128)}, f32[40,256]{1,0:T(8,128)S(1)}, u32[]{:S(2)}, u32[]{:S(2)}) collective-permute-start(f32[40,256]{1,0:T(8,128)} %get-tuple-element.98), channel_id=1, source_target_pairs={{0,16},{8,24},{16,0},{24,8},{1,17},{9,25},{17,1},{25,9},{2,18},{10... | collective-permute-start | bytes 122888 | tf_op jit(solution)/shard_map/ppermute | solution.py:877
  38.6 2.1 %collective-permute-done.6 = f32[40,256]{1,0:T(8,128)S(1)} collective-permute-done((f32[40,256]{1,0:T(8,128)}, f32[40,256]{1,0:T(8,128)S(1)}, u32[]{:S(2)}, u32[]{:S(2)}) %collective-permute-start.6) | collective-permute-done | bytes 40992 | tf_op jit(solution)/shard_map/ppermute | solution.py:877
  40.8 0.8 add.51
  41.6 2.8 %collective-permute-start.7 = (f32[40,256]{1,0:T(8,128)S(1)}, f32[40,256]{1,0:T(8,128)S(1)}, u32[]{:S(2)}, u32[]{:S(2)}) collective-permute-start(f32[40,256]{1,0:T(8,128)S(1)} %add.51), channel_id=1, source_target_pairs={{0,8},{8,0},{16,24},{24,16},{1,9},{9,1},{17,25},{25,17},{2,10},{10... | collective-permute-start | bytes 122888 | tf_op jit(solution)/shard_map/ppermute | solution.py:877
  44.3 0.0 copy-done.4
  44.3 2.9 %copy-done = f32[93,144,128]{2,1,0:T(8,128)S(1)} copy-done((f32[93,144,128]{2,1,0:T(8,128)S(1)}, f32[93,144,128]{2,1,0:T(8,128)}, u32[]{:S(2)}) %copy-start) | copy-done | bytes 6856728
  47.3 0.9 copy-done.2
  48.2 5.8 %shard_map.369 = (f32[21,144,128]{2,1,0:T(8,128)S(1)}, f32[15,144,128]{2,1,0:T(8,128)S(1)}, f32[7,144,128]{2,1,0:T(8,128)S(1)}) custom-call(s32[1,916]{1,0:T(1,128)S(1)} %copy-done.4, f32[93,144,128]{2,1,0:T(8,128)S(1)} %copy-done, f32[288,128]{1,0:T(8,128)S(1)} %copy-done.2), custom_call_target="tpu_custom_call" | custom-call | flops 1 | bytes 1 | tf_op jit(solution)/shard_map/pallas_call | solution.py:844
  54.0 4.4 %collective-permute-start.8 = (f32[21,144,128]{2,1,0:T(8,128)S(1)}, f32[21,144,128]{2,1,0:T(8,128)S(1)}, u32[]{:S(2)}, u32[]{:S(2)}) collective-permute-start(f32[21,144,128]{2,1,0:T(8,128)S(1)} %get-tuple-element.100), channel_id=1, source_target_pairs={{2,3},{5,4},{0,1},{7,6},{1,0},{6,7},{10,11},{13,12},{8,9},{15,14},... | collective-permute-start | bytes 4644872 | tf_op jit(solution)/shard_map/ppermute | solution.py:1098
  58.4 0.0 collective-permute-done.7
  58.5 1.3 %multiply_reduce_fusion = (f32[]{:T(128)}, f32[36,144]{1,0:T(8,128)S(1)}, f32[144,36]{0,1:T(8,128)}, f32[144,36]{0,1:T(8,128)}) fusion(f32[144,36]{0,1:T(8,128)S(1)} %copy-done.3, f32[144,36]{0,1:T(8,128)S(1)} %copy-done.19, f32[40,256]{1,0:T(8,128)S(1)} %add.52, f32[144,36]{0,1:T(8,128)S(1)} %copy-done.20), kind=kLoop, calls=%fused_computation.6 | loop fusion | flops 77759 | bytes 145156 | tf_op jit(solution)/shard_map/reduce_sum | solution.py:1109
  59.7 7.1 %shard_map.370.refs_1_ = f32[25,288,128]{2,1,0:T(8,128)S(1)} custom-call(s32[1,916]{1,0:T(1,128)S(1)} %copy-done.4, f32[93,144,128]{2,1,0:T(8,128)S(1)} %copy-done, f32[288,128]{1,0:T(8,128)S(1)} %copy-done.2, f32[36,144]{1,0:T(8,128)S(1)} %get-tuple-element.134.refs_2_.refs_17_), custom_call_target="tpu_custom_call" | custom-call | flops 1 | bytes 1 | tf_op jit(solution)/shard_map/pallas_call | solution.py:844
  66.8 0.2 slice_reduce_fusion
  67.0 1.1 multiply_reduce_fusion.1
  68.2 5.6 %collective-permute-done.4.refs_3_.refs_4_ = f32[10,144,128]{2,1,0:T(8,128)S(1)} collective-permute-done((f32[10,144,128]{2,1,0:T(8,128)}, f32[10,144,128]{2,1,0:T(8,128)S(1)}, u32[]{:S(2)}, u32[]{:S(2)}) %collective-permute-start.4) | collective-permute-done | bytes 737312 | tf_op jit(solution)/shard_map/ppermute | solution.py:1044
  73.8 0.0 collective-permute-done.5.refs_4_.refs_5_
  73.8 1.9 %collective-permute-start.9 = (f32[15,144,128]{2,1,0:T(8,128)S(1)}, f32[15,144,128]{2,1,0:T(8,128)S(1)}, u32[]{:S(2)}, u32[]{:S(2)}) collective-permute-start(f32[15,144,128]{2,1,0:T(8,128)S(1)} %get-tuple-element.101), channel_id=1, source_target_pairs={{3,4},{4,3},{1,2},{2,1},{5,6},{6,5},{11,12},{12,11},{9,10},{10,9},... | collective-permute-start | bytes 3317768 | tf_op jit(solution)/shard_map/ppermute | solution.py:1128
  75.7 6.3 %shard_map.371.refs_2_ = f32[16,384]{1,0:T(8,128)S(1)} custom-call(s32[1,916]{1,0:T(1,128)S(1)} %copy-done.4, f32[93,144,128]{2,1,0:T(8,128)S(1)} %bitcast.58, f32[25,2,144,128]{3,2,1,0:T(8,128)S(1)} %copy-done.1, f32[11,144,128]{2,1,0:T(8,128)S(1)} %collective-permute-done.3.refs_2_.refs_3_, f32[10,144,128]{2,1,0:T(8,128)S(1)} %collective-permute-done.4.refs_3_.refs_4_, ...), custom_call_target="tpu_custom_call" | custom-call | flops 1 | bytes 1 | tf_op jit(solution)/shard_map/pallas_call | solution.py:844
  82.1 1.3 %collective-permute-start.11 = (f32[16,384]{1,0:T(8,128)S(1)}, f32[16,384]{1,0:T(8,128)S(1)}, u32[]{:S(2)}, u32[]{:S(2)}) collective-permute-start(f32[16,384]{1,0:T(8,128)S(1)} %shard_map.371.refs_2_), channel_id=1, source_target_pairs={{0,16},{8,24},{16,0},{24,8},{1,17},{9,25},{17,1},{25,9},{2,18},{10... | collective-permute-start | bytes 73736 | tf_op jit(solution)/shard_map/ppermute | solution.py:877
  83.3 1.3 %collective-permute-start.10 = (f32[7,144,128]{2,1,0:T(8,128)S(1)}, f32[7,144,128]{2,1,0:T(8,128)S(1)}, u32[]{:S(2)}, u32[]{:S(2)}) collective-permute-start(f32[7,144,128]{2,1,0:T(8,128)S(1)} %get-tuple-element.102), channel_id=1, source_target_pairs={{3,2},{4,5},{11,10},{12,13},{19,18},{20,21},{27,26},{28,29}} | collective-permute-start | bytes 1548296 | tf_op jit(solution)/shard_map/ppermute | solution.py:1128
  84.6 0.5 collective-permute-done.11
  85.1 1.3 %collective-permute-start.12 = (f32[16,384]{1,0:T(8,128)S(1)}, f32[16,384]{1,0:T(8,128)S(1)}, u32[]{:S(2)}, u32[]{:S(2)}) collective-permute-start(f32[16,384]{1,0:T(8,128)S(1)} %add.63), channel_id=1, source_target_pairs={{0,8},{8,0},{16,24},{24,16},{1,9},{9,1},{17,25},{25,17},{2,10},{10... | collective-permute-start | bytes 73736 | tf_op jit(solution)/shard_map/ppermute | solution.py:877
  86.5 0.8 collective-permute-done.12
  87.3 1.4 %select_select_fusion = f32[16,384]{1,0:T(8,128)S(1)} fusion(f32[16,384]{1,0:T(8,128)S(1)} %add.63, f32[16,384]{1,0:T(8,128)S(1)} %collective-permute-done.12, f32[]{:T(128)} %get-tuple-element.104, f32[]{:T(128)} %get-tuple-element.103, pred[384]{0:T(512)(128)(4,1)S(1)} %get-tuple-element.137, pred[384]{0:T(512)(128)(4,1)S(1)} %get-tuple-element.138, ...), kind=kLoop, calls=%fused_computation.8 | loop fusion | flops 30720 | bytes 74520 | tf_op jit(solution)/shard_map/jit(_where)/select_n | solution.py:1156
  88.7 0.0 copy-start.7
  88.7 0.0 copy-start.8
  88.7 0.0 copy-start.9
  88.7 0.0 copy-start.10
  88.7 0.0 copy-start.12
  88.7 0.0 copy-start.13
  88.8 0.0 copy-start.14
  88.8 0.0 copy-start.15
  88.8 0.0 copy-start.16
  88.8 0.0 copy-start.17
  88.8 5.8 %collective-permute-start.13 = (f32[16,384]{1,0:T(8,128)S(1)}, f32[16,384]{1,0:T(8,128)S(1)}, u32[]{:S(2)}, u32[]{:S(2)}) collective-permute-start(f32[16,384]{1,0:T(8,128)S(1)} %select_select_fusion), channel_id=1, source_target_pairs={{0,4},{1,5},{2,6},{3,7},{4,0},{5,1},{6,2},{7,3},{8,12},{9,13},{10,... | collective-permute-start | bytes 73736 | tf_op jit(solution)/shard_map/ppermute | solution.py:877
  94.6 11.0 %shard_map.372 = f32[144,11664]{1,0:T(8,128)} custom-call(s32[1,916]{1,0:T(1,128)S(1)} %copy-done.4, f32[25,2,144,128]{3,2,1,0:T(8,128)S(1)} %copy-done.1, f32[288,128]{1,0:T(8,128)S(1)} %copy-done.2, f32[16,384]{1,0:T(8,128)S(1)} %shard_map.371.refs_2_, f32[11,144,128]{2,1,0:T(8,128)S(1)} %collective-permute-done.3.refs_2_.refs_3_, ...), custom_call_target="tpu_custom_call" | custom-call | flops 1 | bytes 1 | tf_op jit(solution)/shard_map/pallas_call | solution.py:844
  105.6 0.0 collective-permute-done.13
  105.6 0.1 collective-permute-start.14
  105.7 3.0 %collective-permute-done.14 = f32[16,384]{1,0:T(8,128)S(1)} collective-permute-done((f32[16,384]{1,0:T(8,128)S(1)}, f32[16,384]{1,0:T(8,128)S(1)}, u32[]{:S(2)}, u32[]{:S(2)}) %collective-permute-start.14) | collective-permute-done | bytes 24608 | tf_op jit(solution)/shard_map/ppermute | solution.py:877
  108.7 0.0 collective-permute-start.15
  108.7 7.2 %collective-permute-done.15 = f32[16,384]{1,0:T(8,128)S(1)} collective-permute-done((f32[16,384]{1,0:T(8,128)S(1)}, f32[16,384]{1,0:T(8,128)S(1)}, u32[]{:S(2)}, u32[]{:S(2)}) %collective-permute-start.15) | collective-permute-done | bytes 24608 | tf_op jit(solution)/shard_map/ppermute | solution.py:877
  115.8 0.0 collective-permute-done.8.refs_2_
  115.8 0.0 collective-permute-done.10.refs_4_
  115.8 0.0 collective-permute-done.9.refs_3_
  116.0 5.0 %shard_map.373 = (f32[288,3136]{1,0:T(8,128)}, f32[9,36]{1,0:T(8,128)}, f32[9,36]{1,0:T(8,128)}, f32[9,36]{1,0:T(8,128)}, f32[9,36]{1,0:T(8,128)}, /*index=5*/f3...) custom-call(s32[1,916]{1,0:T(1,128)S(1)} %copy-done.4, ...), custom_call_target="tpu_custom_call" | custom-call | flops 1 | bytes 1 | tf_op jit(solution)/shard_map/pallas_call | solution.py:844
  (46 shorter events, 0.1 us)
Async XLA Ops:
  2.3 7.4 %copy-start.18 = (f32[144,128]{1,0:T(8,128)S(1)}, f32[144,128]{1,0:T(8,128)}, u32[]{:S(2)}) copy-start(f32[144,128]{1,0:T(8,128)} %get-tuple-element.76.refs_1_) | copy-start | bytes 221188
  2.3 7.4 %collective-permute-start = (f32[1,144,128]{2,1,0:T(8,128)}, f32[1,144,128]{2,1,0:T(8,128)S(1)}, u32[]{:S(2)}, u32[]{:S(2)}) collective-permute-start(f32[1,144,128]{2,1,0:T(8,128)} %bitcast.84), channel_id=1, source_target_pairs={{0,1},{1,0},{2,3},{3,2},{4,5},{5,4},{6,7},{7,6},{8,9},{9,8},{10,11... | collective-permute-start | bytes 221192 | tf_op jit(solution)/shard_map/ppermute | solution.py:877
  9.7 19.0 %collective-permute-start.3 = (f32[11,144,128]{2,1,0:T(8,128)}, f32[11,144,128]{2,1,0:T(8,128)S(1)}, u32[]{:S(2)}, u32[]{:S(2)}) collective-permute-start(f32[11,144,128]{2,1,0:T(8,128)} %get-tuple-element.88.refs_1_), channel_id=1, source_target_pairs={{0,1},{1,0},{3,2},{4,5},{6,7},{7,6},{2,3},{5,4},{8,9},{9,8},{11,10... | collective-permute-start | bytes 2433032 | tf_op jit(solution)/shard_map/ppermute | solution.py:1044
  10.0 8.9 %collective-permute-start.1 = (f32[2,144,128]{2,1,0:T(8,128)S(1)}, f32[2,144,128]{2,1,0:T(8,128)S(1)}, u32[]{:S(2)}, u32[]{:S(2)}) collective-permute-start(f32[2,144,128]{2,1,0:T(8,128)S(1)} %pad_maximum_fusion.2), channel_id=1, source_target_pairs={{0,4},{1,5},{2,6},{3,7},{4,0},{5,1},{6,2},{7,3},{8,12},{9,13},{10,... | collective-permute-start | bytes 442376 | tf_op jit(solution)/shard_map/ppermute | solution.py:877
  18.9 8.9 %collective-permute-start.2 = (f32[4,144,128]{2,1,0:T(8,128)S(1)}, f32[4,144,128]{2,1,0:T(8,128)S(1)}, u32[]{:S(2)}, u32[]{:S(2)}) collective-permute-start(f32[4,144,128]{2,1,0:T(8,128)S(1)} %pad_maximum_fusion.1), channel_id=1, source_target_pairs={{0,2},{1,3},{2,0},{3,1},{4,6},{5,7},{6,4},{7,5},{8,10},{9,11},{10,... | collective-permute-start | bytes 884744 | tf_op jit(solution)/shard_map/ppermute | solution.py:877
  19.0 9.7 %copy-start.23 = (f32[15,144,128]{2,1,0:T(8,128)S(1)}, f32[15,144,128]{2,1,0:T(8,128)}, u32[]{:S(2)}) copy-start(f32[15,144,128]{2,1,0:T(8,128)} %get-tuple-element.97) | copy-start | bytes 3317764
  28.7 15.7 %copy-start.4 = (s32[1,916]{1,0:T(1,128)S(1)}, s32[1,916]{1,0:T(1,128)}, u32[]{:S(2)}) copy-start(s32[1,916]{1,0:T(1,128)} %get-tuple-element.75.tab) | copy-start | bytes 10996
  28.7 45.1 %collective-permute-start.5 = (f32[15,144,128]{2,1,0:T(8,128)S(1)}, f32[15,144,128]{2,1,0:T(8,128)S(1)}, u32[]{:S(2)}, u32[]{:S(2)}) collective-permute-start(f32[15,144,128]{2,1,0:T(8,128)S(1)} %copy-done.23), channel_id=1, source_target_pairs={{3,4},{4,3},{1,2},{2,1},{5,6},{6,5},{11,12},{12,11},{9,10},{10,9},... | collective-permute-start | bytes 3317768 | tf_op jit(solution)/shard_map/ppermute | solution.py:1051
  33.1 40.6 %collective-permute-start.4 = (f32[10,144,128]{2,1,0:T(8,128)}, f32[10,144,128]{2,1,0:T(8,128)S(1)}, u32[]{:S(2)}, u32[]{:S(2)}) collective-permute-start(f32[10,144,128]{2,1,0:T(8,128)} %get-tuple-element.89), channel_id=1, source_target_pairs={{3,2},{4,5},{1,0},{6,7},{11,10},{12,13},{9,8},{14,15},{19,18},{20,... | collective-permute-start | bytes 2211848 | tf_op jit(solution)/shard_map/ppermute | solution.py:1044
  37.3 21.1 %copy-start.3 = (f32[144,36]{0,1:T(8,128)S(1)}, f32[144,36]{0,1:T(8,128)}, u32[]{:S(2)}) copy-start(f32[144,36]{0,1:T(8,128)} %param.25) | copy-start | bytes 62212
  37.3 21.1 %copy-start.19 = (f32[144,36]{0,1:T(8,128)S(1)}, f32[144,36]{0,1:T(8,128)}, u32[]{:S(2)}) copy-start(f32[144,36]{0,1:T(8,128)} %param.33) | copy-start | bytes 62212
  37.3 21.1 %copy-start.20 = (f32[144,36]{0,1:T(8,128)S(1)}, f32[144,36]{0,1:T(8,128)}, u32[]{:S(2)}) copy-start(f32[144,36]{0,1:T(8,128)} %param.29) | copy-start | bytes 62212
  37.4 3.4 %collective-permute-start.6 = (f32[40,256]{1,0:T(8,128)}, f32[40,256]{1,0:T(8,128)S(1)}, u32[]{:S(2)}, u32[]{:S(2)}) collective-permute-start(f32[40,256]{1,0:T(8,128)} %get-tuple-element.98), channel_id=1, source_target_pairs={{0,16},{8,24},{16,0},{24,8},{1,17},{9,25},{17,1},{25,9},{2,18},{10... | collective-permute-start | bytes 122888 | tf_op jit(solution)/shard_map/ppermute | solution.py:877
  41.6 16.9 %collective-permute-start.7 = (f32[40,256]{1,0:T(8,128)S(1)}, f32[40,256]{1,0:T(8,128)S(1)}, u32[]{:S(2)}, u32[]{:S(2)}) collective-permute-start(f32[40,256]{1,0:T(8,128)S(1)} %add.51), channel_id=1, source_target_pairs={{0,8},{8,0},{16,24},{24,16},{1,9},{9,1},{17,25},{25,17},{2,10},{10... | collective-permute-start | bytes 122888 | tf_op jit(solution)/shard_map/ppermute | solution.py:877
  44.3 2.9 %copy-start = (f32[93,144,128]{2,1,0:T(8,128)S(1)}, f32[93,144,128]{2,1,0:T(8,128)}, u32[]{:S(2)}) copy-start(f32[93,144,128]{2,1,0:T(8,128)} %shard_map.367.after.refs_0_) | copy-start | bytes 20570116
  47.3 0.9 copy-start.2
  48.2 27.5 %slice-start = ((s8[6856704]{0:T(1024)(128)(4,1)}), s8[4194304]{0:T(1024)(128)(4,1)S(1)}, s32[]{:S(2)}) async-start(s8[6856704]{0:T(1024)(128)(4,1)} %bitcast.57), calls=%async_computation | async-start | bytes 8388608
  54.0 61.8 %collective-permute-start.8 = (f32[21,144,128]{2,1,0:T(8,128)S(1)}, f32[21,144,128]{2,1,0:T(8,128)S(1)}, u32[]{:S(2)}, u32[]{:S(2)}) collective-permute-start(f32[21,144,128]{2,1,0:T(8,128)S(1)} %get-tuple-element.100), channel_id=1, source_target_pairs={{2,3},{5,4},{0,1},{7,6},{1,0},{6,7},{10,11},{13,12},{8,9},{15,14},... | collective-permute-start | bytes 4644872 | tf_op jit(solution)/shard_map/ppermute | solution.py:1098
  59.7 7.3 %copy-start.11 = (f32[36]{0:T(128)S(1)}, f32[36]{0:T(128)}, u32[]{:S(2)}) copy-start(f32[36]{0:T(128)} %param.26) | copy-start | bytes 436
  59.7 7.3 %copy-start.21 = (f32[36]{0:T(128)S(1)}, f32[36]{0:T(128)}, u32[]{:S(2)}) copy-start(f32[36]{0:T(128)} %param.30) | copy-start | bytes 436
  59.7 7.3 %copy-start.22 = (f32[36]{0:T(128)S(1)}, f32[36]{0:T(128)}, u32[]{:S(2)}) copy-start(f32[36]{0:T(128)} %param.34) | copy-start | bytes 436
  59.7 16.0 %slice-start.1 = ((s8[6856704]{0:T(1024)(128)(4,1)}), s8[2662400]{0:T(1024)(128)(4,1)S(1)}, s32[]{:S(2)}) async-start(s8[6856704]{0:T(1024)(128)(4,1)} %bitcast.57), calls=%async_computation.1 | async-start | bytes 5324800
  59.7 16.0 %copy-start.1 = (f32[25,2,144,128]{3,2,1,0:T(8,128)S(1)}, f32[25,2,144,128]{3,2,1,0:T(8,128)}, u32[]{:S(2)}) copy-start(f32[25,2,144,128]{3,2,1,0:T(8,128)} %shard_map.366.refs_1_.refs_0_) | copy-start | bytes 11059204
  73.8 42.1 %collective-permute-start.9 = (f32[15,144,128]{2,1,0:T(8,128)S(1)}, f32[15,144,128]{2,1,0:T(8,128)S(1)}, u32[]{:S(2)}, u32[]{:S(2)}) collective-permute-start(f32[15,144,128]{2,1,0:T(8,128)S(1)} %get-tuple-element.101), channel_id=1, source_target_pairs={{3,4},{4,3},{1,2},{2,1},{5,6},{6,5},{11,12},{12,11},{9,10},{10,9},... | collective-permute-start | bytes 3317768 | tf_op jit(solution)/shard_map/ppermute | solution.py:1128
  82.1 3.0 %collective-permute-start.11 = (f32[16,384]{1,0:T(8,128)S(1)}, f32[16,384]{1,0:T(8,128)S(1)}, u32[]{:S(2)}, u32[]{:S(2)}) collective-permute-start(f32[16,384]{1,0:T(8,128)S(1)} %shard_map.371.refs_2_), channel_id=1, source_target_pairs={{0,16},{8,24},{16,0},{24,8},{1,17},{9,25},{17,1},{25,9},{2,18},{10... | collective-permute-start | bytes 73736 | tf_op jit(solution)/shard_map/ppermute | solution.py:877
  83.3 32.5 %collective-permute-start.10 = (f32[7,144,128]{2,1,0:T(8,128)S(1)}, f32[7,144,128]{2,1,0:T(8,128)S(1)}, u32[]{:S(2)}, u32[]{:S(2)}) collective-permute-start(f32[7,144,128]{2,1,0:T(8,128)S(1)} %get-tuple-element.102), channel_id=1, source_target_pairs={{3,2},{4,5},{11,10},{12,13},{19,18},{20,21},{27,26},{28,29}} | collective-permute-start | bytes 1548296 | tf_op jit(solution)/shard_map/ppermute | solution.py:1128
  85.1 2.2 %collective-permute-start.12 = (f32[16,384]{1,0:T(8,128)S(1)}, f32[16,384]{1,0:T(8,128)S(1)}, u32[]{:S(2)}, u32[]{:S(2)}) collective-permute-start(f32[16,384]{1,0:T(8,128)S(1)} %add.63), channel_id=1, source_target_pairs={{0,8},{8,0},{16,24},{24,16},{1,9},{9,1},{17,25},{25,17},{2,10},{10... | collective-permute-start | bytes 73736 | tf_op jit(solution)/shard_map/ppermute | solution.py:877
  88.7 27.2 %copy-start.5 = (f32[128,384]{1,0:T(8,128)S(1)}, f32[128,384]{1,0:T(8,128)}, u32[]{:S(2)}) copy-start(f32[128,384]{1,0:T(8,128)} %get-tuple-element.110.refs_6_) | copy-start | bytes 589828
  88.7 27.2 %copy-start.6 = (f32[144,36]{0,1:T(8,128)S(1)}, f32[144,36]{0,1:T(8,128)}, u32[]{:S(2)}) copy-start(f32[144,36]{0,1:T(8,128)} %param.37) | copy-start | bytes 62212
  88.7 27.2 %copy-start.7 = (f32[36,9]{0,1:T(8,128)S(1)}, f32[36,9]{0,1:T(8,128)}, u32[]{:S(2)}) copy-start(f32[36,9]{0,1:T(8,128)} %param.23) | copy-start | bytes 3892
  88.7 27.2 %copy-start.8 = (f32[36,9]{0,1:T(8,128)S(1)}, f32[36,9]{0,1:T(8,128)}, u32[]{:S(2)}) copy-start(f32[36,9]{0,1:T(8,128)} %param.27) | copy-start | bytes 3892
  88.7 27.2 %copy-start.9 = (f32[36,9]{0,1:T(8,128)S(1)}, f32[36,9]{0,1:T(8,128)}, u32[]{:S(2)}) copy-start(f32[36,9]{0,1:T(8,128)} %param.31) | copy-start | bytes 3892
  88.7 27.2 %copy-start.10 = (f32[36,9]{0,1:T(8,128)S(1)}, f32[36,9]{0,1:T(8,128)}, u32[]{:S(2)}) copy-start(f32[36,9]{0,1:T(8,128)} %param.35) | copy-start | bytes 3892
  88.7 27.2 %copy-start.12 = (f32[8,128]{1,0:T(8,128)S(1)}, f32[8,128]{1,0:T(8,128)}, u32[]{:S(2)}) copy-start(f32[8,128]{1,0:T(8,128)} %get-tuple-element.111.refs_7_) | copy-start | bytes 12292
  88.7 27.2 %copy-start.13 = (f32[36]{0:T(128)S(1)}, f32[36]{0:T(128)}, u32[]{:S(2)}) copy-start(f32[36]{0:T(128)} %param.24) | copy-start | bytes 436
  88.8 27.2 %copy-start.14 = (f32[36]{0:T(128)S(1)}, f32[36]{0:T(128)}, u32[]{:S(2)}) copy-start(f32[36]{0:T(128)} %param.28) | copy-start | bytes 436
  88.8 27.2 %copy-start.15 = (f32[36]{0:T(128)S(1)}, f32[36]{0:T(128)}, u32[]{:S(2)}) copy-start(f32[36]{0:T(128)} %param.32) | copy-start | bytes 436
  88.8 27.2 %copy-start.16 = (f32[36]{0:T(128)S(1)}, f32[36]{0:T(128)}, u32[]{:S(2)}) copy-start(f32[36]{0:T(128)} %param.36) | copy-start | bytes 436
  88.8 27.2 %copy-start.17 = (f32[36]{0:T(128)S(1)}, f32[36]{0:T(128)}, u32[]{:S(2)}) copy-start(f32[36]{0:T(128)} %param.38) | copy-start | bytes 436
  88.8 16.8 %collective-permute-start.13 = (f32[16,384]{1,0:T(8,128)S(1)}, f32[16,384]{1,0:T(8,128)S(1)}, u32[]{:S(2)}, u32[]{:S(2)}) collective-permute-start(f32[16,384]{1,0:T(8,128)S(1)} %select_select_fusion), channel_id=1, source_target_pairs={{0,4},{1,5},{2,6},{3,7},{4,0},{5,1},{6,2},{7,3},{8,12},{9,13},{10,... | collective-permute-start | bytes 73736 | tf_op jit(solution)/shard_map/ppermute | solution.py:877
  105.6 3.0 %collective-permute-start.14 = (f32[16,384]{1,0:T(8,128)S(1)}, f32[16,384]{1,0:T(8,128)S(1)}, u32[]{:S(2)}, u32[]{:S(2)}) collective-permute-start(f32[16,384]{1,0:T(8,128)S(1)} %add.65), channel_id=1, source_target_pairs={{0,2},{1,3},{2,0},{3,1},{4,6},{5,7},{6,4},{7,5},{8,10},{9,11},{10,... | collective-permute-start | bytes 73736 | tf_op jit(solution)/shard_map/ppermute | solution.py:877
  108.7 7.2 %collective-permute-start.15 = (f32[16,384]{1,0:T(8,128)S(1)}, f32[16,384]{1,0:T(8,128)S(1)}, u32[]{:S(2)}, u32[]{:S(2)}) collective-permute-start(f32[16,384]{1,0:T(8,128)S(1)} %add.66), channel_id=1, source_target_pairs={{0,1},{1,0},{2,3},{3,2},{4,5},{5,4},{6,7},{7,6},{8,9},{9,8},{10,11... | collective-permute-start | bytes 73736 | tf_op jit(solution)/shard_map/ppermute | solution.py:877
